TPU v7x, 768 devices: a whole 4x8x12 slice. The times are simulated.
768 devices in a mesh: ctx: 96 (over z, y_hi, core), head: 4 (over x), scene: 2 (over y_lo).
Axes of the slice: x: 4, y: 8 (y_hi: 4, y_lo: 2; y = y_hi * 2 + y_lo), z: 12, core: 2. Of those that a mesh axis runs over, the one named last changes fastest.
Arguments:
- queries: bfloat16 [2, 15360, 512], P('scene', 'ctx', 'head'), may hold values from -8 to 8
- key_states: bfloat16 [2, 15360, 512], P('scene', 'ctx', 'head'), may hold values from -8 to 8
- value_states: bfloat16 [2, 15360, 512], P('scene', 'ctx', 'head'), may hold values from -6 to 6
- splat_weight: float32 [2, 15360], P('scene', 'ctx'), may hold values from 0.25 to 2.5
- tile_of: int32 [2, 15360, 1], P('scene', 'ctx'), may hold values from 0 to 95; in each aligned block of 160 rows (0 to 159, 160 to 319, ..., all dimensions but the last counted through in order) at most 4 rows name the same one
- cell_of: int32 [2, 15360], P('scene', 'ctx'), may hold values from 0 to 255
- bev_base: bfloat16 [2, 24576, 1024], P('scene', 'ctx'), may hold values from -3 to 3
- norm_gain: float32 [1024], replicated, may hold values from 0.1 to 1.9
- out_weight: bfloat16 [512, 1024], P('head'), may hold values from -0.25 to 0.25
- up_weight: bfloat16 [1024, 4096], P(None, 'head'), may hold values from -0.1875 to 0.1875
- down_weight: bfloat16 [4096, 1024], P('head'), may hold values from -0.09375 to 0.09375
Outputs:
- bev_out: bfloat16 [2, 24576, 1024], P('scene', ('ctx', 'head'))
Inputs may be any that keep to these rules, and one draw needn't show every extreme that they name: `tile_of`: among the rows of one index of ctx no tile is named by more than 4 rows; on some devices a tile is named by exactly 4.
All inputs are finite; a program needn't handle non-finite values.
Results may differ from a plain program's by a relative error of at most 0.017.
Values may be sent and summed in bfloat16 or wider, within the bound.
No kernel may reach another device: no remote copies, remote signals or barrier semaphores. Data moves between devices by JAX's collectives and lax.ppermute only.
A program may use at most 32 MiB of HBM per device.

v0:
```python
import math

import jax
import jax.numpy as jnp
from jax import lax
from jax.sharding import PartitionSpec as P

HS = 64


def attend_keys(carry, query_heads, key_rows, value_rows):
    top_seen, denominator, numerator = carry
    head_count = query_heads.shape[1]
    key_heads = key_rows.reshape(key_rows.shape[0], head_count, HS)
    value_heads = value_rows.reshape(value_rows.shape[0], head_count, HS)
    scores = jnp.einsum(
        "qhd,khd->hqk", query_heads, key_heads, preferred_element_type=jnp.float32
    ) * (1.0 / math.sqrt(HS))
    new_top = jnp.maximum(top_seen, jnp.max(scores, axis=2))
    factor = jnp.exp(top_seen - new_top)
    exp_scores = jnp.exp(scores - new_top[:, :, None])
    denominator = denominator * factor + jnp.sum(exp_scores, axis=2)
    contribution = jnp.einsum(
        "hqk,khd->qhd",
        exp_scores.astype(jnp.bfloat16),
        value_heads,
        preferred_element_type=jnp.float32,
    )
    numerator = numerator * jnp.transpose(factor)[:, :, None] + contribution
    return (new_top, denominator, numerator)


def pack_rows(weighted, target, cell_index, cycle_size, capacity, cells_here):
    onehot = (target[:, None] == jnp.arange(cycle_size, dtype=jnp.int32)[None, :]).astype(jnp.int32)
    within = jnp.sum(jnp.cumsum(onehot, axis=0) * onehot, axis=1) - 1
    slot_index = target * capacity + within
    place_matrix = (
        slot_index[None, :] == jnp.arange(cycle_size * capacity, dtype=jnp.int32)[:, None]
    ).astype(jnp.int32)
    send_rows = jnp.dot(
        place_matrix.astype(jnp.bfloat16), weighted, preferred_element_type=jnp.float32
    ).astype(jnp.bfloat16)
    filled = jnp.sum(place_matrix, axis=1)
    send_cells = jnp.sum(place_matrix * cell_index[None, :], axis=1)
    send_cells = jnp.where(filled > 0, send_cells, cells_here)
    return (
        send_rows.reshape(cycle_size, capacity, weighted.shape[1]),
        send_cells.reshape(cycle_size, capacity),
    )


def body(
    queries,
    key_states,
    value_states,
    splat_weight,
    tile_of,
    cell_of,
    bev_base,
    norm_gain,
    out_weight,
    up_weight,
    down_weight,
):
    tok_rows = queries.shape[1]
    width = queries.shape[2]
    head_count = width // HS
    query_heads = queries[0].reshape(tok_rows, head_count, HS)
    stacked = jnp.stack([key_states[0], value_states[0]])
    start_state = (
        jnp.full((head_count, tok_rows), -1e30, jnp.float32),
        jnp.zeros((head_count, tok_rows), jnp.float32),
        jnp.zeros((tok_rows, head_count, HS), jnp.float32),
    )
    cycle_size = lax.axis_size("ctx")
    piece = lax.all_gather(stacked, "ctx", axis=1, tiled=True)
    length = piece.shape[1]
    block = math.gcd(length, 1024)

    def one_block(index, state):
        block_rows = lax.dynamic_slice_in_dim(piece, index * block, block, 1)
        return attend_keys(state, query_heads, block_rows[0], block_rows[1])

    carry = lax.fori_loop(0, length // block, one_block, start_state)
    top_seen, denominator, numerator = carry
    attended = numerator / jnp.transpose(denominator)[:, :, None]
    weighted = (attended.reshape(tok_rows, width) * splat_weight[0][:, None]).astype(jnp.bfloat16)
    capacity = max(2, (2 * tok_rows + cycle_size - 1) // cycle_size)
    cells_here = bev_base.shape[1]
    send_rows, send_cells = pack_rows(
        weighted, tile_of[0, :, 0], cell_of[0], cycle_size, capacity, cells_here
    )
    recv_rows, recv_cells = (
        lax.all_to_all(send_rows, "ctx", split_axis=0, concat_axis=0, tiled=True),
        lax.all_to_all(send_cells, "ctx", split_axis=0, concat_axis=0, tiled=True),
    )
    slot_rows = recv_rows.reshape(cycle_size * capacity, width)
    slot_cells = recv_cells.reshape(cycle_size * capacity)
    splat_matrix = (slot_cells[None, :] == jnp.arange(cells_here, dtype=jnp.int32)[:, None]).astype(
        jnp.bfloat16
    )
    cell_features = jnp.dot(splat_matrix, slot_rows, preferred_element_type=jnp.float32).astype(
        jnp.bfloat16
    )
    share_rows = cells_here // lax.axis_size("head")
    own_start = lax.axis_index("head") * share_rows
    base_rows = bev_base[0].astype(jnp.float32)
    partial_proj = jnp.dot(cell_features, out_weight, preferred_element_type=jnp.float32)
    bev = base_rows + lax.psum(partial_proj.astype(jnp.bfloat16), "head").astype(jnp.float32)
    mean_square = jnp.mean(bev * bev, axis=1, keepdims=True)
    hidden = jax.nn.gelu(
        jnp.dot(
            (bev * lax.rsqrt(mean_square + 1e-06) * norm_gain[None, :]).astype(jnp.bfloat16),
            up_weight,
            preferred_element_type=jnp.float32,
        ),
        approximate=False,
    ).astype(jnp.bfloat16)
    bev_rows = lax.dynamic_slice_in_dim(bev, own_start, share_rows, 0)
    mixed = lax.psum_scatter(
        jnp.dot(hidden, down_weight, preferred_element_type=jnp.float32).astype(jnp.bfloat16),
        "head",
        scatter_dimension=0,
        tiled=True,
    ).astype(jnp.float32)
    return (bev_rows + mixed).astype(jnp.bfloat16)[None]


def solution(mesh):
    placed = (
        P("scene", "ctx", "head"),
        P("scene", "ctx", "head"),
        P("scene", "ctx", "head"),
        P("scene", "ctx"),
        P("scene", "ctx", None),
        P("scene", "ctx"),
        P("scene", "ctx", None),
        P(),
        P("head", None),
        P(None, "head"),
        P("head", None),
    )
    return jax.shard_map(
        body,
        mesh=mesh,
        in_specs=placed,
        out_specs=P("scene", ("ctx", "head"), None),
        check_vma=False,
    )
```

profile of v0, /device:TPU:56, one launch (start us, length us, event | category | flops | bytes accessed | tf_op | source)
XLA Modules:
  0.0 349.8 jit_solution(123817748227667986)
XLA Ops:
  12.6 21.5 %all-to-all-start = ((s32[96,1,4]{2,1,0:T(1,128)}), s32[96,1,4]{2,1,0:T(1,128)}, u32[]{:S(2)}, u32[]{:S(2)}) async-start(s32[96,1,4]{2,1,0:T(1,128)} %bitcast.4), calls=%async_computation | async-start | bytes 98304 | tf_op jit(solution)/shard_map/all_to_all | solution.py:95
  34.9 112.9 %all-gather.2.cloned.1.call-done = bf16[2,15360,128]{2,0,1:T(2,128)(2,1)} async-done(((bf16[2,160,128]{2,0,1:T(2,128)(2,1)}), bf16[2,15360,128]{2,0,1:T(2,128)(2,1)}) %all-gather.2.cloned.1.call-update) | async-done | bytes 7864336 | tf_op jit(solution)/shard_map/all_gather | solution.py:76
  147.8 74.9 %while.18 = (s32[]{:T(128)}, f32[2,160]{1,0:T(2,128)S(1)}, f32[2,160]{1,0:T(2,128)S(1)}, f32[160,2,64]{0,2,1:T(8,128)S(1)}, bf16[2,15360,128]{2,0,1:T(2,128)(2,1...) while((s32[]{:T(128)}, f32[2,160]{1,0:T(2,128)S(1)}, ...), condition=%wide.region_8.9_spmd.clone, body=%wide.region_5.0_spmd.clone.sunk | while | flops 85915528 | bytes 6779075 | solution.py:84
  147.8 2.1 constant_dynamic-slice_fusion.3
  150.5 1.3 fusion.114
  152.7 2.1 constant_dynamic-slice_fusion.3
  157.7 2.1 constant_dynamic-slice_fusion.3
  162.7 2.1 constant_dynamic-slice_fusion.3
  167.7 2.1 constant_dynamic-slice_fusion.3
  170.5 1.3 fusion.114
  172.7 2.1 constant_dynamic-slice_fusion.3
  177.7 2.1 constant_dynamic-slice_fusion.3
  182.7 2.1 constant_dynamic-slice_fusion.3
  187.7 2.1 constant_dynamic-slice_fusion.3
  192.6 2.1 constant_dynamic-slice_fusion.3
  195.4 1.3 fusion.114
  197.6 2.1 constant_dynamic-slice_fusion.3
  200.4 1.3 fusion.114
  202.6 2.1 constant_dynamic-slice_fusion.3
  205.4 1.3 fusion.114
  207.6 2.1 constant_dynamic-slice_fusion.3
  212.6 2.2 constant_dynamic-slice_fusion.3
  217.7 2.1 constant_dynamic-slice_fusion.3
  223.7 12.9 %all-to-all-start.1 = ((bf16[96,4,128]{2,1,0:T(4,128)(2,1)}), bf16[96,4,128]{2,1,0:T(4,128)(2,1)S(1)}, u32[]{:S(2)}, u32[]{:S(2)}) async-start(bf16[96,4,128]{2,1,0:T(4,128)(2,1)} %bitcast.9), calls=%async_computation.1 | async-start | bytes 196608 | tf_op jit(solution)/shard_map/all_to_all | solution.py:94
  237.3 1.6 reduce.5
  239.0 10.4 %all-to-all-done.1 = bf16[96,4,128]{2,1,0:T(4,128)(2,1)S(1)} async-done(((bf16[96,4,128]{2,1,0:T(4,128)(2,1)}), bf16[96,4,128]{2,1,0:T(4,128)(2,1)S(1)}, u32[]{:S(2)}, u32[]{:S(2)}) %all-to-all-start.1) | async-done | bytes 98336 | tf_op jit(solution)/shard_map/all_to_all | solution.py:94
  249.4 2.2 convolution_convert_fusion.1
  251.7 51.8 %all-reduce.3.cloned.1.call-done = bf16[256,1024]{1,0:T(8,128)(2,1)} async-done(((bf16[256,1024]{1,0:T(8,128)(2,1)}), bf16[256,1024]{1,0:T(8,128)(2,1)}) %all-reduce.3.cloned.1.call-update) | async-done | bytes 524304 | tf_op jit(solution)/shard_map/psum | solution.py:109
  303.5 1.4 convert_add_fusion
  305.0 6.3 %convolution_convert_fusion = bf16[256,1024]{1,0:T(8,128)(2,1)} fusion(bf16[1024,1024]{1,0:T(8,128)(2,1)S(1)} %copy-done, bf16[1024,1024]{1,0:T(8,128)(2,1)} %param.22, f32[1024]{0:T(1024)S(1)} %copy-done.5, f32[256]{0:T(256)S(1)} %add_rsqrt_fusion, bf16[256,1024]{1,0:T(8,128)(2,1)} %all-reduce.3.cloned.1.call-done, bf16[1,256,1024]{2,1,0:T(8,128)(2,1)} %param.19), kind=kOutput, calls=%fused_computation.18 | convolution fusion | flops 1092616192 | bytes 5772288 | tf_op jit(solution)/shard_map/dot_general | solution.py:121
  311.3 30.3 %reduce-scatter.2.cloned.1.call-done = bf16[64,1024]{1,0:T(8,128)(2,1)} async-done(((bf16[256,1024]{1,0:T(8,128)(2,1)}), bf16[64,1024]{1,0:T(8,128)(2,1)}) %reduce-scatter.2.cloned.1.call-update) | async-done | bytes 131088 | tf_op jit(solution)/shard_map/reduce_scatter | solution.py:120
  341.7 1.6 fusion.57
  (159 shorter events, 44.8 us)
Async XLA Ops:
  6.5 298.5 %copy-start = (bf16[1024,1024]{1,0:T(8,128)(2,1)S(1)}, bf16[1024,1024]{1,0:T(8,128)(2,1)}, u32[]{:S(2)}) copy-start(bf16[1024,1024]{1,0:T(8,128)(2,1)} %param.23) | copy-start | bytes 6291460
  6.5 5.2 %copy-start.2 = (s32[1,160,1]{1,2,0:T(1,128)S(1)}, s32[1,160,1]{1,2,0:T(1,128)}, u32[]{:S(2)}) copy-start(s32[1,160,1]{1,2,0:T(1,128)} %param.17) | copy-start | bytes 1924
  6.5 5.2 %copy-start.4 = (s32[1,160]{1,0:T(1,128)S(1)}, s32[1,160]{1,0:T(1,128)}, u32[]{:S(2)}) copy-start(s32[1,160]{1,0:T(1,128)} %param.18) | copy-start | bytes 1924
  6.5 27.6 %copy-start.1 = (bf16[1,160,128]{2,1,0:T(8,128)(2,1)S(1)}, bf16[1,160,128]{2,1,0:T(8,128)(2,1)}, u32[]{:S(2)}) copy-start(bf16[1,160,128]{2,1,0:T(8,128)(2,1)} %param.13) | copy-start | bytes 122884
  6.5 141.2 %all-gather.2.cloned.1.call-start = ((), (), s32[]{:S(2)}) async-start(), calls=%async_computation.3 | async-start | bytes 7946240 | tf_op jit(solution)/shard_map/all_gather | solution.py:76
  12.6 211.2 %all-to-all-start = ((s32[96,1,4]{2,1,0:T(1,128)}), s32[96,1,4]{2,1,0:T(1,128)}, u32[]{:S(2)}, u32[]{:S(2)}) async-start(s32[96,1,4]{2,1,0:T(1,128)} %bitcast.4), calls=%async_computation | async-start | bytes 98304 | tf_op jit(solution)/shard_map/all_to_all | solution.py:95
  147.8 75.0 %copy-start.3 = (f32[1,160]{1,0:T(1,128)S(1)}, f32[1,160]{1,0:T(1,128)}, u32[]{:S(2)}) copy-start(f32[1,160]{1,0:T(1,128)} %param.16) | copy-start | bytes 1924
  223.7 25.7 %all-to-all-start.1 = ((bf16[96,4,128]{2,1,0:T(4,128)(2,1)}), bf16[96,4,128]{2,1,0:T(4,128)(2,1)S(1)}, u32[]{:S(2)}, u32[]{:S(2)}) async-start(bf16[96,4,128]{2,1,0:T(4,128)(2,1)} %bitcast.9), calls=%async_computation.1 | async-start | bytes 196608 | tf_op jit(solution)/shard_map/all_to_all | solution.py:94
  236.6 66.9 %all-reduce.3.cloned.1.call-start = ((), (), s32[]{:S(2)}) async-start(), calls=%async_computation.4 | async-start | bytes 1048576 | tf_op jit(solution)/shard_map/psum | solution.py:109
  251.6 53.4 %copy-start.5 = (f32[1024]{0:T(1024)S(1)}, f32[1024]{0:T(1024)}, u32[]{:S(2)}) copy-start(f32[1024]{0:T(1024)} %param.20) | copy-start | bytes 12292
  251.7 90.0 %reduce-scatter.2.cloned.1.call-start = ((), (), s32[]{:S(2)}) async-start(), calls=%async_computation.5 | async-start | bytes 655360 | tf_op jit(solution)/shard_map/reduce_scatter | solution.py:120
Sparse Core Ops, SparseCore 0:
  11.0 136.6 all-gather.1
  251.8 51.7 all-reduce.2
  311.4 30.1 reduce-scatter.1
where the time goes:
time: 352 us; the launch traced here: 350 us
  waiting for transfers between devices  206 us (59%)
  local copies, waits for them, and re-layouts  45.9 us (13%)
  matrix products  35.8 us (10%)
  starting transfers between devices  34.5 us (10%)
  other arithmetic  13.8 us (4%)
  between operations  13.3 us (4%)
    all_gather x1, waiting for transfers between devices, body(): piece = lax.all_gather(stacked, 'ctx', axis=1, tiled=True)  113 us
    psum x1, waiting for transfers between devices, body(): lax.psum(partial_proj.astype(jnp.bfloat16), 'head').astype(jnp.float32)  51.8 us
    slice x15, local copies, waits for them, and re-layouts, one_block(): return attend_keys(state, query_heads, block_rows[0], block_rows[1])  31.1 us
    reduce_scatter x1, waiting for transfers between devices, body(): lax.psum_scatter(jnp.dot(hidden, down_weight, preferred_element_type=jnp....  30.3 us
    all_to_all x1, starting transfers between devices, body(): lax.all_to_all(send_cells, 'ctx', split_axis=0, concat_axis=0, tiled=True)  21.5 us
    dot_general x15, matrix products, attend_keys(): jnp.einsum('qhd,khd->hqk', query_heads, key_heads, preferred_element_type...  19.6 us
    all_to_all x1, starting transfers between devices, body(): lax.all_to_all(send_rows, 'ctx', split_axis=0, concat_axis=0, tiled=True)  12.9 us
    while x45, local copies, waits for them, and re-layouts  10.6 us
  transfers between devices with their start and end apart: 5, of which 4 were waited for; matrix products, arithmetic and copies ran while one was open for 23% of the time, Pallas kernels for 0%

commit v1 on v0

v1 whole, which is shorter than its diff:
```python
import functools
import math

import jax
import jax.numpy as jnp
from jax import lax
from jax.experimental import pallas as pl
from jax.experimental.pallas import tpu as pltpu
from jax.sharding import Mesh
from jax.sharding import PartitionSpec as P

HS = 64
LANES = 128
SLOTS = 4
PIECE = 20
EXPONENT = math.log2(math.e) / math.sqrt(HS)
VMEM_LIMIT = 56 * 1024 * 1024

f32 = jnp.float32
bf16 = jnp.bfloat16


def dot(a, b):
    return lax.dot_general(a, b, (((1,), (0,)), ((), ())), preferred_element_type=f32)


def dot_nt(a, b):
    return lax.dot_general(a, b, (((1,), (1,)), ((), ())), preferred_element_type=f32)


def attend_kernel(tiles, own_ref, other_ref, q_ref, out_ref, k_s, v_s, ox_s, slot_s, slot_t):
    blocks, tok = own_ref.shape[0], own_ref.shape[1] // 2
    span = blocks * tok
    groups = q_ref.shape[0]
    low = lax.broadcasted_iota(jnp.int32, (1, LANES), 1) < HS
    low_f = jnp.where(low, 1.0, 0.0)
    low_b, high_b = low_f.astype(bf16), (1.0 - low_f).astype(bf16)
    for part, kv_ref in enumerate((own_ref, other_ref)):
        rows = pl.ds(part * span, span)
        k_s[rows, :] = kv_ref[:, :tok, :].reshape(span, LANES)
        values = kv_ref[:, tok:, :].reshape(span, LANES)
        v_s[0, rows, :] = values * low_b + high_b
        v_s[1, rows, :] = values * high_b + low_b
    lane = lax.broadcasted_iota(jnp.int32, (tok, LANES), 1)
    lane_f = lane.astype(f32)
    for group in range(groups):
        q = q_ref[group, :, :LANES]
        meta = q_ref[group, :, LANES:].astype(f32)
        tile, cell = meta[:, 0:1], meta[:, 2:3]
        place = meta[:, 1:2] + float(group * SLOTS)
        splat = meta[:, 3:4] + meta[:, 4:5]
        rows = pl.ds(group * tok, tok)
        sums = []
        extra = jnp.where(lane_f == 96.0 + place, cell, 0.0)
        for head, keep in enumerate((low_b, high_b)):
            s = dot_nt(q * keep, k_s[...])
            top = jnp.max(s, axis=1, keepdims=True)
            p = jnp.exp2((s - top) * EXPONENT).astype(bf16)
            o = dot(p, v_s[head])
            at = LANES - 1 if head == 0 else 0
            total = o[:, at : at + 1]
            sums.append(o * (splat / total))
            left = top * EXPONENT + jnp.log2(total)
            for step in range(3):
                piece = left.astype(bf16).astype(f32)
                left = left - piece
                extra = jnp.where(lane_f == step * 32.0 + head * 16.0 + place, piece, extra)
        ox_s[rows, :] = jnp.where(low, sums[0], sums[1]).astype(bf16)
        ox_s[pl.ds(groups * tok + group * tok, tok), :] = extra.astype(bf16)
        slot_s[rows, :] = jnp.where(
            lane == 0, tile * PIECE + place, jnp.where(lane == 1, tile * PIECE + float(SLOTS * groups), -1.0)
        )
    slot_t[...] = jnp.transpose(slot_s[...])
    chunk = 8 * PIECE * 3
    width = groups * tok
    for begin in range(0, tiles * PIECE, chunk):
        row = (lax.broadcasted_iota(jnp.int32, (chunk, width), 0) + begin).astype(f32)
        main = jnp.where(row == slot_t[0:1, :], 1.0, 0.0).astype(bf16)
        tail = jnp.where(row == slot_t[1:2, :], 1.0, 0.0).astype(bf16)
        packed = dot(main, ox_s[:width, :]) + dot(tail, ox_s[width:, :])
        out_ref[pl.ds(begin, chunk), :] = packed.astype(bf16)


def attend(own, other, q_all, tiles):
    blocks, tok2, _ = own.shape
    groups, tok, _ = q_all.shape
    keys = blocks * tok2
    return pl.pallas_call(
        functools.partial(attend_kernel, tiles),
        out_shape=jax.ShapeDtypeStruct((tiles * PIECE, LANES), bf16),
        in_specs=[pl.BlockSpec(memory_space=pltpu.VMEM)] * 3,
        out_specs=pl.BlockSpec(memory_space=pltpu.VMEM),
        scratch_shapes=[
            pltpu.VMEM((keys, LANES), bf16),
            pltpu.VMEM((2, keys, LANES), bf16),
            pltpu.VMEM((2 * groups * tok, LANES), bf16),
            pltpu.VMEM((groups * tok, LANES), f32),
            pltpu.VMEM((LANES, groups * tok), f32),
        ],
        compiler_params=pltpu.CompilerParams(vmem_limit_bytes=VMEM_LIMIT),
        name="attend_pack",
    )(own, other, q_all)


def splat_kernel(cells, groups, x_ref, out_ref, x_s, y_s, r_s):
    sources = x_ref.shape[0] // PIECE
    slots = groups * SLOTS
    x_s[...] = x_ref[...].astype(f32)
    meta = x_s[pl.ds(slots, sources, stride=PIECE), :]
    lse = meta + pltpu.roll(meta, LANES - 32, 1) + pltpu.roll(meta, LANES - 64, 1)
    lse = lse.reshape(sources // (2 * groups), 2 * groups, LANES)
    turns = [lse] + [pltpu.roll(lse, 2 * k, 1) for k in range(1, groups)]
    top = functools.reduce(jnp.maximum, turns)
    powers = [jnp.exp2(t - top) for t in turns]
    weight = powers[0] / functools.reduce(jnp.add, powers)
    weight = weight.reshape(sources, LANES)
    lane = lax.broadcasted_iota(jnp.int32, (sources, LANES), 1)
    y_s[...] = jnp.zeros_like(y_s)
    y_s[:sources, :] = jnp.where(lane < 32, weight, meta)
    y_t = jnp.transpose(y_s[...])
    r_s[...] = jnp.zeros_like(r_s)
    for slot in range(slots):
        r_s[pl.ds(slot * LANES, sources), :] = x_s[pl.ds(slot, sources, stride=PIECE), :].astype(bf16)
    cell = (lax.broadcasted_iota(jnp.int32, (cells, LANES), 0) + 1).astype(f32)
    hits = [cell == y_t[96 + slot : 97 + slot, :] for slot in range(slots)]
    sums = []
    for head in range(2):
        spread = jnp.concatenate(
            [
                jnp.where(hits[slot], y_t[head * 16 + slot : head * 16 + slot + 1, :], 0.0).astype(bf16)
                for slot in range(slots)
            ],
            axis=1,
        )
        sums.append(dot(spread, r_s[...]))
    low = lax.broadcasted_iota(jnp.int32, (1, LANES), 1) < HS
    out_ref[...] = jnp.where(low, sums[0], sums[1]).astype(bf16)


def splat(received, cells, groups):
    rows = received.shape[0]
    return pl.pallas_call(
        functools.partial(splat_kernel, cells, groups),
        out_shape=jax.ShapeDtypeStruct((cells, LANES), bf16),
        in_specs=[pl.BlockSpec(memory_space=pltpu.VMEM)],
        out_specs=pl.BlockSpec(memory_space=pltpu.VMEM),
        scratch_shapes=[
            pltpu.VMEM((rows, LANES), f32),
            pltpu.VMEM((LANES, LANES), f32),
            pltpu.VMEM((groups * SLOTS * LANES, LANES), bf16),
        ],
        compiler_params=pltpu.CompilerParams(vmem_limit_bytes=VMEM_LIMIT),
        name="join_splat",
    )(received)


def mlp_kernel(own_ref, f_ref, ow_ref, base_ref, gain_ref, up_ref, down_ref, bev_ref, mix_ref, bev_s):
    heads = f_ref.shape[0]
    share = bev_ref.shape[0]
    bev = base_ref[...].astype(f32) + functools.reduce(
        jnp.add, [dot(f_ref[h], ow_ref[h]) for h in range(heads)]
    )
    bev_s[...] = bev
    mean_square = jnp.mean(bev * bev, axis=1, keepdims=True)
    normed = (bev * lax.rsqrt(mean_square + 1e-06) * gain_ref[...]).astype(bf16)
    hidden_units = up_ref.shape[1]
    step = 256
    mixed = None
    for begin in range(0, hidden_units, step):
        u = dot(normed, up_ref[:, begin : begin + step])
        hidden = (0.5 * u * (1.0 + lax.erf(u * math.sqrt(0.5)))).astype(bf16)
        term = dot(hidden, down_ref[begin : begin + step, :])
        mixed = term if mixed is None else mixed + term
    mix_ref[...] = mixed.astype(bf16)
    start = pl.multiple_of(own_ref[0] * share, share)
    bev_ref[...] = bev_s[pl.ds(start, share), :]


def mlp(own, features, out_weight, base, gain, up, down):
    heads = features.shape[0]
    cells, width = base.shape
    vmem = pl.BlockSpec(memory_space=pltpu.VMEM)
    return pl.pallas_call(
        mlp_kernel,
        out_shape=(
            jax.ShapeDtypeStruct((cells // heads, width), f32),
            jax.ShapeDtypeStruct((cells, width), bf16),
        ),
        in_specs=[pl.BlockSpec(memory_space=pltpu.SMEM)] + [vmem] * 6,
        out_specs=(vmem, vmem),
        scratch_shapes=[pltpu.VMEM((cells, width), f32)],
        compiler_params=pltpu.CompilerParams(vmem_limit_bytes=VMEM_LIMIT),
        name="project_mlp",
    )(own, features, out_weight, base, gain, up, down)


def to_all(x, axis):
    count = lax.axis_size(axis)
    return lax.all_to_all(jnp.broadcast_to(x[None], (count,) + x.shape), axis, 0, 0)


def body(
    queries,
    key_states,
    value_states,
    splat_weight,
    tile_of,
    cell_of,
    bev_base,
    norm_gain,
    out_weight,
    up_weight,
    down_weight,
):
    tok = queries.shape[1]
    tiles = lax.axis_size("z") * lax.axis_size("y") * lax.axis_size("core")
    groups = lax.axis_size("y")
    heads = lax.axis_size("head")
    cells = bev_base.shape[1]
    tile = tile_of[0, :, 0]
    index = jnp.arange(tok, dtype=jnp.int32)
    earlier = (tile[:, None] == tile[None, :]) & (index[None, :] < index[:, None])
    rank = jnp.sum(earlier.astype(jnp.int32), axis=1)
    coarse = lax.reduce_precision(splat_weight[0], 8, 7)
    fine = splat_weight[0] - coarse
    columns = [tile.astype(f32), rank.astype(f32), (cell_of[0] + 1).astype(f32), coarse, fine]
    meta = jnp.pad(jnp.stack(columns, axis=1), ((0, 0), (0, LANES - len(columns)))).astype(bf16)
    q_all = to_all(jnp.concatenate([queries[0], meta], axis=1), "y")
    ow_all = to_all(out_weight, "head")
    kv = jnp.concatenate([key_states[0], value_states[0]], axis=0)
    own_kv = lax.all_gather(kv, "z")
    other_kv = lax.ppermute(own_kv, "core", [(0, 1), (1, 0)])
    packed = attend(own_kv, other_kv, q_all, tiles)
    received = lax.all_to_all(packed.reshape(tiles, PIECE, LANES), ("z", "y", "core"), 0, 0)
    features = splat(received.reshape(tiles * PIECE, LANES), cells, groups)
    features = to_all(features, "head")
    own = lax.axis_index("head").astype(jnp.int32).reshape(1)
    bev_rows, mixed = mlp(own, features, ow_all, bev_base[0], norm_gain[None, :], up_weight, down_weight)
    mixed = lax.all_to_all(mixed.reshape(heads, cells // heads, mixed.shape[1]), "head", 0, 0)
    return (bev_rows + jnp.sum(mixed.astype(f32), axis=0)).astype(bf16)[None]


def solution(mesh):
    core, y = 2, 4
    z = mesh.shape["ctx"] // (core * y)
    split = Mesh(
        mesh.devices.reshape(z, y, core, mesh.shape["head"], mesh.shape["scene"]),
        ("z", "y", "core", "head", "scene"),
    )
    ctx = ("z", "y", "core")
    placed = (
        P("scene", ctx, "head"),
        P("scene", ctx, "head"),
        P("scene", ctx, "head"),
        P("scene", ctx),
        P("scene", ctx, None),
        P("scene", ctx),
        P("scene", ctx, None),
        P(),
        P("head", None),
        P(None, "head"),
        P("head", None),
    )
    return jax.shard_map(
        body,
        mesh=split,
        in_specs=placed,
        out_specs=P("scene", ctx + ("head",), None),
        check_vma=False,
    )
```

time: 352 us -> 168 us (0.48)
  waiting for transfers between devices: 206 us -> 19.8 us
  blocking collectives: 0 us -> 103 us
  local copies, waits for them, and re-layouts: 45.9 us -> 7.55 us
  matrix products: 35.8 us -> 0 us
  starting transfers between devices: 34.5 us -> 9.78 us
  Pallas kernels: 0 us -> 20.9 us
  between operations: 13.3 us -> 0.1 us
  other arithmetic: 13.8 us -> 5.54 us
    all_gather x1 -> x0, waiting for transfers between devices: 113 us -> none  [body(): piece = lax.all_gather(stacked, 'ctx', axis=1, tiled=True)]
    all_to_all x0 -> x3, blocking collectives: none -> 64.7 us  [the longest x1 37.1 us: body(): lax.all_to_all(packed.reshape(tiles, PIECE, LANES), ('z', 'y', 'core'), 0...]
    psum x1 -> x0, waiting for transfers between devices: 51.8 us -> none  [body(): lax.psum(partial_proj.astype(jnp.bfloat16), 'head').astype(jnp.float32)]
    all_gather x0 -> x1, blocking collectives: none -> 38.6 us  [body(): own_kv = lax.all_gather(kv, 'z')]
    dot_general x33 -> x0, matrix products: 35.8 us -> none  [the longest x15 19.6 us: attend_keys(): jnp.einsum('qhd,khd->hqk', query_heads, key_heads, preferred_element_type...]
    slice x15 -> x0, local copies, waits for them, and re-layouts: 31.1 us -> none  [one_block(): return attend_keys(state, query_heads, block_rows[0], block_rows[1])]
    reduce_scatter x1 -> x0, waiting for transfers between devices: 30.3 us -> none  [body(): lax.psum_scatter(jnp.dot(hidden, down_weight, preferred_element_type=jnp....]
    all_to_all x2, starting transfers between devices: 34.4 us -> 7.87 us  [to_all(): lax.all_to_all(jnp.broadcast_to(x[None], (count,) + x.shape), axis, 0, 0)]
  transfers between devices with their start and end apart: 5 -> 3, of which waited for: 4 -> 2; matrix products, arithmetic and copies ran while one was open for 23% -> 3% of each run, Pallas kernels for 0% -> 2%
where the time goes in v1:
time: 168 us; the launch traced here: 167 us
  blocking collectives  103 us (61%)
  Pallas kernels  20.9 us (12%)
  waiting for transfers between devices  19.8 us (12%)
  starting transfers between devices  9.78 us (6%)
  local copies, waits for them, and re-layouts  7.55 us (4%)
  other arithmetic  5.54 us (3%)
    all_gather x1, blocking collectives, body(): own_kv = lax.all_gather(kv, 'z')  38.6 us
    all_to_all x1, blocking collectives, body(): lax.all_to_all(packed.reshape(tiles, PIECE, LANES), ('z', 'y', 'core'), 0...  37.1 us
    all_to_all x2, waiting for transfers between devices, to_all(): lax.all_to_all(jnp.broadcast_to(x[None], (count,) + x.shape), axis, 0, 0)  19.8 us
    all_to_all x1, blocking collectives, to_all(): lax.all_to_all(jnp.broadcast_to(x[None], (count,) + x.shape), axis, 0, 0)  14.4 us
    all_to_all x1, blocking collectives, body(): lax.all_to_all(mixed.reshape(heads, cells // heads, mixed.shape[1]), 'hea...  13.2 us
    pallas_call x1, Pallas kernels, attend(): pl.pallas_call(functools.partial(attend_kernel, tiles), out_shape=jax.Sha...  12.1 us
    all_to_all x2, starting transfers between devices, to_all(): lax.all_to_all(jnp.broadcast_to(x[None], (count,) + x.shape), axis, 0, 0)  7.87 us
    pallas_call x1, Pallas kernels, mlp(): pl.pallas_call(mlp_kernel, out_shape=(jax.ShapeDtypeStruct((cells // head...  6.14 us
  transfers between devices with their start and end apart: 3, of which 2 were waited for; matrix products, arithmetic and copies ran while one was open for 3% of the time, Pallas kernels for 2%

profile of v1, /device:TPU:56, one launch (start us, length us, event | category | flops | bytes accessed | tf_op | source)
XLA Modules:
  0.0 167.0 jit_solution(12278206315568248535)
XLA Ops:
  0.0 0.8 pad_maximum_fusion
  0.8 38.6 %all-gather = bf16[3840,128]{1,0:T(8,128)(2,1)S(1)} all-gather(bf16[320,128]{1,0:T(8,128)(2,1)S(1)} %pad_maximum_fusion), channel_id=2, replica_groups=mesh['z'=12,'y'=4,'core'=2,'head'=4,'scene'=2] {'z'}, dimensions={0}, use_global_device_ids=true | all-gather | bytes 1064960 | tf_op jit(solution)/shard_map/all_gather | solution.py:231
  39.4 1.9 %collective-permute-start = (bf16[12,320,128]{2,1,0:T(8,128)(2,1)S(1)}, bf16[12,320,128]{2,1,0:T(8,128)(2,1)S(1)}, u32[]{:S(2)}, u32[]{:S(2)}) collective-permute-start(bf16[12,320,128]{2,1,0:T(8,128)(2,1)S(1)} %bitcast.18), channel_id=1, source_target_pairs={{0,8},{8,0},{1,9},{9,1},{2,10},{10,2},{3,11},{11,3},{4,12},{12,4},... | collective-permute-start | bytes 2949128 | tf_op jit(solution)/shard_map/ppermute | solution.py:232
  41.3 0.7 convert_bitcast_fusion.1
  42.0 0.9 convert_reduce_fusion.1
  43.0 0.9 copy.14
  43.9 0.7 convert_bitcast_fusion
  44.5 0.7 fusion.4
  45.3 0.1 copy.15
  45.4 14.4 %all_to_all.25.q_ref = bf16[4,160,256]{2,1,0:T(8,128)(2,1)} all-to-all(bf16[4,160,256]{2,1,0:T(8,128)(2,1)S(1)} %broadcast_in_dim.10), channel_id=1, replica_groups=mesh['z'=12,'y'=4,'core'=2,'head'=4,'scene'=2] {'y'}, dimensions={0} | all-to-all | bytes 655360 | tf_op jit(solution)/shard_map/all_to_all | solution.py:199
  59.8 0.0 collective-permute-done.other_ref
  59.8 0.0 copy-done.1
  59.9 0.0 copy-start.3
  59.9 1.0 copy-done.3
  60.9 12.1 %attend_pack.1 = bf16[1920,128]{1,0:T(8,128)(2,1)} custom-call(bf16[12,320,128]{2,1,0:T(8,128)(2,1)} %bitcast.19, bf16[12,320,128]{2,1,0:T(8,128)(2,1)} %copy-done.3, bf16[4,160,256]{2,1,0:T(8,128)(2,1)} %all_to_all.25.q_ref), custom_call_target="tpu_custom_call" | custom-call | tf_op jit(solution)/shard_map/attend_pack/pallas_call | solution.py:88
  73.0 1.2 reshape.79
  74.1 37.1 %all_to_all.26 = bf16[96,20,128]{2,1,0:T(8,128)(2,1)S(1)} all-to-all(bf16[96,20,128]{2,1,0:T(8,128)(2,1)S(1)} %reshape.79), channel_id=1, replica_groups=mesh['z'=12,'y'=4,'core'=2,'head'=4,'scene'=2] {'z','y','core'}, dimensions={0} | all-to-all | bytes 983040 | tf_op jit(solution)/shard_map/all_to_all | solution.py:234
  111.3 0.0 copy-done.4
  111.3 1.1 broadcast_in_dim.12
  112.4 4.5 %all-to-all-start.3 = ((bf16[4,128,1024]{2,1,0:T(8,128)(2,1)}), bf16[4,128,1024]{2,1,0:T(8,128)(2,1)S(1)}, u32[]{:S(2)}, u32[]{:S(2)}) async-start(bf16[4,128,1024]{2,1,0:T(8,128)(2,1)} %broadcast_in_dim.12), calls=%async_computation.3 | async-start | bytes 2097152 | tf_op jit(solution)/shard_map/all_to_all | solution.py:199
  116.8 0.9 reshape.80.x_ref
  117.7 2.7 %join_splat.1 = bf16[256,128]{1,0:T(8,128)(2,1)} custom-call(bf16[1920,128]{1,0:T(8,128)(2,1)} %reshape.80.x_ref), custom_call_target="tpu_custom_call" | custom-call | tf_op jit(solution)/shard_map/join_splat/pallas_call | solution.py:142
  120.4 12.1 %all-to-all-done.3.ow_ref = bf16[4,128,1024]{2,1,0:T(8,128)(2,1)S(1)} async-done(((bf16[4,128,1024]{2,1,0:T(8,128)(2,1)}), bf16[4,128,1024]{2,1,0:T(8,128)(2,1)S(1)}, u32[]{:S(2)}, u32[]{:S(2)}) %all-to-all-start.3) | async-done | bytes 1048608 | tf_op jit(solution)/shard_map/all_to_all | solution.py:199
  132.5 1.6 broadcast_in_dim.11
  134.1 3.4 %all-to-all-start.2 = ((bf16[4,256,128]{2,1,0:T(8,128)(2,1)}), bf16[4,256,128]{2,1,0:T(8,128)(2,1)S(1)}, u32[]{:S(2)}, u32[]{:S(2)}) async-start(bf16[4,256,128]{2,1,0:T(8,128)(2,1)} %broadcast_in_dim.11), calls=%async_computation.2 | async-start | bytes 524288 | tf_op jit(solution)/shard_map/all_to_all | solution.py:199
  137.5 7.7 %all-to-all-done.2.f_ref = bf16[4,256,128]{2,1,0:T(8,128)(2,1)S(1)} async-done(((bf16[4,256,128]{2,1,0:T(8,128)(2,1)}), bf16[4,256,128]{2,1,0:T(8,128)(2,1)S(1)}, u32[]{:S(2)}, u32[]{:S(2)}) %all-to-all-start.2) | async-done | bytes 262176 | tf_op jit(solution)/shard_map/all_to_all | solution.py:199
  145.3 0.0 copy-done
  145.3 0.7 copy-done.2
  146.0 6.1 %project_mlp.1 = (f32[64,1024]{1,0:T(8,128)}, bf16[256,1024]{1,0:T(8,128)(2,1)}) custom-call(s32[1]{0:T(128)} %bitcast.own_ref, bf16[4,256,128]{2,1,0:T(8,128)(2,1)} %copy-done.2, bf16[4,128,1024]{2,1,0:T(8,128)(2,1)} %copy-done, bf16[256,1024]{1,0:T(8,128)(2,1)} %bitcast.21, f32[1,1024]{1,0:T(1,128)} %bitcast.26, bf16[1024,1024]{1,0:T(8,128)(2,1)} %up_ref.1, ...), custom_call_target="tpu_custom_call" | custom-call | tf_op jit(solution)/shard_map/project_mlp/pallas_call | solution.py:183
  152.1 13.2 %all_to_all.27 = bf16[4,64,1024]{2,1,0:T(8,128)(2,1)S(1)} all-to-all(bf16[4,64,1024]{2,1,0:T(8,128)(2,1)} %bitcast.20), channel_id=1, replica_groups=mesh['z'=12,'y'=4,'core'=2,'head'=4,'scene'=2] {'head'}, dimensions={0} | all-to-all | bytes 1048576 | tf_op jit(solution)/shard_map/all_to_all | solution.py:239
  165.3 0.1 convert_reduce_fusion
  165.3 1.6 fusion.3
  (9 shorter events, 0.1 us)
Async XLA Ops:
  39.4 20.5 %copy-start.1 = (bf16[3840,128]{1,0:T(8,128)(2,1)}, bf16[3840,128]{1,0:T(8,128)(2,1)S(1)}, u32[]{:S(2)}) copy-start(bf16[3840,128]{1,0:T(8,128)(2,1)S(1)} %all-gather) | copy-start | bytes 2949124
  39.4 20.4 %collective-permute-start = (bf16[12,320,128]{2,1,0:T(8,128)(2,1)S(1)}, bf16[12,320,128]{2,1,0:T(8,128)(2,1)S(1)}, u32[]{:S(2)}, u32[]{:S(2)}) collective-permute-start(bf16[12,320,128]{2,1,0:T(8,128)(2,1)S(1)} %bitcast.18), channel_id=1, source_target_pairs={{0,8},{8,0},{1,9},{9,1},{2,10},{10,2},{3,11},{11,3},{4,12},{12,4},... | collective-permute-start | bytes 2949128 | tf_op jit(solution)/shard_map/ppermute | solution.py:232
  59.8 51.4 %copy-start.4 = (bf16[128,1024]{1,0:T(8,128)(2,1)S(1)}, bf16[128,1024]{1,0:T(8,128)(2,1)}, u32[]{:S(2)}) copy-start(bf16[128,1024]{1,0:T(8,128)(2,1)} %param.19) | copy-start | bytes 786436
  59.9 1.0 copy-start.3
  112.4 20.1 %all-to-all-start.3 = ((bf16[4,128,1024]{2,1,0:T(8,128)(2,1)}), bf16[4,128,1024]{2,1,0:T(8,128)(2,1)S(1)}, u32[]{:S(2)}, u32[]{:S(2)}) async-start(bf16[4,128,1024]{2,1,0:T(8,128)(2,1)} %broadcast_in_dim.12), calls=%async_computation.3 | async-start | bytes 2097152 | tf_op jit(solution)/shard_map/all_to_all | solution.py:199
  132.5 12.8 %copy-start = (bf16[4,128,1024]{2,1,0:T(8,128)(2,1)}, bf16[4,128,1024]{2,1,0:T(8,128)(2,1)S(1)}, u32[]{:S(2)}) copy-start(bf16[4,128,1024]{2,1,0:T(8,128)(2,1)S(1)} %all-to-all-done.3.ow_ref) | copy-start | bytes 3145732
  134.1 11.2 %all-to-all-start.2 = ((bf16[4,256,128]{2,1,0:T(8,128)(2,1)}), bf16[4,256,128]{2,1,0:T(8,128)(2,1)S(1)}, u32[]{:S(2)}, u32[]{:S(2)}) async-start(bf16[4,256,128]{2,1,0:T(8,128)(2,1)} %broadcast_in_dim.11), calls=%async_computation.2 | async-start | bytes 524288 | tf_op jit(solution)/shard_map/all_to_all | solution.py:199
  145.3 0.7 copy-start.2

commit v2 on v1

--- a/solution.py
+++ b/solution.py
@@ -12,9 +12,9 @@
 HS = 64
 LANES = 128
 SLOTS = 4
-PIECE = 20
+PIECE = 24
 EXPONENT = math.log2(math.e) / math.sqrt(HS)
-VMEM_LIMIT = 56 * 1024 * 1024
+MIB = 1024 * 1024
 
 f32 = jnp.float32
 bf16 = jnp.bfloat16
@@ -28,51 +28,112 @@
     return lax.dot_general(a, b, (((1,), (1,)), ((), ())), preferred_element_type=f32)
 
 
-def attend_kernel(tiles, own_ref, other_ref, q_ref, out_ref, k_s, v_s, ox_s, slot_s, slot_t):
-    blocks, tok = own_ref.shape[0], own_ref.shape[1] // 2
+def prologue_kernel(q_ref, k_ref, v_ref, tile_ref, cell_ref, splat_ref, q_out, kv_out, rows_s):
+    copies, tok = q_out.shape[0], q_out.shape[1]
+    tile = tile_ref[...].astype(f32)
+    coarse = splat_ref[...].astype(bf16).astype(f32)
+    rows_s[...] = jnp.zeros_like(rows_s)
+    rows_s[0:1, :tok] = tile
+    rows_s[2:3, :tok] = (cell_ref[...] + 1).astype(f32)
+    rows_s[3:4, :tok] = coarse
+    rows_s[4:5, :tok] = splat_ref[...] - coarse
+    columns = jnp.transpose(rows_s[...])[:tok, :]
+    shape = (tok, tok)
+    earlier = lax.broadcasted_iota(jnp.int32, shape, 1) < lax.broadcasted_iota(jnp.int32, shape, 0)
+    alike = jnp.where(columns[:, 0:1] == tile, 1.0, 0.0)
+    rank = jnp.sum(jnp.where(earlier, alike, 0.0), axis=1, keepdims=True)
+    lane = lax.broadcasted_iota(jnp.int32, (tok, LANES), 1)
+    meta = jnp.where(lane == 1, rank, columns).astype(bf16)
+    for copy in range(copies):
+        q_out[copy, :, :LANES] = q_ref[0]
+        q_out[copy, :, LANES:] = meta
+    kv_out[:tok, :] = k_ref[0]
+    kv_out[tok:, :] = v_ref[0]
+
+
+def prologue(queries, key_states, value_states, tile, cell, splat_weight, copies):
+    tok = queries.shape[1]
+    vmem = pl.BlockSpec(memory_space=pltpu.VMEM)
+    return pl.pallas_call(
+        prologue_kernel,
+        out_shape=(
+            jax.ShapeDtypeStruct((copies, tok, 2 * LANES), bf16),
+            jax.ShapeDtypeStruct((2 * tok, LANES), bf16),
+        ),
+        in_specs=[vmem] * 6,
+        out_specs=(vmem, vmem),
+        scratch_shapes=[pltpu.VMEM((LANES, 2 * LANES), f32)],
+        compiler_params=pltpu.CompilerParams(vmem_limit_bytes=58 * MIB),
+        name="prologue",
+    )(queries, key_states, value_states, tile, cell, splat_weight)
+
+
+def attend_block(q_ref, group, k_s, v_s):
+    low = lax.broadcasted_iota(jnp.int32, (1, LANES), 1) < HS
+    q = q_ref[group, :, :LANES]
+    for head in range(2):
+        keep = jnp.where(low if head == 0 else ~low, 1.0, 0.0).astype(bf16)
+        s = dot_nt(q * keep, k_s[...])
+        top = jnp.max(s, axis=1, keepdims=True)
+        p = jnp.exp2((s - top) * EXPONENT).astype(bf16)
+        yield head, top * EXPONENT, dot(p, v_s[head])
+
+
+def stage_keys(kv_ref, k_s, v_s):
+    blocks, tok = kv_ref.shape[0], kv_ref.shape[1] // 2
     span = blocks * tok
-    groups = q_ref.shape[0]
+    low = jnp.where(lax.broadcasted_iota(jnp.int32, (1, LANES), 1) < HS, 1.0, 0.0)
+    low_b, high_b = low.astype(bf16), (1.0 - low).astype(bf16)
+    k_s[...] = kv_ref[:, :tok, :].reshape(span, LANES)
+    values = kv_ref[:, tok:, :].reshape(span, LANES)
+    v_s[0] = values * low_b + high_b
+    v_s[1] = values * high_b + low_b
+
+
+def first_kernel(kv_ref, q_ref, top_ref, sum_ref, k_s, v_s):
+    groups, tok = q_ref.shape[0], q_ref.shape[1]
+    stage_keys(kv_ref, k_s, v_s)
+    for group in range(groups):
+        rows = pl.ds(group * tok, tok)
+        for head, top, sums in attend_block(q_ref, group, k_s, v_s):
+            top_ref[head, rows, :] = jnp.broadcast_to(top, (tok, LANES))
+            sum_ref[head, rows, :] = sums
+
+
+def second_kernel(tiles, kv_ref, q_ref, top_ref, sum_ref, _, out_ref, k_s, v_s, ox_s, slot_s, slot_t):
+    groups, tok = q_ref.shape[0], q_ref.shape[1]
+    stage_keys(kv_ref, k_s, v_s)
     low = lax.broadcasted_iota(jnp.int32, (1, LANES), 1) < HS
-    low_f = jnp.where(low, 1.0, 0.0)
-    low_b, high_b = low_f.astype(bf16), (1.0 - low_f).astype(bf16)
-    for part, kv_ref in enumerate((own_ref, other_ref)):
-        rows = pl.ds(part * span, span)
-        k_s[rows, :] = kv_ref[:, :tok, :].reshape(span, LANES)
-        values = kv_ref[:, tok:, :].reshape(span, LANES)
-        v_s[0, rows, :] = values * low_b + high_b
-        v_s[1, rows, :] = values * high_b + low_b
     lane = lax.broadcasted_iota(jnp.int32, (tok, LANES), 1)
     lane_f = lane.astype(f32)
+    width = groups * tok
     for group in range(groups):
-        q = q_ref[group, :, :LANES]
         meta = q_ref[group, :, LANES:].astype(f32)
         tile, cell = meta[:, 0:1], meta[:, 2:3]
         place = meta[:, 1:2] + float(group * SLOTS)
-        splat = meta[:, 3:4] + meta[:, 4:5]
+        gain = meta[:, 3:4] + meta[:, 4:5]
         rows = pl.ds(group * tok, tok)
         sums = []
         extra = jnp.where(lane_f == 96.0 + place, cell, 0.0)
-        for head, keep in enumerate((low_b, high_b)):
-            s = dot_nt(q * keep, k_s[...])
-            top = jnp.max(s, axis=1, keepdims=True)
-            p = jnp.exp2((s - top) * EXPONENT).astype(bf16)
-            o = dot(p, v_s[head])
+        for head, top_b, sum_b in attend_block(q_ref, group, k_s, v_s):
+            top_a = top_ref[head, rows, :][:, 0:1]
+            top = jnp.maximum(top_a, top_b)
+            o = sum_ref[head, rows, :] * jnp.exp2(top_a - top) + sum_b * jnp.exp2(top_b - top)
             at = LANES - 1 if head == 0 else 0
             total = o[:, at : at + 1]
-            sums.append(o * (splat / total))
-            left = top * EXPONENT + jnp.log2(total)
+            sums.append(o * (gain / total))
+            left = top + jnp.log2(total)
             for step in range(3):
                 piece = left.astype(bf16).astype(f32)
                 left = left - piece
                 extra = jnp.where(lane_f == step * 32.0 + head * 16.0 + place, piece, extra)
         ox_s[rows, :] = jnp.where(low, sums[0], sums[1]).astype(bf16)
-        ox_s[pl.ds(groups * tok + group * tok, tok), :] = extra.astype(bf16)
+        ox_s[pl.ds(width + group * tok, tok), :] = extra.astype(bf16)
         slot_s[rows, :] = jnp.where(
             lane == 0, tile * PIECE + place, jnp.where(lane == 1, tile * PIECE + float(SLOTS * groups), -1.0)
         )
     slot_t[...] = jnp.transpose(slot_s[...])
-    chunk = 8 * PIECE * 3
-    width = groups * tok
+    chunk = 16 * PIECE
     for begin in range(0, tiles * PIECE, chunk):
         row = (lax.broadcasted_iota(jnp.int32, (chunk, width), 0) + begin).astype(f32)
         main = jnp.where(row == slot_t[0:1, :], 1.0, 0.0).astype(bf16)
@@ -81,25 +142,51 @@
         out_ref[pl.ds(begin, chunk), :] = packed.astype(bf16)
 
 
-def attend(own, other, q_all, tiles):
-    blocks, tok2, _ = own.shape
+def attention_cost(queries, keys):
+    return pl.CostEstimate(
+        flops=2 * 2 * 2 * queries * keys * LANES, bytes_accessed=4 * queries * LANES, transcendentals=2 * queries * keys
+    )
+
+
+def attend_first(kv, q_all):
+    blocks, tok2, _ = kv.shape
     groups, tok, _ = q_all.shape
-    keys = blocks * tok2
-    return pl.pallas_call(
-        functools.partial(attend_kernel, tiles),
+    span, rows = blocks * tok2 // 2, groups * tok
+    vmem = pl.BlockSpec(memory_space=pltpu.VMEM)
+    state = jax.ShapeDtypeStruct((2, rows, LANES), f32)
+    return pl.pallas_call(
+        first_kernel,
+        out_shape=(state, state),
+        in_specs=[vmem, vmem],
+        out_specs=(vmem, vmem),
+        scratch_shapes=[pltpu.VMEM((span, LANES), bf16), pltpu.VMEM((2, span, LANES), bf16)],
+        compiler_params=pltpu.CompilerParams(vmem_limit_bytes=20 * MIB),
+        cost_estimate=attention_cost(rows, span),
+        name="attend_own_core",
+    )(kv, q_all)
+
+
+def attend_second(kv, q_all, top, sums, early, tiles):
+    blocks, tok2, _ = kv.shape
+    groups, tok, _ = q_all.shape
+    span, rows = blocks * tok2 // 2, groups * tok
+    vmem = pl.BlockSpec(memory_space=pltpu.VMEM)
+    return pl.pallas_call(
+        functools.partial(second_kernel, tiles),
         out_shape=jax.ShapeDtypeStruct((tiles * PIECE, LANES), bf16),
-        in_specs=[pl.BlockSpec(memory_space=pltpu.VMEM)] * 3,
-        out_specs=pl.BlockSpec(memory_space=pltpu.VMEM),
+        in_specs=[vmem] * 4 + [pl.BlockSpec(memory_space=pl.ANY)],
+        out_specs=vmem,
         scratch_shapes=[
-            pltpu.VMEM((keys, LANES), bf16),
-            pltpu.VMEM((2, keys, LANES), bf16),
-            pltpu.VMEM((2 * groups * tok, LANES), bf16),
-            pltpu.VMEM((groups * tok, LANES), f32),
-            pltpu.VMEM((LANES, groups * tok), f32),
+            pltpu.VMEM((span, LANES), bf16),
+            pltpu.VMEM((2, span, LANES), bf16),
+            pltpu.VMEM((2 * rows, LANES), bf16),
+            pltpu.VMEM((rows, LANES), f32),
+            pltpu.VMEM((LANES, rows), f32),
         ],
-        compiler_params=pltpu.CompilerParams(vmem_limit_bytes=VMEM_LIMIT),
-        name="attend_pack",
-    )(own, other, q_all)
+        compiler_params=pltpu.CompilerParams(vmem_limit_bytes=24 * MIB),
+        cost_estimate=attention_cost(rows, span),
+        name="attend_other_core",
+    )(kv, q_all, top, sums, early)
 
 
 def splat_kernel(cells, groups, x_ref, out_ref, x_s, y_s, r_s):
@@ -134,14 +221,16 @@
         )
         sums.append(dot(spread, r_s[...]))
     low = lax.broadcasted_iota(jnp.int32, (1, LANES), 1) < HS
-    out_ref[...] = jnp.where(low, sums[0], sums[1]).astype(bf16)
-
-
-def splat(received, cells, groups):
+    features = jnp.where(low, sums[0], sums[1]).astype(bf16)
+    for copy in range(out_ref.shape[0]):
+        out_ref[copy] = features
+
+
+def splat(received, cells, groups, copies):
     rows = received.shape[0]
     return pl.pallas_call(
         functools.partial(splat_kernel, cells, groups),
-        out_shape=jax.ShapeDtypeStruct((cells, LANES), bf16),
+        out_shape=jax.ShapeDtypeStruct((copies, cells, LANES), bf16),
         in_specs=[pl.BlockSpec(memory_space=pltpu.VMEM)],
         out_specs=pl.BlockSpec(memory_space=pltpu.VMEM),
         scratch_shapes=[
@@ -149,7 +238,7 @@
             pltpu.VMEM((LANES, LANES), f32),
             pltpu.VMEM((groups * SLOTS * LANES, LANES), bf16),
         ],
-        compiler_params=pltpu.CompilerParams(vmem_limit_bytes=VMEM_LIMIT),
+        compiler_params=pltpu.CompilerParams(vmem_limit_bytes=12 * MIB),
         name="join_splat",
     )(received)
 
@@ -157,9 +246,8 @@
 def mlp_kernel(own_ref, f_ref, ow_ref, base_ref, gain_ref, up_ref, down_ref, bev_ref, mix_ref, bev_s):
     heads = f_ref.shape[0]
     share = bev_ref.shape[0]
-    bev = base_ref[...].astype(f32) + functools.reduce(
-        jnp.add, [dot(f_ref[h], ow_ref[h]) for h in range(heads)]
-    )
+    features = jnp.concatenate([f_ref[h] for h in range(heads)], axis=1)
+    bev = base_ref[...].astype(f32) + dot(features, ow_ref[...].reshape(features.shape[1], -1))
     bev_s[...] = bev
     mean_square = jnp.mean(bev * bev, axis=1, keepdims=True)
     normed = (bev * lax.rsqrt(mean_square + 1e-06) * gain_ref[...]).astype(bf16)
@@ -189,7 +277,7 @@
         in_specs=[pl.BlockSpec(memory_space=pltpu.SMEM)] + [vmem] * 6,
         out_specs=(vmem, vmem),
         scratch_shapes=[pltpu.VMEM((cells, width), f32)],
-        compiler_params=pltpu.CompilerParams(vmem_limit_bytes=VMEM_LIMIT),
+        compiler_params=pltpu.CompilerParams(vmem_limit_bytes=20 * MIB),
         name="project_mlp",
     )(own, features, out_weight, base, gain, up, down)
 
@@ -217,23 +305,18 @@
     groups = lax.axis_size("y")
     heads = lax.axis_size("head")
     cells = bev_base.shape[1]
-    tile = tile_of[0, :, 0]
-    index = jnp.arange(tok, dtype=jnp.int32)
-    earlier = (tile[:, None] == tile[None, :]) & (index[None, :] < index[:, None])
-    rank = jnp.sum(earlier.astype(jnp.int32), axis=1)
-    coarse = lax.reduce_precision(splat_weight[0], 8, 7)
-    fine = splat_weight[0] - coarse
-    columns = [tile.astype(f32), rank.astype(f32), (cell_of[0] + 1).astype(f32), coarse, fine]
-    meta = jnp.pad(jnp.stack(columns, axis=1), ((0, 0), (0, LANES - len(columns)))).astype(bf16)
-    q_all = to_all(jnp.concatenate([queries[0], meta], axis=1), "y")
+    q_copies, kv = prologue(
+        queries, key_states, value_states, tile_of.reshape(1, tok), cell_of, splat_weight, groups
+    )
+    q_all = lax.all_to_all(q_copies, "y", 0, 0)
     ow_all = to_all(out_weight, "head")
-    kv = jnp.concatenate([key_states[0], value_states[0]], axis=0)
     own_kv = lax.all_gather(kv, "z")
     other_kv = lax.ppermute(own_kv, "core", [(0, 1), (1, 0)])
-    packed = attend(own_kv, other_kv, q_all, tiles)
+    top, sums = attend_first(own_kv, q_all)
+    packed = attend_second(other_kv, q_all, top, sums, ow_all, tiles)
     received = lax.all_to_all(packed.reshape(tiles, PIECE, LANES), ("z", "y", "core"), 0, 0)
-    features = splat(received.reshape(tiles * PIECE, LANES), cells, groups)
-    features = to_all(features, "head")
+    features = splat(received.reshape(tiles * PIECE, LANES), cells, groups, heads)
+    features = lax.all_to_all(features, "head", 0, 0)
     own = lax.axis_index("head").astype(jnp.int32).reshape(1)
     bev_rows, mixed = mlp(own, features, ow_all, bev_base[0], norm_gain[None, :], up_weight, down_weight)
     mixed = lax.all_to_all(mixed.reshape(heads, cells // heads, mixed.shape[1]), "head", 0, 0)

time: 168 us -> 150 us (0.89)
  blocking collectives: 103 us -> 87.6 us
  starting transfers between devices: 9.78 us -> 16.6 us
  other arithmetic: 5.54 us -> 0.77 us
  Pallas kernels: 20.9 us -> 17.4 us
  waiting for transfers between devices: 19.8 us -> 16.4 us
  local copies, waits for them, and re-layouts: 7.55 us -> 9.26 us
    all_to_all x1 -> x0, blocking collectives: 14.4 us -> none  [to_all(): lax.all_to_all(jnp.broadcast_to(x[None], (count,) + x.shape), axis, 0, 0)]
    all_to_all x0 -> x2, starting transfers between devices: none -> 10.4 us  [the longest x1 6.97 us: body(): q_all = lax.all_to_all(q_copies, 'y', 0, 0)]
    all_to_all x2 -> x1, waiting for transfers between devices: 19.8 us -> 9.51 us  [to_all(): lax.all_to_all(jnp.broadcast_to(x[None], (count,) + x.shape), axis, 0, 0)]
    all_to_all x0 -> x2, waiting for transfers between devices: none -> 6.89 us  [the longest x1 6.89 us: body(): features = lax.all_to_all(features, 'head', 0, 0)]
    unnamed x11 -> x18, local copies, waits for them, and re-layouts: 2.59 us -> 7.2 us
    pallas_call x1, Pallas kernels: 6.14 us -> 2.28 us  [mlp(): pl.pallas_call(mlp_kernel, out_shape=(jax.ShapeDtypeStruct((cells // head...]
    all_to_all x2 -> x1, starting transfers between devices: 7.87 us -> 4.29 us  [to_all(): lax.all_to_all(jnp.broadcast_to(x[None], (count,) + x.shape), axis, 0, 0)]
    reshape x2 -> x0, local copies, waits for them, and re-layouts: 2.08 us -> none  [the longest x1 1.17 us: body(): packed.reshape(tiles, PIECE, LANES)]
  transfers between devices with their start and end apart: 3 -> 4, of which waited for: 2 -> 2; matrix products, arithmetic and copies ran while one was open for 3% -> 1% of each run, Pallas kernels for 2% -> 3%
where the time goes in v2:
time: 150 us; the launch traced here: 148 us
  blocking collectives  87.6 us (58%)
  Pallas kernels  17.4 us (12%)
  starting transfers between devices  16.6 us (11%)
  waiting for transfers between devices  16.4 us (11%)
  local copies, waits for them, and re-layouts  9.26 us (6%)
    all_gather x1, blocking collectives, body(): own_kv = lax.all_gather(kv, 'z')  38.7 us
    all_to_all x1, blocking collectives, body(): lax.all_to_all(packed.reshape(tiles, PIECE, LANES), ('z', 'y', 'core'), 0...  35.6 us
    all_to_all x1, blocking collectives, body(): lax.all_to_all(mixed.reshape(heads, cells // heads, mixed.shape[1]), 'hea...  13.3 us
    all_to_all x1, waiting for transfers between devices, to_all(): lax.all_to_all(jnp.broadcast_to(x[None], (count,) + x.shape), axis, 0, 0)  9.51 us
    pallas_call x1, Pallas kernels, attend_second(): pl.pallas_call(functools.partial(second_kernel, tiles), out_shape=jax.Sha...  7.73 us
    unnamed x18, local copies, waits for them, and re-layouts  7.2 us
    all_to_all x1, starting transfers between devices, body(): q_all = lax.all_to_all(q_copies, 'y', 0, 0)  6.97 us
    all_to_all x1, waiting for transfers between devices, body(): features = lax.all_to_all(features, 'head', 0, 0)  6.89 us
  transfers between devices with their start and end apart: 4, of which 2 were waited for; matrix products, arithmetic and copies ran while one was open for 1% of the time, Pallas kernels for 3%

profile of v2, /device:TPU:56, one launch (start us, length us, event | category | flops | bytes accessed | tf_op | source)
XLA Modules:
  0.0 148.1 jit_solution(12335839224171161757)
XLA Ops:
  0.0 1.8 %prologue.1 = (bf16[4,160,256]{2,1,0:T(8,128)(2,1)}, bf16[320,128]{1,0:T(8,128)(2,1)}) custom-call(bf16[1,160,128]{2,1,0:T(8,128)(2,1)} %q_ref.1, bf16[1,160,128]{2,1,0:T(8,128)(2,1)} %k_ref.1, bf16[1,160,128]{2,1,0:T(8,128)(2,1)} %v_ref.1, s32[1,160]{1,0:T(1,128)} %bitcast.17, s32[1,160]{1,0:T(1,128)} %cell_ref.1, f32[1,160]{1,0:T(1,128)} %splat_ref.1), custom_call_target="tpu_custom_call" | custom-call | tf_op jit(solution)/shard_map/prologue/pallas_call | solution.py:57
  1.8 7.0 %all-to-all-start = ((bf16[4,160,256]{2,1,0:T(8,128)(2,1)}), bf16[4,160,256]{2,1,0:T(8,128)(2,1)S(1)}, u32[]{:S(2)}, u32[]{:S(2)}) async-start(bf16[4,160,256]{2,1,0:T(8,128)(2,1)} %get-tuple-element.12), calls=%async_computation | async-start | bytes 655360 | tf_op jit(solution)/shard_map/all_to_all | solution.py:311
  8.8 38.7 %all-gather = bf16[3840,128]{1,0:T(8,128)(2,1)S(1)} all-gather(bf16[320,128]{1,0:T(8,128)(2,1)} %get-tuple-element.11), channel_id=2, replica_groups=mesh['z'=12,'y'=4,'core'=2,'head'=4,'scene'=2] {'z'}, dimensions={0}, use_global_device_ids=true | all-gather | bytes 1064960 | tf_op jit(solution)/shard_map/all_gather | solution.py:313
  47.5 1.9 %collective-permute-start = (bf16[12,320,128]{2,1,0:T(8,128)(2,1)S(1)}, bf16[12,320,128]{2,1,0:T(8,128)(2,1)S(1)}, u32[]{:S(2)}, u32[]{:S(2)}) collective-permute-start(bf16[12,320,128]{2,1,0:T(8,128)(2,1)S(1)} %bitcast.11), channel_id=1, source_target_pairs={{0,8},{8,0},{1,9},{9,1},{2,10},{10,2},{3,11},{11,3},{4,12},{12,4},... | collective-permute-start | bytes 2949128 | tf_op jit(solution)/shard_map/ppermute | solution.py:314
  49.4 0.0 all-to-all-done.q_ref
  49.4 2.1 %broadcast_in_dim.12 = bf16[4,128,1024]{2,1,0:T(8,128)(2,1)} broadcast(bf16[128,1024]{1,0:T(8,128)(2,1)} %param.19), dimensions={1,2} | broadcast | bytes 1310720 | tf_op jit(solution)/shard_map/broadcast_in_dim | solution.py:287
  51.4 4.3 %all-to-all-start.1 = ((bf16[4,128,1024]{2,1,0:T(8,128)(2,1)}), bf16[4,128,1024]{2,1,0:T(8,128)(2,1)S(1)}, u32[]{:S(2)}, u32[]{:S(2)}) async-start(bf16[4,128,1024]{2,1,0:T(8,128)(2,1)} %broadcast_in_dim.12), calls=%async_computation.1 | async-start | bytes 2097152 | tf_op jit(solution)/shard_map/all_to_all | solution.py:287
  55.7 4.5 %attend_own_core.1 = (f32[2,640,128]{2,1,0:T(8,128)S(1)}, f32[2,640,128]{2,1,0:T(8,128)S(1)}) custom-call(bf16[12,320,128]{2,1,0:T(8,128)(2,1)S(1)} %bitcast.12, bf16[4,160,256]{2,1,0:T(8,128)(2,1)S(1)} %all-to-all-done.q_ref), custom_call_target="tpu_custom_call" | custom-call | flops 1258291200 | bytes 327680 | tf_op jit(solution)/shard_map/attend_own_core/pallas_call | solution.py:157
  60.3 0.0 copy-start.5
  60.3 0.9 copy-done.5
  61.2 0.8 copy-done.7
  62.0 9.5 %all-to-all-done.1._.ow_ref = bf16[4,128,1024]{2,1,0:T(8,128)(2,1)S(1)} async-done(((bf16[4,128,1024]{2,1,0:T(8,128)(2,1)}), bf16[4,128,1024]{2,1,0:T(8,128)(2,1)S(1)}, u32[]{:S(2)}, u32[]{:S(2)}) %all-to-all-start.1) | async-done | bytes 1048608 | tf_op jit(solution)/shard_map/all_to_all | solution.py:287
  71.5 0.0 collective-permute-done.kv_ref
  71.5 1.1 copy-done.6
  72.6 1.1 copy-done.8
  73.7 7.7 %attend_other_core.1 = bf16[2304,128]{1,0:T(8,128)(2,1)S(1)} custom-call(bf16[12,320,128]{2,1,0:T(8,128)(2,1)S(1)} %collective-permute-done.kv_ref, bf16[4,160,256]{2,1,0:T(8,128)(2,1)S(1)} %all-to-all-done.q_ref, f32[2,640,128]{2,1,0:T(8,128)S(1)} %copy-done.6, f32[2,640,128]{2,1,0:T(8,128)S(1)} %copy-done.8, bf16[4,128,1024]{2,1,0:T(8,128)(2,1)S(1)} %all-to-all-done.1._.ow_ref), custom_call_target="tpu_custom_call" | custom-call | flops 1258291200 | bytes 327680 | tf_op jit(solution)/shard_map/attend_other_core/pallas_call | solution.py:174
  81.4 0.0 copy-start
  81.4 0.0 copy-start.4
  81.4 35.6 %all_to_all.25 = bf16[96,24,128]{2,1,0:T(8,128)(2,1)S(1)} all-to-all(bf16[96,24,128]{2,1,0:T(8,128)(2,1)S(1)} %bitcast.13), channel_id=1, replica_groups=mesh['z'=12,'y'=4,'core'=2,'head'=4,'scene'=2] {'z','y','core'}, dimensions={0} | all-to-all | bytes 1179648 | tf_op jit(solution)/shard_map/all_to_all | solution.py:317
  117.1 1.0 join_splat.1
  118.1 0.0 copy-start.2
  118.1 0.7 copy-done.2
  118.8 3.4 %all-to-all-start.3 = ((bf16[4,256,128]{2,1,0:T(8,128)(2,1)}), bf16[4,256,128]{2,1,0:T(8,128)(2,1)S(1)}, u32[]{:S(2)}, u32[]{:S(2)}) async-start(bf16[4,256,128]{2,1,0:T(8,128)(2,1)} %copy-done.2), calls=%async_computation.3 | async-start | bytes 524288 | tf_op jit(solution)/shard_map/all_to_all | solution.py:319
  122.2 6.9 %all-to-all-done.3.f_ref = bf16[4,256,128]{2,1,0:T(8,128)(2,1)S(1)} async-done(((bf16[4,256,128]{2,1,0:T(8,128)(2,1)}), bf16[4,256,128]{2,1,0:T(8,128)(2,1)S(1)}, u32[]{:S(2)}, u32[]{:S(2)}) %all-to-all-start.3) | async-done | bytes 262176 | tf_op jit(solution)/shard_map/all_to_all | solution.py:319
  129.1 0.0 copy-done
  129.1 0.0 copy-done.4
  129.1 1.6 %copy-done.1 = bf16[1024,1024]{1,0:T(8,128)(2,1)S(1)} copy-done((bf16[1024,1024]{1,0:T(8,128)(2,1)S(1)}, bf16[1024,1024]{1,0:T(8,128)(2,1)}, u32[]{:S(2)}) %copy-start.1) | copy-done | bytes 2097176
  130.7 1.0 copy-done.3
  131.7 2.3 %project_mlp.1 = (f32[64,1024]{1,0:T(8,128)S(1)}, bf16[256,1024]{1,0:T(8,128)(2,1)S(1)}) custom-call(s32[1]{0:T(128)} %bitcast.own_ref, bf16[4,256,128]{2,1,0:T(8,128)(2,1)S(1)} %all-to-all-done.3.f_ref, bf16[4,128,1024]{2,1,0:T(8,128)(2,1)S(1)} %all-to-all-done.1._.ow_ref, bf16[256,1024]{1,0:T(8,128)(2,1)S(1)} %bitcast.15, f32[1,1024]{1,0:T(1,128)S(1)} %bitcast.16, ...), custom_call_target="tpu_custom_call" | custom-call | tf_op jit(solution)/shard_map/project_mlp/pallas_call | solution.py:271
  134.0 13.3 %all_to_all.26 = bf16[4,64,1024]{2,1,0:T(8,128)(2,1)S(1)} all-to-all(bf16[4,64,1024]{2,1,0:T(8,128)(2,1)S(1)} %bitcast.14), channel_id=1, replica_groups=mesh['z'=12,'y'=4,'core'=2,'head'=4,'scene'=2] {'head'}, dimensions={0} | all-to-all | bytes 1048576 | tf_op jit(solution)/shard_map/all_to_all | solution.py:322
  147.3 0.1 convert_reduce_fusion
  147.4 0.7 fusion
  (5 shorter events, 0.0 us)
Async XLA Ops:
  1.8 47.6 %all-to-all-start = ((bf16[4,160,256]{2,1,0:T(8,128)(2,1)}), bf16[4,160,256]{2,1,0:T(8,128)(2,1)S(1)}, u32[]{:S(2)}, u32[]{:S(2)}) async-start(bf16[4,160,256]{2,1,0:T(8,128)(2,1)} %get-tuple-element.12), calls=%async_computation | async-start | bytes 655360 | tf_op jit(solution)/shard_map/all_to_all | solution.py:311
  47.5 24.0 %collective-permute-start = (bf16[12,320,128]{2,1,0:T(8,128)(2,1)S(1)}, bf16[12,320,128]{2,1,0:T(8,128)(2,1)S(1)}, u32[]{:S(2)}, u32[]{:S(2)}) collective-permute-start(bf16[12,320,128]{2,1,0:T(8,128)(2,1)S(1)} %bitcast.11), channel_id=1, source_target_pairs={{0,8},{8,0},{1,9},{9,1},{2,10},{10,2},{3,11},{11,3},{4,12},{12,4},... | collective-permute-start | bytes 2949128 | tf_op jit(solution)/shard_map/ppermute | solution.py:314
  51.4 20.1 %all-to-all-start.1 = ((bf16[4,128,1024]{2,1,0:T(8,128)(2,1)}), bf16[4,128,1024]{2,1,0:T(8,128)(2,1)S(1)}, u32[]{:S(2)}, u32[]{:S(2)}) async-start(bf16[4,128,1024]{2,1,0:T(8,128)(2,1)} %broadcast_in_dim.12), calls=%async_computation.1 | async-start | bytes 2097152 | tf_op jit(solution)/shard_map/all_to_all | solution.py:287
  60.3 0.9 copy-start.5
  61.1 0.8 copy-start.7
  71.5 1.1 copy-start.6
  72.6 1.1 copy-start.8
  81.4 47.7 %copy-start = (bf16[1024,1024]{1,0:T(8,128)(2,1)S(1)}, bf16[1024,1024]{1,0:T(8,128)(2,1)}, u32[]{:S(2)}) copy-start(bf16[1024,1024]{1,0:T(8,128)(2,1)} %up_ref.1) | copy-start | bytes 6291460
  81.4 47.7 %copy-start.4 = (f32[1024]{0:T(1024)S(1)}, f32[1024]{0:T(1024)}, u32[]{:S(2)}) copy-start(f32[1024]{0:T(1024)} %param.18) | copy-start | bytes 12292
  118.1 0.7 copy-start.2
  118.8 10.3 %all-to-all-start.3 = ((bf16[4,256,128]{2,1,0:T(8,128)(2,1)}), bf16[4,256,128]{2,1,0:T(8,128)(2,1)S(1)}, u32[]{:S(2)}, u32[]{:S(2)}) async-start(bf16[4,256,128]{2,1,0:T(8,128)(2,1)} %copy-done.2), calls=%async_computation.3 | async-start | bytes 524288 | tf_op jit(solution)/shard_map/all_to_all | solution.py:319
  129.1 1.6 %copy-start.1 = (bf16[1024,1024]{1,0:T(8,128)(2,1)S(1)}, bf16[1024,1024]{1,0:T(8,128)(2,1)}, u32[]{:S(2)}) copy-start(bf16[1024,1024]{1,0:T(8,128)(2,1)} %down_ref.1) | copy-start | bytes 6291460
  130.7 1.0 copy-start.3

commit v3 on v2

v3 whole, which is shorter than its diff:
```python
import functools
import math

import jax
import jax.numpy as jnp
from jax import lax
from jax.experimental import pallas as pl
from jax.experimental.pallas import tpu as pltpu
from jax.sharding import Mesh
from jax.sharding import PartitionSpec as P

HS = 64
LANES = 128
SLOTS = 4
PIECE = 8
EXTRA = 16
EXPONENT = math.log2(math.e) / math.sqrt(HS)
MIB = 1024 * 1024

f32 = jnp.float32
bf16 = jnp.bfloat16


def dot(a, b):
    return lax.dot_general(a, b, (((1,), (0,)), ((), ())), preferred_element_type=f32)


def dot_nt(a, b):
    return lax.dot_general(a, b, (((1,), (1,)), ((), ())), preferred_element_type=f32)


def prologue_kernel(q_ref, k_ref, v_ref, q_out, kv_out):
    tok = q_ref.shape[1]
    for copy in range(q_out.shape[0]):
        q_out[copy] = q_ref[0]
    kv_out[:tok, :] = k_ref[0]
    kv_out[tok:, :] = v_ref[0]


def prologue(queries, key_states, value_states, copies):
    tok = queries.shape[1]
    vmem = pl.BlockSpec(memory_space=pltpu.VMEM)
    return pl.pallas_call(
        prologue_kernel,
        out_shape=(
            jax.ShapeDtypeStruct((copies, tok, LANES), bf16),
            jax.ShapeDtypeStruct((2 * tok, LANES), bf16),
        ),
        in_specs=[vmem] * 3,
        out_specs=(vmem, vmem),
        compiler_params=pltpu.CompilerParams(vmem_limit_bytes=58 * MIB),
        name="prologue",
    )(queries, key_states, value_states)


def attend_block(q_ref, group, k_s, v_s):
    low = lax.broadcasted_iota(jnp.int32, (1, LANES), 1) < HS
    q = q_ref[group]
    for head in range(2):
        keep = jnp.where(low if head == 0 else ~low, 1.0, 0.0).astype(bf16)
        s = dot_nt(q * keep, k_s[...])
        top = jnp.max(s, axis=1, keepdims=True)
        p = jnp.exp2((s - top) * EXPONENT).astype(bf16)
        yield head, top * EXPONENT, dot(p, v_s[head])


def stage_keys(kv_ref, k_s, v_s):
    blocks, tok = kv_ref.shape[0], kv_ref.shape[1] // 2
    span = blocks * tok
    low = jnp.where(lax.broadcasted_iota(jnp.int32, (1, LANES), 1) < HS, 1.0, 0.0)
    low_b, high_b = low.astype(bf16), (1.0 - low).astype(bf16)
    k_s[...] = kv_ref[:, :tok, :].reshape(span, LANES)
    values = kv_ref[:, tok:, :].reshape(span, LANES)
    v_s[0] = values * low_b + high_b
    v_s[1] = values * high_b + low_b


def other_half(head):
    return (LANES - 1, LANES - 2) if head == 0 else (0, 1)


def first_kernel(kv_ref, q_ref, sum_ref, k_s, v_s):
    groups, tok = q_ref.shape[0], q_ref.shape[1]
    stage_keys(kv_ref, k_s, v_s)
    lane = lax.broadcasted_iota(jnp.int32, (1, LANES), 1)
    for group in range(groups):
        for head, top, sums in attend_block(q_ref, group, k_s, v_s):
            sum_ref[head, pl.ds(group * tok, tok), :] = jnp.where(lane == other_half(head)[1], top, sums)


def second_kernel(kv_ref, q_ref, sum_ref, out_ref, k_s, v_s, lse_s):
    groups, tok = q_ref.shape[0], q_ref.shape[1]
    padded = lse_s.shape[0] // groups
    stage_keys(kv_ref, k_s, v_s)
    lane = lax.broadcasted_iota(jnp.int32, (tok, LANES), 1)
    lse_s[...] = jnp.zeros_like(lse_s)
    for group in range(groups):
        sums = []
        extra = jnp.zeros((tok, LANES), f32)
        for head, top_b, sum_b in attend_block(q_ref, group, k_s, v_s):
            at, top_at = other_half(head)
            sum_a = sum_ref[head, pl.ds(group * tok, tok), :]
            top_a = sum_a[:, top_at : top_at + 1]
            top = jnp.maximum(top_a, top_b)
            o = sum_a * jnp.exp2(top_a - top) + sum_b * jnp.exp2(top_b - top)
            total = o[:, at : at + 1]
            sums.append(o * (1.0 / total))
            left = top + jnp.log2(total)
            for step in range(3):
                piece = left.astype(bf16).astype(f32)
                left = left - piece
                extra = jnp.where(lane == 2 * step + head, piece, extra)
        out_ref[group, :tok, :] = jnp.where(lane < HS, sums[0], sums[1]).astype(bf16)
        lse_s[pl.ds(group * padded, tok), :] = extra
    turned = jnp.transpose(lse_s[...])[:8, :]
    for group in range(groups):
        for half in range(2):
            begin = group * padded + half * LANES
            out_ref[group, pl.ds(tok + 8 * half, 8), :] = turned[:, begin : begin + LANES].astype(bf16)


def attention_cost(queries, keys):
    return pl.CostEstimate(
        flops=2 * 2 * 2 * queries * keys * LANES, bytes_accessed=4 * queries * LANES, transcendentals=2 * queries * keys
    )


def attend_first(kv, q_all):
    blocks, tok2, _ = kv.shape
    groups, tok, _ = q_all.shape
    span, rows = blocks * tok2 // 2, groups * tok
    vmem = pl.BlockSpec(memory_space=pltpu.VMEM)
    return pl.pallas_call(
        first_kernel,
        out_shape=jax.ShapeDtypeStruct((2, rows, LANES), f32),
        in_specs=[vmem, vmem],
        out_specs=vmem,
        scratch_shapes=[pltpu.VMEM((span, LANES), bf16), pltpu.VMEM((2, span, LANES), bf16)],
        compiler_params=pltpu.CompilerParams(vmem_limit_bytes=16 * MIB),
        cost_estimate=attention_cost(rows, span),
        name="attend_own_core",
    )(kv, q_all)


def attend_second(kv, q_all, sums):
    blocks, tok2, _ = kv.shape
    groups, tok, _ = q_all.shape
    span, rows = blocks * tok2 // 2, groups * tok
    vmem = pl.BlockSpec(memory_space=pltpu.VMEM)
    return pl.pallas_call(
        second_kernel,
        out_shape=jax.ShapeDtypeStruct((groups, tok + EXTRA, LANES), bf16),
        in_specs=[vmem] * 3,
        out_specs=vmem,
        scratch_shapes=[
            pltpu.VMEM((span, LANES), bf16),
            pltpu.VMEM((2, span, LANES), bf16),
            pltpu.VMEM((groups * 2 * LANES, LANES), f32),
        ],
        compiler_params=pltpu.CompilerParams(vmem_limit_bytes=16 * MIB),
        cost_estimate=attention_cost(rows, span),
        name="attend_other_core",
    )(kv, q_all, sums)


def join_kernel(tiles, x_ref, _, tile_ref, cell_ref, splat_ref, out_ref, rows_s):
    groups, tok = x_ref.shape[0], x_ref.shape[1] - EXTRA
    width = 2 * LANES
    rows_s[...] = jnp.zeros_like(rows_s)
    rows_s[0:1, :tok] = splat_ref[...]
    halves = [x_ref[:, pl.ds(tok + 8 * half, 8), :].astype(f32) for half in range(2)]
    parts = jnp.concatenate(halves, axis=2)
    lse = parts + pltpu.roll(parts, 6, 1) + pltpu.roll(parts, 4, 1)
    top = jnp.max(lse, axis=0, keepdims=True)
    power = jnp.exp2(lse - top)
    weight = power * (rows_s[0:1, :] / jnp.sum(power, axis=0, keepdims=True))
    rows_s[: 8 * groups, :] = weight.reshape(8 * groups, width)
    tile = tile_ref[...].astype(f32)
    rows_s[64:65, :tok] = tile
    rows_s[65:66, :tok] = (cell_ref[...] + 1).astype(f32)
    columns = jnp.transpose(rows_s[...])[:tok, :]
    lane = lax.broadcasted_iota(jnp.int32, (tok, LANES), 1)
    weighted = jnp.zeros((tok, LANES), f32)
    for group in range(groups):
        by = jnp.where(lane < HS, columns[:, 8 * group : 8 * group + 1], columns[:, 8 * group + 1 : 8 * group + 2])
        weighted = weighted + x_ref[group, :tok, :].astype(f32) * by
    tile_column, cell_column = columns[:, 64:65], columns[:, 65:66]
    down = lax.broadcasted_iota(jnp.int32, (tok, tok), 0)
    across = lax.broadcasted_iota(jnp.int32, (tok, tok), 1)
    alike = jnp.where(tile_column == tile, 1.0, 0.0)
    rank_row = jnp.sum(jnp.where(down < across, alike, 0.0), axis=0, keepdims=True)
    rank_column = jnp.sum(jnp.where(across < down, alike, 0.0), axis=1, keepdims=True)
    cells = jnp.where(lane.astype(f32) == rank_column, cell_column, 0.0).astype(bf16)
    row = lax.broadcasted_iota(jnp.int32, (tiles * PIECE, tok), 0).astype(f32)
    main = jnp.where(row == tile * PIECE + rank_row, 1.0, 0.0).astype(bf16)
    tail = jnp.where(row == tile * PIECE + float(SLOTS), 1.0, 0.0).astype(bf16)
    out_ref[...] = (dot(main, weighted.astype(bf16)) + dot(tail, cells)).astype(bf16)


def join(received, early, tile, cell, splat_weight, tiles):
    vmem = pl.BlockSpec(memory_space=pltpu.VMEM)
    return pl.pallas_call(
        functools.partial(join_kernel, tiles),
        out_shape=jax.ShapeDtypeStruct((tiles * PIECE, LANES), bf16),
        in_specs=[vmem, pl.BlockSpec(memory_space=pl.ANY)] + [vmem] * 3,
        out_specs=vmem,
        scratch_shapes=[pltpu.VMEM((LANES, 2 * LANES), f32)],
        compiler_params=pltpu.CompilerParams(vmem_limit_bytes=8 * MIB),
        name="join_pack",
    )(received, early, tile, cell, splat_weight)


def splat_kernel(x_ref, out_ref, x_s, y_s, r_s):
    sources = x_ref.shape[0] // PIECE
    cells = out_ref.shape[1]
    x_s[...] = x_ref[...].astype(f32)
    y_s[...] = jnp.zeros_like(y_s)
    y_s[:sources, :] = x_s[pl.ds(SLOTS, sources, stride=PIECE), :]
    y_t = jnp.transpose(y_s[...])
    r_s[...] = jnp.zeros_like(r_s)
    for slot in range(SLOTS):
        r_s[pl.ds(slot * LANES, sources), :] = x_s[pl.ds(slot, sources, stride=PIECE), :].astype(bf16)
    cell = (lax.broadcasted_iota(jnp.int32, (cells, LANES), 0) + 1).astype(f32)
    hits = [jnp.where(cell == y_t[slot : slot + 1, :], 1.0, 0.0).astype(bf16) for slot in range(SLOTS)]
    features = dot(jnp.concatenate(hits, axis=1), r_s[...]).astype(bf16)
    for copy in range(out_ref.shape[0]):
        out_ref[copy] = features


def splat(received, cells, copies):
    rows = received.shape[0]
    vmem = pl.BlockSpec(memory_space=pltpu.VMEM)
    return pl.pallas_call(
        splat_kernel,
        out_shape=jax.ShapeDtypeStruct((copies, cells, LANES), bf16),
        in_specs=[vmem],
        out_specs=vmem,
        scratch_shapes=[
            pltpu.VMEM((rows, LANES), f32),
            pltpu.VMEM((LANES, LANES), f32),
            pltpu.VMEM((SLOTS * LANES, LANES), bf16),
        ],
        compiler_params=pltpu.CompilerParams(vmem_limit_bytes=8 * MIB),
        name="splat",
    )(received)


def mlp_kernel(own_ref, f_ref, near_ref, far_ref, base_ref, gain_ref, up_hbm, down_hbm, bev_ref, mix_ref, bev_s, up_ref, down_ref, sems):
    copies = [
        pltpu.make_async_copy(up_hbm, up_ref, sems.at[0]),
        pltpu.make_async_copy(down_hbm, down_ref, sems.at[1]),
    ]
    for copy in copies:
        copy.start()
    share = bev_ref.shape[0]
    own = own_ref[0]
    near = jnp.concatenate([f_ref[own], f_ref[own ^ 1]], axis=1)
    far = jnp.concatenate([f_ref[own ^ 2], f_ref[own ^ 3]], axis=1)
    depth = near.shape[1]
    bev = (
        base_ref[...].astype(f32)
        + dot(near, near_ref[...].reshape(depth, -1))
        + dot(far, far_ref[...].reshape(depth, -1))
    )
    bev_s[...] = bev
    mean_square = jnp.mean(bev * bev, axis=1, keepdims=True)
    normed = (bev * lax.rsqrt(mean_square + 1e-06) * gain_ref[...]).astype(bf16)
    bev_ref[...] = bev_s[pl.ds(pl.multiple_of(own * share, share), share), :]
    step = 256
    mixed = None
    copies[0].wait()
    for begin in range(0, up_ref.shape[1], step):
        u = dot(normed, up_ref[:, begin : begin + step])
        hidden = (0.5 * u * (1.0 + lax.erf(u * math.sqrt(0.5)))).astype(bf16)
        if begin == 0:
            copies[1].wait()
        term = dot(hidden, down_ref[begin : begin + step, :])
        mixed = term if mixed is None else mixed + term
    mix_ref[...] = mixed.astype(bf16)


def mlp(own, features, near, far, base, gain, up, down):
    heads = features.shape[0]
    cells, width = base.shape
    vmem, hbm = pl.BlockSpec(memory_space=pltpu.VMEM), pl.BlockSpec(memory_space=pl.ANY)
    return pl.pallas_call(
        mlp_kernel,
        out_shape=(
            jax.ShapeDtypeStruct((cells // heads, width), f32),
            jax.ShapeDtypeStruct((cells, width), bf16),
        ),
        in_specs=[pl.BlockSpec(memory_space=pltpu.SMEM)] + [vmem] * 5 + [hbm] * 2,
        out_specs=(vmem, vmem),
        scratch_shapes=[
            pltpu.VMEM((cells, width), f32),
            pltpu.VMEM(up.shape, bf16),
            pltpu.VMEM(down.shape, bf16),
            pltpu.SemaphoreType.DMA((2,)),
        ],
        compiler_params=pltpu.CompilerParams(vmem_limit_bytes=24 * MIB),
        name="project_mlp",
    )(own, features, near, far, base, gain, up, down)


def swap(x, axis, bit):
    return lax.ppermute(x, axis, [(i, i ^ bit) for i in range(lax.axis_size(axis))])


def body(
    queries,
    key_states,
    value_states,
    splat_weight,
    tile_of,
    cell_of,
    bev_base,
    norm_gain,
    out_weight,
    up_weight,
    down_weight,
):
    tok = queries.shape[1]
    tiles = lax.axis_size("z") * lax.axis_size("y") * lax.axis_size("core")
    groups = lax.axis_size("y")
    heads = lax.axis_size("head")
    cells = bev_base.shape[1]
    q_copies, kv = prologue(queries, key_states, value_states, groups)
    q_all = lax.all_to_all(q_copies, "y", 0, 0)
    near_weight = jnp.stack([out_weight, swap(out_weight, "head", 1)])
    own_kv = lax.all_gather(kv, "z")
    own_kv, q_all, near_weight = lax.optimization_barrier((own_kv, q_all, near_weight))
    other_kv = swap(own_kv, "core", 1)
    far_weight = swap(near_weight, "head", 2)
    sums = attend_first(own_kv, q_all)
    partial = attend_second(other_kv, q_all, sums)
    partial = lax.all_to_all(partial, "y", 0, 0)
    packed = join(partial, far_weight, tile_of.reshape(1, tok), cell_of, splat_weight, tiles)
    received = lax.all_to_all(packed.reshape(tiles, PIECE, LANES), ("z", "y", "core"), 0, 0)
    features = splat(received.reshape(tiles * PIECE, LANES), cells, heads)
    features = lax.all_to_all(features, "head", 0, 0)
    own = lax.axis_index("head").astype(jnp.int32).reshape(1)
    bev_rows, mixed = mlp(
        own, features, near_weight, far_weight, bev_base[0], norm_gain[None, :], up_weight, down_weight
    )
    mixed = lax.all_to_all(mixed.reshape(heads, cells // heads, mixed.shape[1]), "head", 0, 0)
    return (bev_rows + jnp.sum(mixed.astype(f32), axis=0)).astype(bf16)[None]


def solution(mesh):
    core, y = 2, 4
    z = mesh.shape["ctx"] // (core * y)
    split = Mesh(
        mesh.devices.reshape(z, y, core, mesh.shape["head"], mesh.shape["scene"]),
        ("z", "y", "core", "head", "scene"),
    )
    ctx = ("z", "y", "core")
    placed = (
        P("scene", ctx, "head"),
        P("scene", ctx, "head"),
        P("scene", ctx, "head"),
        P("scene", ctx),
        P("scene", ctx, None),
        P("scene", ctx),
        P("scene", ctx, None),
        P(),
        P("head", None),
        P(None, "head"),
        P("head", None),
    )
    return jax.shard_map(
        body,
        mesh=split,
        in_specs=placed,
        out_specs=P("scene", ctx + ("head",), None),
        check_vma=False,
    )
```

time: 150 us -> 140 us (0.933)
  blocking collectives: 87.6 us -> 73.6 us
  starting transfers between devices: 16.6 us -> 27.7 us
  local copies, waits for them, and re-layouts: 9.26 us -> 3.35 us
    all_to_all x1, blocking collectives: 35.6 us -> 22.2 us  [body(): lax.all_to_all(packed.reshape(tiles, PIECE, LANES), ('z', 'y', 'core'), 0...]
    ppermute x1 -> x3, starting transfers between devices: 1.91 us -> 9.95 us  [swap(): lax.ppermute(x, axis, [(i, i ^ bit) for i in range(lax.axis_size(axis))])]
    unnamed x18 -> x16, local copies, waits for them, and re-layouts: 7.2 us -> 3.35 us
    all_to_all x1, starting transfers between devices: 4.29 us -> 7.33 us  [body(): partial = lax.all_to_all(partial, 'y', 0, 0)]
    all_to_all x1, waiting for transfers between devices: 9.51 us -> 7.23 us  [body(): partial = lax.all_to_all(partial, 'y', 0, 0)]
    broadcast_in_dim x1 -> x0, local copies, waits for them, and re-layouts: 2.06 us -> none  [to_all(): jnp.broadcast_to(x[None], (count,) + x.shape)]
    pallas_call x3 -> x4, Pallas kernels: 13.3 us -> 11.5 us  [the longest x1 5.64 us: attend_second(): pl.pallas_call(second_kernel, out_shape=jax.ShapeDtypeStruct((groups, tok...]
  transfers between devices with their start and end apart: 4 -> 6, of which waited for: 2 -> 2; matrix products, arithmetic and copies ran while one was open for 1% -> 1% of each run, Pallas kernels for 3% -> 7%
where the time goes in v3:
time: 140 us; the launch traced here: 138 us
  blocking collectives  73.6 us (53%)
  starting transfers between devices  27.7 us (20%)
  Pallas kernels  16.1 us (12%)
  waiting for transfers between devices  14.9 us (11%)
  local copies, waits for them, and re-layouts  3.35 us (2%)
  other arithmetic  1.77 us (1%)
    all_gather x1, blocking collectives, body(): own_kv = lax.all_gather(kv, 'z')  38.9 us
    all_to_all x1, blocking collectives, body(): lax.all_to_all(packed.reshape(tiles, PIECE, LANES), ('z', 'y', 'core'), 0...  22.2 us
    all_to_all x1, blocking collectives, body(): lax.all_to_all(mixed.reshape(heads, cells // heads, mixed.shape[1]), 'hea...  12.5 us
    ppermute x3, starting transfers between devices, swap(): lax.ppermute(x, axis, [(i, i ^ bit) for i in range(lax.axis_size(axis))])  9.95 us
    all_to_all x1, waiting for transfers between devices, body(): features = lax.all_to_all(features, 'head', 0, 0)  7.64 us
    all_to_all x1, starting transfers between devices, body(): partial = lax.all_to_all(partial, 'y', 0, 0)  7.33 us
    all_to_all x1, waiting for transfers between devices, body(): partial = lax.all_to_all(partial, 'y', 0, 0)  7.23 us
    all_to_all x1, starting transfers between devices, body(): q_all = lax.all_to_all(q_copies, 'y', 0, 0)  6.97 us
  transfers between devices with their start and end apart: 6, of which 2 were waited for; matrix products, arithmetic and copies ran while one was open for 1% of the time, Pallas kernels for 7%

profile of v3, /device:TPU:56, one launch (start us, length us, event | category | flops | bytes accessed | tf_op | source)
XLA Modules:
  0.0 137.5 jit_solution(8193862749958489448)
XLA Ops:
  0.0 1.5 %prologue.1 = (bf16[4,160,128]{2,1,0:T(8,128)(2,1)}, bf16[320,128]{1,0:T(8,128)(2,1)}) custom-call(bf16[1,160,128]{2,1,0:T(8,128)(2,1)} %q_ref.1, bf16[1,160,128]{2,1,0:T(8,128)(2,1)} %k_ref.1, bf16[1,160,128]{2,1,0:T(8,128)(2,1)} %v_ref.1), custom_call_target="tpu_custom_call" | custom-call | tf_op jit(solution)/shard_map/prologue/pallas_call | solution.py:43
  1.5 7.0 %all-to-all-start = ((bf16[4,160,128]{2,1,0:T(8,128)(2,1)}), bf16[4,160,128]{2,1,0:T(8,128)(2,1)S(1)}, u32[]{:S(2)}, u32[]{:S(2)}) async-start(bf16[4,160,128]{2,1,0:T(8,128)(2,1)} %get-tuple-element.13), calls=%async_computation | async-start | bytes 327680 | tf_op jit(solution)/shard_map/all_to_all | solution.py:328
  8.5 3.4 %collective-permute-start = (bf16[128,1024]{1,0:T(8,128)(2,1)}, bf16[128,1024]{1,0:T(8,128)(2,1)S(1)}, u32[]{:S(2)}, u32[]{:S(2)}) collective-permute-start(bf16[128,1024]{1,0:T(8,128)(2,1)} %param.19), channel_id=1, source_target_pairs={{0,2},{2,0},{4,6},{6,4},{1,3},{3,1},{5,7},{7,5},{8,10},{10,8},{12,... | collective-permute-start | bytes 786440 | tf_op jit(solution)/shard_map/ppermute | solution.py:306
  11.9 38.9 %all-gather = bf16[3840,128]{1,0:T(8,128)(2,1)S(1)} all-gather(bf16[320,128]{1,0:T(8,128)(2,1)} %get-tuple-element.12), channel_id=2, replica_groups=mesh['z'=12,'y'=4,'core'=2,'head'=4,'scene'=2] {'z'}, dimensions={0}, use_global_device_ids=true | all-gather | bytes 1064960 | tf_op jit(solution)/shard_map/all_gather | solution.py:330
  50.8 0.0 collective-permute-done
  50.8 1.0 pad_maximum_fusion.near_ref
  51.8 0.0 all-to-all-done.q_ref
  51.8 1.9 %collective-permute-start.1 = (bf16[12,320,128]{2,1,0:T(8,128)(2,1)S(1)}, bf16[12,320,128]{2,1,0:T(8,128)(2,1)S(1)}, u32[]{:S(2)}, u32[]{:S(2)}) collective-permute-start(bf16[12,320,128]{2,1,0:T(8,128)(2,1)S(1)} %bitcast.12), channel_id=1, source_target_pairs={{0,8},{8,0},{1,9},{9,1},{2,10},{10,2},{3,11},{11,3},{4,12},{12,4},... | collective-permute-start | bytes 2949128 | tf_op jit(solution)/shard_map/ppermute | solution.py:306
  53.7 4.6 %collective-permute-start.2 = (bf16[2,128,1024]{2,1,0:T(8,128)(2,1)S(1)}, bf16[2,128,1024]{2,1,0:T(8,128)(2,1)S(1)}, u32[]{:S(2)}, u32[]{:S(2)}) collective-permute-start(bf16[2,128,1024]{2,1,0:T(8,128)(2,1)S(1)} %pad_maximum_fusion.near_ref), channel_id=1, source_target_pairs={{0,4},{2,6},{4,0},{6,2},{1,5},{3,7},{5,1},{7,3},{8,12},{10,14},{12... | collective-permute-start | bytes 1572872 | tf_op jit(solution)/shard_map/ppermute | solution.py:306
  58.4 4.5 %attend_own_core.1.sum_ref = f32[2,640,128]{2,1,0:T(8,128)S(1)} custom-call(bf16[12,320,128]{2,1,0:T(8,128)(2,1)S(1)} %bitcast.13, bf16[4,160,128]{2,1,0:T(8,128)(2,1)S(1)} %all-to-all-done.q_ref), custom_call_target="tpu_custom_call" | custom-call | flops 1258291200 | bytes 327680 | tf_op jit(solution)/shard_map/attend_own_core/pallas_call | solution.py:133
  62.9 0.0 copy-start.5
  62.9 0.0 copy-start.6
  62.9 0.0 copy-start.7
  62.9 0.0 collective-permute-done.1.kv_ref
  62.9 5.6 %attend_other_core.1 = bf16[4,176,128]{2,1,0:T(8,128)(2,1)} custom-call(bf16[12,320,128]{2,1,0:T(8,128)(2,1)S(1)} %collective-permute-done.1.kv_ref, bf16[4,160,128]{2,1,0:T(8,128)(2,1)S(1)} %all-to-all-done.q_ref, f32[2,640,128]{2,1,0:T(8,128)S(1)} %attend_own_core.1.sum_ref), custom_call_target="tpu_custom_call" | custom-call | flops 1258291200 | bytes 327680 | tf_op jit(solution)/shard_map/attend_other_core/pallas_call | solution.py:150
  68.6 7.3 %all-to-all-start.1 = ((bf16[4,176,128]{2,1,0:T(8,128)(2,1)}), bf16[4,176,128]{2,1,0:T(8,128)(2,1)S(1)}, u32[]{:S(2)}, u32[]{:S(2)}) async-start(bf16[4,176,128]{2,1,0:T(8,128)(2,1)} %attend_other_core.1), calls=%async_computation.1 | async-start | bytes 360448 | tf_op jit(solution)/shard_map/all_to_all | solution.py:336
  75.9 0.0 collective-permute-done.2._.far_ref
  75.9 7.2 %all-to-all-done.1.x_ref = bf16[4,176,128]{2,1,0:T(8,128)(2,1)S(1)} async-done(((bf16[4,176,128]{2,1,0:T(8,128)(2,1)}), bf16[4,176,128]{2,1,0:T(8,128)(2,1)S(1)}, u32[]{:S(2)}, u32[]{:S(2)}) %all-to-all-start.1) | async-done | bytes 180256 | tf_op jit(solution)/shard_map/all_to_all | solution.py:336
  83.2 0.0 copy-done.5
  83.2 0.0 copy-done.7
  83.2 1.0 join_pack.1
  84.2 22.2 %all_to_all.25 = bf16[96,8,128]{2,1,0:T(8,128)(2,1)S(1)} all-to-all(bf16[96,8,128]{2,1,0:T(8,128)(2,1)S(1)} %bitcast.15), channel_id=1, replica_groups=mesh['z'=12,'y'=4,'core'=2,'head'=4,'scene'=2] {'z','y','core'}, dimensions={0} | all-to-all | bytes 393216 | tf_op jit(solution)/shard_map/all_to_all | solution.py:338
  106.4 0.3 splat.1
  106.7 0.7 copy-done.2
  107.4 3.4 %all-to-all-start.3 = ((bf16[4,256,128]{2,1,0:T(8,128)(2,1)}), bf16[4,256,128]{2,1,0:T(8,128)(2,1)S(1)}, u32[]{:S(2)}, u32[]{:S(2)}) async-start(bf16[4,256,128]{2,1,0:T(8,128)(2,1)} %copy-done.2), calls=%async_computation.3 | async-start | bytes 524288 | tf_op jit(solution)/shard_map/all_to_all | solution.py:340
  110.8 7.6 %all-to-all-done.3.f_ref = bf16[4,256,128]{2,1,0:T(8,128)(2,1)S(1)} async-done(((bf16[4,256,128]{2,1,0:T(8,128)(2,1)}), bf16[4,256,128]{2,1,0:T(8,128)(2,1)S(1)}, u32[]{:S(2)}, u32[]{:S(2)}) %all-to-all-start.3) | async-done | bytes 262176 | tf_op jit(solution)/shard_map/all_to_all | solution.py:340
  118.5 1.6 %copy-done.1 = bf16[1024,1024]{1,0:T(8,128)(2,1)S(1)} copy-done((bf16[1024,1024]{1,0:T(8,128)(2,1)S(1)}, bf16[1024,1024]{1,0:T(8,128)(2,1)}, u32[]{:S(2)}) %copy-start.1) | copy-done | bytes 2097176
  120.1 1.0 copy-done.3
  121.1 3.1 %project_mlp.1 = (f32[64,1024]{1,0:T(8,128)S(1)}, bf16[256,1024]{1,0:T(8,128)(2,1)S(1)}) custom-call(s32[1]{0:T(128)} %bitcast.own_ref, bf16[4,256,128]{2,1,0:T(8,128)(2,1)S(1)} %all-to-all-done.3.f_ref, bf16[2,128,1024]{2,1,0:T(8,128)(2,1)S(1)} %pad_maximum_fusion.near_ref, bf16[2,128,1024]{2,1,0:T(8,128)(2,1)S(1)} %collective-permute-done.2._.far_ref, ...), custom_call_target="tpu_custom_call" | custom-call | tf_op jit(solution)/shard_map/project_mlp/pallas_call | solution.py:286
  124.2 12.5 %all_to_all.26 = bf16[4,64,1024]{2,1,0:T(8,128)(2,1)S(1)} all-to-all(bf16[4,64,1024]{2,1,0:T(8,128)(2,1)S(1)} %bitcast.16), channel_id=1, replica_groups=mesh['z'=12,'y'=4,'core'=2,'head'=4,'scene'=2] {'head'}, dimensions={0} | all-to-all | bytes 1048576 | tf_op jit(solution)/shard_map/all_to_all | solution.py:345
  136.7 0.1 convert_reduce_fusion
  136.8 0.7 fusion
  (8 shorter events, 0.0 us)
Async XLA Ops:
  1.5 50.2 %all-to-all-start = ((bf16[4,160,128]{2,1,0:T(8,128)(2,1)}), bf16[4,160,128]{2,1,0:T(8,128)(2,1)S(1)}, u32[]{:S(2)}, u32[]{:S(2)}) async-start(bf16[4,160,128]{2,1,0:T(8,128)(2,1)} %get-tuple-element.13), calls=%async_computation | async-start | bytes 327680 | tf_op jit(solution)/shard_map/all_to_all | solution.py:328
  8.5 42.3 %collective-permute-start = (bf16[128,1024]{1,0:T(8,128)(2,1)}, bf16[128,1024]{1,0:T(8,128)(2,1)S(1)}, u32[]{:S(2)}, u32[]{:S(2)}) collective-permute-start(bf16[128,1024]{1,0:T(8,128)(2,1)} %param.19), channel_id=1, source_target_pairs={{0,2},{2,0},{4,6},{6,4},{1,3},{3,1},{5,7},{7,5},{8,10},{10,8},{12,... | collective-permute-start | bytes 786440 | tf_op jit(solution)/shard_map/ppermute | solution.py:306
  51.8 11.2 %collective-permute-start.1 = (bf16[12,320,128]{2,1,0:T(8,128)(2,1)S(1)}, bf16[12,320,128]{2,1,0:T(8,128)(2,1)S(1)}, u32[]{:S(2)}, u32[]{:S(2)}) collective-permute-start(bf16[12,320,128]{2,1,0:T(8,128)(2,1)S(1)} %bitcast.12), channel_id=1, source_target_pairs={{0,8},{8,0},{1,9},{9,1},{2,10},{10,2},{3,11},{11,3},{4,12},{12,4},... | collective-permute-start | bytes 2949128 | tf_op jit(solution)/shard_map/ppermute | solution.py:306
  53.7 22.2 %collective-permute-start.2 = (bf16[2,128,1024]{2,1,0:T(8,128)(2,1)S(1)}, bf16[2,128,1024]{2,1,0:T(8,128)(2,1)S(1)}, u32[]{:S(2)}, u32[]{:S(2)}) collective-permute-start(bf16[2,128,1024]{2,1,0:T(8,128)(2,1)S(1)} %pad_maximum_fusion.near_ref), channel_id=1, source_target_pairs={{0,4},{2,6},{4,0},{6,2},{1,5},{3,7},{5,1},{7,3},{8,12},{10,14},{12... | collective-permute-start | bytes 1572872 | tf_op jit(solution)/shard_map/ppermute | solution.py:306
  62.9 20.3 %copy-start.5 = (s32[1,160,1]{1,2,0:T(1,128)S(1)}, s32[1,160,1]{1,2,0:T(1,128)}, u32[]{:S(2)}) copy-start(s32[1,160,1]{1,2,0:T(1,128)} %param.15) | copy-start | bytes 1924
  62.9 20.3 %copy-start.6 = (s32[1,160]{1,0:T(1,128)S(1)}, s32[1,160]{1,0:T(1,128)}, u32[]{:S(2)}) copy-start(s32[1,160]{1,0:T(1,128)} %cell_ref.1) | copy-start | bytes 1924
  62.9 20.2 %copy-start.7 = (f32[1,160]{1,0:T(1,128)S(1)}, f32[1,160]{1,0:T(1,128)}, u32[]{:S(2)}) copy-start(f32[1,160]{1,0:T(1,128)} %splat_ref.1) | copy-start | bytes 1924
  68.6 49.9 %copy-start = (bf16[1024,1024]{1,0:T(8,128)(2,1)S(1)}, bf16[1024,1024]{1,0:T(8,128)(2,1)}, u32[]{:S(2)}) copy-start(bf16[1024,1024]{1,0:T(8,128)(2,1)} %up_hbm.1) | copy-start | bytes 6291460
  68.6 49.9 %copy-start.4 = (f32[1024]{0:T(1024)S(1)}, f32[1024]{0:T(1024)}, u32[]{:S(2)}) copy-start(f32[1024]{0:T(1024)} %param.18) | copy-start | bytes 12292
  68.6 14.6 %all-to-all-start.1 = ((bf16[4,176,128]{2,1,0:T(8,128)(2,1)}), bf16[4,176,128]{2,1,0:T(8,128)(2,1)S(1)}, u32[]{:S(2)}, u32[]{:S(2)}) async-start(bf16[4,176,128]{2,1,0:T(8,128)(2,1)} %attend_other_core.1), calls=%async_computation.1 | async-start | bytes 360448 | tf_op jit(solution)/shard_map/all_to_all | solution.py:336
  106.7 0.7 copy-start.2
  107.4 11.1 %all-to-all-start.3 = ((bf16[4,256,128]{2,1,0:T(8,128)(2,1)}), bf16[4,256,128]{2,1,0:T(8,128)(2,1)S(1)}, u32[]{:S(2)}, u32[]{:S(2)}) async-start(bf16[4,256,128]{2,1,0:T(8,128)(2,1)} %copy-done.2), calls=%async_computation.3 | async-start | bytes 524288 | tf_op jit(solution)/shard_map/all_to_all | solution.py:340
  118.5 1.6 %copy-start.1 = (bf16[1024,1024]{1,0:T(8,128)(2,1)S(1)}, bf16[1024,1024]{1,0:T(8,128)(2,1)}, u32[]{:S(2)}) copy-start(bf16[1024,1024]{1,0:T(8,128)(2,1)} %down_hbm.1) | copy-start | bytes 6291460
  120.1 1.0 copy-start.3

commit v4 on v3

--- a/solution.py
+++ b/solution.py
@@ -56,12 +56,17 @@
 def attend_block(q_ref, group, k_s, v_s):
     low = lax.broadcasted_iota(jnp.int32, (1, LANES), 1) < HS
     q = q_ref[group]
-    for head in range(2):
-        keep = jnp.where(low if head == 0 else ~low, 1.0, 0.0).astype(bf16)
-        s = dot_nt(q * keep, k_s[...])
-        top = jnp.max(s, axis=1, keepdims=True)
-        p = jnp.exp2((s - top) * EXPONENT).astype(bf16)
-        yield head, top * EXPONENT, dot(p, v_s[head])
+    tok, span, step = q.shape[0], k_s.shape[0], 640
+    keeps = [jnp.where(low if head == 0 else ~low, 1.0, 0.0).astype(bf16) for head in range(2)]
+    s = dot_nt(jnp.concatenate([q * keep for keep in keeps], axis=0), k_s[...])
+    top = jnp.max(s, axis=1, keepdims=True)
+    sums = [None, None]
+    for begin in range(0, span, step):
+        p = jnp.exp2((s[:, begin : begin + step] - top) * EXPONENT).astype(bf16)
+        for head in range(2):
+            term = dot(p[head * tok : (head + 1) * tok], v_s[head, begin : begin + step, :])
+            sums[head] = term if sums[head] is None else sums[head] + term
+    return [(head, top[head * tok : (head + 1) * tok] * EXPONENT, sums[head]) for head in range(2)]
 
 
 def stage_keys(kv_ref, k_s, v_s):
@@ -245,36 +250,31 @@
     )(received)
 
 
-def mlp_kernel(own_ref, f_ref, near_ref, far_ref, base_ref, gain_ref, up_hbm, down_hbm, bev_ref, mix_ref, bev_s, up_ref, down_ref, sems):
-    copies = [
-        pltpu.make_async_copy(up_hbm, up_ref, sems.at[0]),
-        pltpu.make_async_copy(down_hbm, down_ref, sems.at[1]),
-    ]
-    for copy in copies:
-        copy.start()
+def mlp_kernel(own_ref, f_ref, near_ref, far_ref, base_hbm, gain_ref, up_ref, down_hbm, bev_ref, mix_ref, bev_s, base_s, down_s, sems):
+    base_copy = pltpu.make_async_copy(base_hbm, base_s, sems.at[0])
+    down_copy = pltpu.make_async_copy(down_hbm, down_s, sems.at[1])
+    base_copy.start()
+    down_copy.start()
     share = bev_ref.shape[0]
     own = own_ref[0]
     near = jnp.concatenate([f_ref[own], f_ref[own ^ 1]], axis=1)
     far = jnp.concatenate([f_ref[own ^ 2], f_ref[own ^ 3]], axis=1)
     depth = near.shape[1]
-    bev = (
-        base_ref[...].astype(f32)
-        + dot(near, near_ref[...].reshape(depth, -1))
-        + dot(far, far_ref[...].reshape(depth, -1))
-    )
+    projected = dot(near, near_ref[...].reshape(depth, -1)) + dot(far, far_ref[...].reshape(depth, -1))
+    base_copy.wait()
+    bev = base_s[...].astype(f32) + projected
     bev_s[...] = bev
     mean_square = jnp.mean(bev * bev, axis=1, keepdims=True)
     normed = (bev * lax.rsqrt(mean_square + 1e-06) * gain_ref[...]).astype(bf16)
     bev_ref[...] = bev_s[pl.ds(pl.multiple_of(own * share, share), share), :]
     step = 256
     mixed = None
-    copies[0].wait()
     for begin in range(0, up_ref.shape[1], step):
         u = dot(normed, up_ref[:, begin : begin + step])
         hidden = (0.5 * u * (1.0 + lax.erf(u * math.sqrt(0.5)))).astype(bf16)
         if begin == 0:
-            copies[1].wait()
-        term = dot(hidden, down_ref[begin : begin + step, :])
+            down_copy.wait()
+        term = dot(hidden, down_s[begin : begin + step, :])
         mixed = term if mixed is None else mixed + term
     mix_ref[...] = mixed.astype(bf16)
 
@@ -282,24 +282,33 @@
 def mlp(own, features, near, far, base, gain, up, down):
     heads = features.shape[0]
     cells, width = base.shape
-    vmem, hbm = pl.BlockSpec(memory_space=pltpu.VMEM), pl.BlockSpec(memory_space=pl.ANY)
+    vmem, hbm = pl.BlockSpec(memory_space=pltpu.VMEM), pl.BlockSpec(memory_space=pltpu.HBM)
     return pl.pallas_call(
         mlp_kernel,
         out_shape=(
             jax.ShapeDtypeStruct((cells // heads, width), f32),
             jax.ShapeDtypeStruct((cells, width), bf16),
         ),
-        in_specs=[pl.BlockSpec(memory_space=pltpu.SMEM)] + [vmem] * 5 + [hbm] * 2,
+        in_specs=[pl.BlockSpec(memory_space=pltpu.SMEM)] + [vmem] * 3 + [hbm, vmem, vmem, hbm],
         out_specs=(vmem, vmem),
         scratch_shapes=[
             pltpu.VMEM((cells, width), f32),
-            pltpu.VMEM(up.shape, bf16),
+            pltpu.VMEM((cells, width), bf16),
             pltpu.VMEM(down.shape, bf16),
             pltpu.SemaphoreType.DMA((2,)),
         ],
-        compiler_params=pltpu.CompilerParams(vmem_limit_bytes=24 * MIB),
+        compiler_params=pltpu.CompilerParams(vmem_limit_bytes=20 * MIB),
         name="project_mlp",
-    )(own, features, near, far, base, gain, up, down)
+    )(
+        own,
+        features,
+        near,
+        far,
+        pltpu.with_memory_space_constraint(base, pltpu.HBM),
+        gain,
+        up,
+        pltpu.with_memory_space_constraint(down, pltpu.HBM),
+    )
 
 
 def swap(x, axis, bit):

time: 140 us -> 137 us (0.979)
  local copies, waits for them, and re-layouts: 3.35 us -> 0.72 us
    unnamed x16 -> x12, local copies, waits for them, and re-layouts: 3.35 us -> 0.72 us
where the time goes in v4:
time: 137 us; the launch traced here: 134 us
  blocking collectives  73.6 us (54%)
  starting transfers between devices  27.7 us (20%)
  Pallas kernels  15.4 us (11%)
  waiting for transfers between devices  14.9 us (11%)
  other arithmetic  1.77 us (1%)
    all_gather x1, blocking collectives, body(): own_kv = lax.all_gather(kv, 'z')  38.9 us
    all_to_all x1, blocking collectives, body(): lax.all_to_all(packed.reshape(tiles, PIECE, LANES), ('z', 'y', 'core'), 0...  22.2 us
    all_to_all x1, blocking collectives, body(): lax.all_to_all(mixed.reshape(heads, cells // heads, mixed.shape[1]), 'hea...  12.5 us
    ppermute x3, starting transfers between devices, swap(): lax.ppermute(x, axis, [(i, i ^ bit) for i in range(lax.axis_size(axis))])  9.95 us
    all_to_all x1, waiting for transfers between devices, body(): features = lax.all_to_all(features, 'head', 0, 0)  7.65 us
    all_to_all x1, starting transfers between devices, body(): partial = lax.all_to_all(partial, 'y', 0, 0)  7.33 us
    all_to_all x1, waiting for transfers between devices, body(): partial = lax.all_to_all(partial, 'y', 0, 0)  7.23 us
    all_to_all x1, starting transfers between devices, body(): q_all = lax.all_to_all(q_copies, 'y', 0, 0)  6.97 us
  transfers between devices with their start and end apart: 6, of which 2 were waited for; matrix products, arithmetic and copies ran while one was open for 1% of the time, Pallas kernels for 7%

profile of v4, /device:TPU:56, one launch (start us, length us, event | category | flops | bytes accessed | tf_op | source)
XLA Modules:
  0.0 134.2 jit_solution(17290914417792253051)
XLA Ops:
  0.0 1.5 %prologue.1 = (bf16[4,160,128]{2,1,0:T(8,128)(2,1)}, bf16[320,128]{1,0:T(8,128)(2,1)}) custom-call(bf16[1,160,128]{2,1,0:T(8,128)(2,1)} %q_ref.1, bf16[1,160,128]{2,1,0:T(8,128)(2,1)} %k_ref.1, bf16[1,160,128]{2,1,0:T(8,128)(2,1)} %v_ref.1), custom_call_target="tpu_custom_call" | custom-call | tf_op jit(solution)/shard_map/prologue/pallas_call | solution.py:43
  1.5 7.0 %all-to-all-start = ((bf16[4,160,128]{2,1,0:T(8,128)(2,1)}), bf16[4,160,128]{2,1,0:T(8,128)(2,1)S(1)}, u32[]{:S(2)}, u32[]{:S(2)}) async-start(bf16[4,160,128]{2,1,0:T(8,128)(2,1)} %get-tuple-element.13), calls=%async_computation | async-start | bytes 327680 | tf_op jit(solution)/shard_map/all_to_all | solution.py:337
  8.5 3.4 %collective-permute-start = (bf16[128,1024]{1,0:T(8,128)(2,1)}, bf16[128,1024]{1,0:T(8,128)(2,1)S(1)}, u32[]{:S(2)}, u32[]{:S(2)}) collective-permute-start(bf16[128,1024]{1,0:T(8,128)(2,1)} %param.19), channel_id=1, source_target_pairs={{0,2},{2,0},{4,6},{6,4},{1,3},{3,1},{5,7},{7,5},{8,10},{10,8},{12,... | collective-permute-start | bytes 786440 | tf_op jit(solution)/shard_map/ppermute | solution.py:315
  11.9 38.9 %all-gather = bf16[3840,128]{1,0:T(8,128)(2,1)S(1)} all-gather(bf16[320,128]{1,0:T(8,128)(2,1)} %get-tuple-element.12), channel_id=2, replica_groups=mesh['z'=12,'y'=4,'core'=2,'head'=4,'scene'=2] {'z'}, dimensions={0}, use_global_device_ids=true | all-gather | bytes 1064960 | tf_op jit(solution)/shard_map/all_gather | solution.py:339
  50.8 0.0 collective-permute-done
  50.8 1.0 pad_maximum_fusion.near_ref
  51.8 0.0 all-to-all-done.q_ref
  51.8 1.9 %collective-permute-start.1 = (bf16[12,320,128]{2,1,0:T(8,128)(2,1)S(1)}, bf16[12,320,128]{2,1,0:T(8,128)(2,1)S(1)}, u32[]{:S(2)}, u32[]{:S(2)}) collective-permute-start(bf16[12,320,128]{2,1,0:T(8,128)(2,1)S(1)} %bitcast.12), channel_id=1, source_target_pairs={{0,8},{8,0},{1,9},{9,1},{2,10},{10,2},{3,11},{11,3},{4,12},{12,4},... | collective-permute-start | bytes 2949128 | tf_op jit(solution)/shard_map/ppermute | solution.py:315
  53.7 4.6 %collective-permute-start.2 = (bf16[2,128,1024]{2,1,0:T(8,128)(2,1)S(1)}, bf16[2,128,1024]{2,1,0:T(8,128)(2,1)S(1)}, u32[]{:S(2)}, u32[]{:S(2)}) collective-permute-start(bf16[2,128,1024]{2,1,0:T(8,128)(2,1)S(1)} %pad_maximum_fusion.near_ref), channel_id=1, source_target_pairs={{0,4},{2,6},{4,0},{6,2},{1,5},{3,7},{5,1},{7,3},{8,12},{10,14},{12... | collective-permute-start | bytes 1572872 | tf_op jit(solution)/shard_map/ppermute | solution.py:315
  58.4 3.8 %attend_own_core.1.sum_ref = f32[2,640,128]{2,1,0:T(8,128)S(1)} custom-call(bf16[12,320,128]{2,1,0:T(8,128)(2,1)S(1)} %bitcast.13, bf16[4,160,128]{2,1,0:T(8,128)(2,1)S(1)} %all-to-all-done.q_ref), custom_call_target="tpu_custom_call" | custom-call | flops 1258291200 | bytes 327680 | tf_op jit(solution)/shard_map/attend_own_core/pallas_call | solution.py:138
  62.1 0.0 copy-start.3
  62.1 0.0 copy-start.4
  62.2 0.0 copy-start.5
  62.2 0.0 collective-permute-done.1.kv_ref
  62.2 5.0 %attend_other_core.1 = bf16[4,176,128]{2,1,0:T(8,128)(2,1)} custom-call(bf16[12,320,128]{2,1,0:T(8,128)(2,1)S(1)} %collective-permute-done.1.kv_ref, bf16[4,160,128]{2,1,0:T(8,128)(2,1)S(1)} %all-to-all-done.q_ref, f32[2,640,128]{2,1,0:T(8,128)S(1)} %attend_own_core.1.sum_ref), custom_call_target="tpu_custom_call" | custom-call | flops 1258291200 | bytes 327680 | tf_op jit(solution)/shard_map/attend_other_core/pallas_call | solution.py:155
  67.2 7.3 %all-to-all-start.1 = ((bf16[4,176,128]{2,1,0:T(8,128)(2,1)}), bf16[4,176,128]{2,1,0:T(8,128)(2,1)S(1)}, u32[]{:S(2)}, u32[]{:S(2)}) async-start(bf16[4,176,128]{2,1,0:T(8,128)(2,1)} %attend_other_core.1), calls=%async_computation.1 | async-start | bytes 360448 | tf_op jit(solution)/shard_map/all_to_all | solution.py:345
  74.5 0.0 collective-permute-done.2._.far_ref
  74.5 7.2 %all-to-all-done.1.x_ref = bf16[4,176,128]{2,1,0:T(8,128)(2,1)S(1)} async-done(((bf16[4,176,128]{2,1,0:T(8,128)(2,1)}), bf16[4,176,128]{2,1,0:T(8,128)(2,1)S(1)}, u32[]{:S(2)}, u32[]{:S(2)}) %all-to-all-start.1) | async-done | bytes 180256 | tf_op jit(solution)/shard_map/all_to_all | solution.py:345
  81.8 0.0 copy-done.3
  81.8 0.0 copy-done.4
  81.8 1.0 join_pack.1
  82.8 22.2 %all_to_all.25 = bf16[96,8,128]{2,1,0:T(8,128)(2,1)S(1)} all-to-all(bf16[96,8,128]{2,1,0:T(8,128)(2,1)S(1)} %bitcast.15), channel_id=1, replica_groups=mesh['z'=12,'y'=4,'core'=2,'head'=4,'scene'=2] {'z','y','core'}, dimensions={0} | all-to-all | bytes 393216 | tf_op jit(solution)/shard_map/all_to_all | solution.py:347
  105.0 0.3 splat.1
  105.3 0.0 copy-start.1
  105.3 0.7 copy-done.1
  106.0 3.4 %all-to-all-start.3 = ((bf16[4,256,128]{2,1,0:T(8,128)(2,1)}), bf16[4,256,128]{2,1,0:T(8,128)(2,1)S(1)}, u32[]{:S(2)}, u32[]{:S(2)}) async-start(bf16[4,256,128]{2,1,0:T(8,128)(2,1)} %copy-done.1), calls=%async_computation.3 | async-start | bytes 524288 | tf_op jit(solution)/shard_map/all_to_all | solution.py:349
  109.4 7.6 %all-to-all-done.3.f_ref = bf16[4,256,128]{2,1,0:T(8,128)(2,1)S(1)} async-done(((bf16[4,256,128]{2,1,0:T(8,128)(2,1)}), bf16[4,256,128]{2,1,0:T(8,128)(2,1)S(1)}, u32[]{:S(2)}, u32[]{:S(2)}) %all-to-all-start.3) | async-done | bytes 262176 | tf_op jit(solution)/shard_map/all_to_all | solution.py:349
  117.1 0.0 copy-done.2
  117.1 3.8 %project_mlp.1 = (f32[64,1024]{1,0:T(8,128)S(1)}, bf16[256,1024]{1,0:T(8,128)(2,1)S(1)}) custom-call(s32[1]{0:T(128)} %bitcast.own_ref, bf16[4,256,128]{2,1,0:T(8,128)(2,1)S(1)} %all-to-all-done.3.f_ref, bf16[2,128,1024]{2,1,0:T(8,128)(2,1)S(1)} %pad_maximum_fusion.near_ref, bf16[2,128,1024]{2,1,0:T(8,128)(2,1)S(1)} %collective-permute-done.2._.far_ref, ...), custom_call_target="tpu_custom_call" | custom-call | tf_op jit(solution)/shard_map/project_mlp/pallas_call | solution.py:286
  120.9 12.5 %all_to_all.26 = bf16[4,64,1024]{2,1,0:T(8,128)(2,1)S(1)} all-to-all(bf16[4,64,1024]{2,1,0:T(8,128)(2,1)S(1)} %bitcast.16), channel_id=1, replica_groups=mesh['z'=12,'y'=4,'core'=2,'head'=4,'scene'=2] {'head'}, dimensions={0} | all-to-all | bytes 1048576 | tf_op jit(solution)/shard_map/all_to_all | solution.py:354
  133.4 0.1 convert_reduce_fusion
  133.5 0.7 fusion
  (4 shorter events, 0.0 us)
Async XLA Ops:
  1.5 50.2 %all-to-all-start = ((bf16[4,160,128]{2,1,0:T(8,128)(2,1)}), bf16[4,160,128]{2,1,0:T(8,128)(2,1)S(1)}, u32[]{:S(2)}, u32[]{:S(2)}) async-start(bf16[4,160,128]{2,1,0:T(8,128)(2,1)} %get-tuple-element.13), calls=%async_computation | async-start | bytes 327680 | tf_op jit(solution)/shard_map/all_to_all | solution.py:337
  8.5 42.3 %collective-permute-start = (bf16[128,1024]{1,0:T(8,128)(2,1)}, bf16[128,1024]{1,0:T(8,128)(2,1)S(1)}, u32[]{:S(2)}, u32[]{:S(2)}) collective-permute-start(bf16[128,1024]{1,0:T(8,128)(2,1)} %param.19), channel_id=1, source_target_pairs={{0,2},{2,0},{4,6},{6,4},{1,3},{3,1},{5,7},{7,5},{8,10},{10,8},{12,... | collective-permute-start | bytes 786440 | tf_op jit(solution)/shard_map/ppermute | solution.py:315
  51.8 10.4 %collective-permute-start.1 = (bf16[12,320,128]{2,1,0:T(8,128)(2,1)S(1)}, bf16[12,320,128]{2,1,0:T(8,128)(2,1)S(1)}, u32[]{:S(2)}, u32[]{:S(2)}) collective-permute-start(bf16[12,320,128]{2,1,0:T(8,128)(2,1)S(1)} %bitcast.12), channel_id=1, source_target_pairs={{0,8},{8,0},{1,9},{9,1},{2,10},{10,2},{3,11},{11,3},{4,12},{12,4},... | collective-permute-start | bytes 2949128 | tf_op jit(solution)/shard_map/ppermute | solution.py:315
  53.7 20.8 %collective-permute-start.2 = (bf16[2,128,1024]{2,1,0:T(8,128)(2,1)S(1)}, bf16[2,128,1024]{2,1,0:T(8,128)(2,1)S(1)}, u32[]{:S(2)}, u32[]{:S(2)}) collective-permute-start(bf16[2,128,1024]{2,1,0:T(8,128)(2,1)S(1)} %pad_maximum_fusion.near_ref), channel_id=1, source_target_pairs={{0,4},{2,6},{4,0},{6,2},{1,5},{3,7},{5,1},{7,3},{8,12},{10,14},{12... | collective-permute-start | bytes 1572872 | tf_op jit(solution)/shard_map/ppermute | solution.py:315
  62.1 19.6 %copy-start.3 = (s32[1,160,1]{1,2,0:T(1,128)S(1)}, s32[1,160,1]{1,2,0:T(1,128)}, u32[]{:S(2)}) copy-start(s32[1,160,1]{1,2,0:T(1,128)} %param.15) | copy-start | bytes 1924
  62.1 19.6 %copy-start.4 = (s32[1,160]{1,0:T(1,128)S(1)}, s32[1,160]{1,0:T(1,128)}, u32[]{:S(2)}) copy-start(s32[1,160]{1,0:T(1,128)} %cell_ref.1) | copy-start | bytes 1924
  62.2 19.6 %copy-start.5 = (f32[1,160]{1,0:T(1,128)S(1)}, f32[1,160]{1,0:T(1,128)}, u32[]{:S(2)}) copy-start(f32[1,160]{1,0:T(1,128)} %splat_ref.1) | copy-start | bytes 1924
  67.2 49.9 %copy-start = (bf16[1024,1024]{1,0:T(8,128)(2,1)S(1)}, bf16[1024,1024]{1,0:T(8,128)(2,1)}, u32[]{:S(2)}) copy-start(bf16[1024,1024]{1,0:T(8,128)(2,1)} %up_ref.1) | copy-start | bytes 6291460
  67.2 49.9 %copy-start.2 = (f32[1024]{0:T(1024)S(1)}, f32[1024]{0:T(1024)}, u32[]{:S(2)}) copy-start(f32[1024]{0:T(1024)} %param.18) | copy-start | bytes 12292
  67.2 14.6 %all-to-all-start.1 = ((bf16[4,176,128]{2,1,0:T(8,128)(2,1)}), bf16[4,176,128]{2,1,0:T(8,128)(2,1)S(1)}, u32[]{:S(2)}, u32[]{:S(2)}) async-start(bf16[4,176,128]{2,1,0:T(8,128)(2,1)} %attend_other_core.1), calls=%async_computation.1 | async-start | bytes 360448 | tf_op jit(solution)/shard_map/all_to_all | solution.py:345
  105.3 0.7 copy-start.1
  106.0 11.1 %all-to-all-start.3 = ((bf16[4,256,128]{2,1,0:T(8,128)(2,1)}), bf16[4,256,128]{2,1,0:T(8,128)(2,1)S(1)}, u32[]{:S(2)}, u32[]{:S(2)}) async-start(bf16[4,256,128]{2,1,0:T(8,128)(2,1)} %copy-done.1), calls=%async_computation.3 | async-start | bytes 524288 | tf_op jit(solution)/shard_map/all_to_all | solution.py:349

commit v5 on v4

--- a/solution.py
+++ b/solution.py
@@ -168,7 +168,7 @@
     )(kv, q_all, sums)
 
 
-def join_kernel(tiles, x_ref, _, tile_ref, cell_ref, splat_ref, out_ref, rows_s):
+def join_kernel(tiles, x_ref, tile_ref, cell_ref, splat_ref, out_ref, rows_s):
     groups, tok = x_ref.shape[0], x_ref.shape[1] - EXTRA
     width = 2 * LANES
     rows_s[...] = jnp.zeros_like(rows_s)
@@ -202,20 +202,21 @@
     out_ref[...] = (dot(main, weighted.astype(bf16)) + dot(tail, cells)).astype(bf16)
 
 
-def join(received, early, tile, cell, splat_weight, tiles):
+def join(received, tile, cell, splat_weight, tiles):
     vmem = pl.BlockSpec(memory_space=pltpu.VMEM)
     return pl.pallas_call(
         functools.partial(join_kernel, tiles),
         out_shape=jax.ShapeDtypeStruct((tiles * PIECE, LANES), bf16),
-        in_specs=[vmem, pl.BlockSpec(memory_space=pl.ANY)] + [vmem] * 3,
+        in_specs=[vmem] * 4,
         out_specs=vmem,
         scratch_shapes=[pltpu.VMEM((LANES, 2 * LANES), f32)],
         compiler_params=pltpu.CompilerParams(vmem_limit_bytes=8 * MIB),
         name="join_pack",
-    )(received, early, tile, cell, splat_weight)
-
-
-def splat_kernel(x_ref, out_ref, x_s, y_s, r_s):
+    )(received, tile, cell, splat_weight)
+
+
+def splat_kernel(x_ref, *refs):
+    out_ref, x_s, y_s, r_s = refs[-4:]
     sources = x_ref.shape[0] // PIECE
     cells = out_ref.shape[1]
     x_s[...] = x_ref[...].astype(f32)
@@ -232,13 +233,13 @@
         out_ref[copy] = features
 
 
-def splat(received, cells, copies):
+def splat(received, early, cells, copies):
     rows = received.shape[0]
     vmem = pl.BlockSpec(memory_space=pltpu.VMEM)
     return pl.pallas_call(
         splat_kernel,
         out_shape=jax.ShapeDtypeStruct((copies, cells, LANES), bf16),
-        in_specs=[vmem],
+        in_specs=[vmem] + [pl.BlockSpec(memory_space=pl.ANY)] * len(early),
         out_specs=vmem,
         scratch_shapes=[
             pltpu.VMEM((rows, LANES), f32),
@@ -247,20 +248,23 @@
         ],
         compiler_params=pltpu.CompilerParams(vmem_limit_bytes=8 * MIB),
         name="splat",
-    )(received)
-
-
-def mlp_kernel(own_ref, f_ref, near_ref, far_ref, base_hbm, gain_ref, up_ref, down_hbm, bev_ref, mix_ref, bev_s, base_s, down_s, sems):
+    )(received, *early)
+
+
+def mlp_kernel(own_ref, *refs):
+    weights, (f_ref, base_hbm, gain_ref, up_ref, down_hbm) = refs[:4], refs[4:9]
+    bev_ref, mix_ref, bev_s, base_s, down_s, sems = refs[9:]
     base_copy = pltpu.make_async_copy(base_hbm, base_s, sems.at[0])
     down_copy = pltpu.make_async_copy(down_hbm, down_s, sems.at[1])
     base_copy.start()
     down_copy.start()
     share = bev_ref.shape[0]
     own = own_ref[0]
-    near = jnp.concatenate([f_ref[own], f_ref[own ^ 1]], axis=1)
-    far = jnp.concatenate([f_ref[own ^ 2], f_ref[own ^ 3]], axis=1)
-    depth = near.shape[1]
-    projected = dot(near, near_ref[...].reshape(depth, -1)) + dot(far, far_ref[...].reshape(depth, -1))
+    projected = None
+    for k in range(0, len(weights), 2):
+        features = jnp.concatenate([f_ref[own ^ k], f_ref[own ^ (k + 1)]], axis=1)
+        term = dot(features, jnp.concatenate([weights[k][...], weights[k + 1][...]], axis=0))
+        projected = term if projected is None else projected + term
     base_copy.wait()
     bev = base_s[...].astype(f32) + projected
     bev_s[...] = bev
@@ -279,7 +283,7 @@
     mix_ref[...] = mixed.astype(bf16)
 
 
-def mlp(own, features, near, far, base, gain, up, down):
+def mlp(own, weights, features, base, gain, up, down):
     heads = features.shape[0]
     cells, width = base.shape
     vmem, hbm = pl.BlockSpec(memory_space=pltpu.VMEM), pl.BlockSpec(memory_space=pltpu.HBM)
@@ -289,7 +293,7 @@
             jax.ShapeDtypeStruct((cells // heads, width), f32),
             jax.ShapeDtypeStruct((cells, width), bf16),
         ),
-        in_specs=[pl.BlockSpec(memory_space=pltpu.SMEM)] + [vmem] * 3 + [hbm, vmem, vmem, hbm],
+        in_specs=[pl.BlockSpec(memory_space=pltpu.SMEM)] + [vmem] * 5 + [hbm, vmem, vmem, hbm],
         out_specs=(vmem, vmem),
         scratch_shapes=[
             pltpu.VMEM((cells, width), f32),
@@ -301,9 +305,8 @@
         name="project_mlp",
     )(
         own,
+        *weights,
         features,
-        near,
-        far,
         pltpu.with_memory_space_constraint(base, pltpu.HBM),
         gain,
         up,
@@ -335,21 +338,21 @@
     cells = bev_base.shape[1]
     q_copies, kv = prologue(queries, key_states, value_states, groups)
     q_all = lax.all_to_all(q_copies, "y", 0, 0)
-    near_weight = jnp.stack([out_weight, swap(out_weight, "head", 1)])
     own_kv = lax.all_gather(kv, "z")
-    own_kv, q_all, near_weight = lax.optimization_barrier((own_kv, q_all, near_weight))
+    own_kv, q_all = lax.optimization_barrier((own_kv, q_all))
     other_kv = swap(own_kv, "core", 1)
-    far_weight = swap(near_weight, "head", 2)
     sums = attend_first(own_kv, q_all)
     partial = attend_second(other_kv, q_all, sums)
     partial = lax.all_to_all(partial, "y", 0, 0)
-    packed = join(partial, far_weight, tile_of.reshape(1, tok), cell_of, splat_weight, tiles)
+    packed = join(partial, tile_of.reshape(1, tok), cell_of, splat_weight, tiles)
+    packed, out_weight = lax.optimization_barrier((packed, out_weight))
+    weights = tuple(swap(out_weight, "head", k) for k in range(heads - 1, 0, -1))[::-1]
     received = lax.all_to_all(packed.reshape(tiles, PIECE, LANES), ("z", "y", "core"), 0, 0)
-    features = splat(received.reshape(tiles * PIECE, LANES), cells, heads)
+    features = splat(received.reshape(tiles * PIECE, LANES), weights, cells, heads)
     features = lax.all_to_all(features, "head", 0, 0)
     own = lax.axis_index("head").astype(jnp.int32).reshape(1)
     bev_rows, mixed = mlp(
-        own, features, near_weight, far_weight, bev_base[0], norm_gain[None, :], up_weight, down_weight
+        own, (out_weight,) + weights, features, bev_base[0], norm_gain[None, :], up_weight, down_weight
     )
     mixed = lax.all_to_all(mixed.reshape(heads, cells // heads, mixed.shape[1]), "head", 0, 0)
     return (bev_rows + jnp.sum(mixed.astype(f32), axis=0)).astype(bf16)[None]

time: 137 us -> 134 us (0.978); the launches traced: 134 us -> 133 us
  blocking collectives: 73.6 us -> 64.5 us
  waiting for transfers between devices: 14.9 us -> 20.3 us
  starting transfers between devices: 27.7 us -> 30.9 us
    ppermute x3 -> x4, waiting for transfers between devices: 0.01 us -> 13.2 us  [swap(): lax.ppermute(x, axis, [(i, i ^ bit) for i in range(lax.axis_size(axis))])]
    all_to_all x1, blocking collectives: 22.2 us -> 14.6 us  [body(): partial = lax.all_to_all(partial, 'y', 0, 0)]
    all_to_all x1, waiting for transfers between devices: 7.23 us -> 0.01 us  [body(): lax.all_to_all(packed.reshape(tiles, PIECE, LANES), ('z', 'y', 'core'), 0...]
    ppermute x3 -> x4, starting transfers between devices: 9.95 us -> 12.3 us  [swap(): lax.ppermute(x, axis, [(i, i ^ bit) for i in range(lax.axis_size(axis))])]
  transfers between devices with their start and end apart: 6 -> 7, of which waited for: 2 -> 4; matrix products, arithmetic and copies ran while one was open for 1% -> 0% of each run, Pallas kernels for 7% -> 3%
where the time goes in v5:
time: 134 us; the launch traced here: 133 us
  blocking collectives  64.5 us (48%)
  starting transfers between devices  30.9 us (23%)
  waiting for transfers between devices  20.3 us (15%)
  Pallas kernels  16.2 us (12%)
    all_gather x1, blocking collectives, body(): own_kv = lax.all_gather(kv, 'z')  38.7 us
    all_to_all x1, blocking collectives, body(): partial = lax.all_to_all(partial, 'y', 0, 0)  14.6 us
    ppermute x4, waiting for transfers between devices, swap(): lax.ppermute(x, axis, [(i, i ^ bit) for i in range(lax.axis_size(axis))])  13.2 us
    ppermute x4, starting transfers between devices, swap(): lax.ppermute(x, axis, [(i, i ^ bit) for i in range(lax.axis_size(axis))])  12.3 us
    all_to_all x1, blocking collectives, body(): lax.all_to_all(mixed.reshape(heads, cells // heads, mixed.shape[1]), 'hea...  11.2 us
    all_to_all x1, starting transfers between devices, body(): lax.all_to_all(packed.reshape(tiles, PIECE, LANES), ('z', 'y', 'core'), 0...  8.16 us
    all_to_all x1, waiting for transfers between devices, body(): features = lax.all_to_all(features, 'head', 0, 0)  7.09 us
    all_to_all x1, starting transfers between devices, body(): q_all = lax.all_to_all(q_copies, 'y', 0, 0)  6.97 us
  transfers between devices with their start and end apart: 7, of which 4 were waited for; matrix products, arithmetic and copies ran while one was open for 0% of the time, Pallas kernels for 3%

profile of v5, /device:TPU:56, one launch (start us, length us, event | category | flops | bytes accessed | tf_op | source)
XLA Modules:
  0.0 132.8 jit_solution(7576704546979358672)
XLA Ops:
  0.0 1.5 %prologue.1 = (bf16[4,160,128]{2,1,0:T(8,128)(2,1)}, bf16[320,128]{1,0:T(8,128)(2,1)}) custom-call(bf16[1,160,128]{2,1,0:T(8,128)(2,1)} %q_ref.1, bf16[1,160,128]{2,1,0:T(8,128)(2,1)} %k_ref.1, bf16[1,160,128]{2,1,0:T(8,128)(2,1)} %v_ref.1), custom_call_target="tpu_custom_call" | custom-call | tf_op jit(solution)/shard_map/prologue/pallas_call | solution.py:43
  1.5 7.0 %all-to-all-start = ((bf16[4,160,128]{2,1,0:T(8,128)(2,1)}), bf16[4,160,128]{2,1,0:T(8,128)(2,1)S(1)}, u32[]{:S(2)}, u32[]{:S(2)}) async-start(bf16[4,160,128]{2,1,0:T(8,128)(2,1)} %get-tuple-element.14), calls=%async_computation | async-start | bytes 327680 | tf_op jit(solution)/shard_map/all_to_all | solution.py:340
  8.5 38.7 %all-gather = bf16[3840,128]{1,0:T(8,128)(2,1)S(1)} all-gather(bf16[320,128]{1,0:T(8,128)(2,1)} %get-tuple-element.13), channel_id=2, replica_groups=mesh['z'=12,'y'=4,'core'=2,'head'=4,'scene'=2] {'z'}, dimensions={0}, use_global_device_ids=true | all-gather | bytes 1064960 | tf_op jit(solution)/shard_map/all_gather | solution.py:341
  47.2 0.0 all-to-all-done.q_ref
  47.2 1.9 %collective-permute-start = (bf16[12,320,128]{2,1,0:T(8,128)(2,1)S(1)}, bf16[12,320,128]{2,1,0:T(8,128)(2,1)S(1)}, u32[]{:S(2)}, u32[]{:S(2)}) collective-permute-start(bf16[12,320,128]{2,1,0:T(8,128)(2,1)S(1)} %bitcast.10), channel_id=1, source_target_pairs={{0,8},{8,0},{1,9},{9,1},{2,10},{10,2},{3,11},{11,3},{4,12},{12,4},... | collective-permute-start | bytes 2949128 | tf_op jit(solution)/shard_map/ppermute | solution.py:318
  49.1 3.8 %attend_own_core.1.sum_ref = f32[2,640,128]{2,1,0:T(8,128)S(1)} custom-call(bf16[12,320,128]{2,1,0:T(8,128)(2,1)S(1)} %bitcast.11, bf16[4,160,128]{2,1,0:T(8,128)(2,1)S(1)} %all-to-all-done.q_ref), custom_call_target="tpu_custom_call" | custom-call | flops 1258291200 | bytes 327680 | tf_op jit(solution)/shard_map/attend_own_core/pallas_call | solution.py:138
  52.8 0.0 copy-start.3
  52.9 0.0 copy-start.4
  52.9 0.0 copy-start.5
  52.9 0.0 copy-start.1
  52.9 0.0 collective-permute-done.kv_ref
  52.9 4.4 %attend_other_core.1 = bf16[4,176,128]{2,1,0:T(8,128)(2,1)S(1)} custom-call(bf16[12,320,128]{2,1,0:T(8,128)(2,1)S(1)} %collective-permute-done.kv_ref, bf16[4,160,128]{2,1,0:T(8,128)(2,1)S(1)} %all-to-all-done.q_ref, f32[2,640,128]{2,1,0:T(8,128)S(1)} %attend_own_core.1.sum_ref), custom_call_target="tpu_custom_call" | custom-call | flops 1258291200 | bytes 327680 | tf_op jit(solution)/shard_map/attend_other_core/pallas_call | solution.py:155
  57.3 14.6 %all_to_all.25.x_ref = bf16[4,176,128]{2,1,0:T(8,128)(2,1)S(1)} all-to-all(bf16[4,176,128]{2,1,0:T(8,128)(2,1)S(1)} %attend_other_core.1), channel_id=1, replica_groups=mesh['z'=12,'y'=4,'core'=2,'head'=4,'scene'=2] {'y'}, dimensions={0} | all-to-all | bytes 360448 | tf_op jit(solution)/shard_map/all_to_all | solution.py:346
  71.9 0.0 copy-done.3
  71.9 0.0 copy-done.4
  71.9 0.0 copy-done.5
  71.9 1.7 %join_pack.1 = bf16[768,128]{1,0:T(8,128)(2,1)} custom-call(bf16[4,176,128]{2,1,0:T(8,128)(2,1)S(1)} %all_to_all.25.x_ref, s32[1,160]{1,0:T(1,128)S(1)} %bitcast.15, s32[1,160]{1,0:T(1,128)S(1)} %copy-done.4, f32[1,160]{1,0:T(1,128)S(1)} %copy-done.5), custom_call_target="tpu_custom_call" | custom-call | tf_op jit(solution)/shard_map/join_pack/pallas_call | solution.py:207
  73.7 8.2 %all-to-all-start.2 = ((bf16[96,8,128]{2,1,0:T(8,128)(2,1)}), bf16[96,8,128]{2,1,0:T(8,128)(2,1)S(1)}, u32[]{:S(2)}, u32[]{:S(2)}) async-start(bf16[96,8,128]{2,1,0:T(8,128)(2,1)} %bitcast.3), calls=%async_computation.2 | async-start | bytes 393216 | tf_op jit(solution)/shard_map/all_to_all | solution.py:350
  81.8 3.4 %collective-permute-start.1 = (bf16[128,1024]{1,0:T(8,128)(2,1)S(1)}, bf16[128,1024]{1,0:T(8,128)(2,1)S(1)}, u32[]{:S(2)}, u32[]{:S(2)}) collective-permute-start(bf16[128,1024]{1,0:T(8,128)(2,1)S(1)} %copy-done.1), channel_id=1, source_target_pairs={{0,2},{2,0},{4,6},{6,4},{1,3},{3,1},{5,7},{7,5},{8,10},{10,8},{12,... | collective-permute-start | bytes 786440 | tf_op jit(solution)/shard_map/ppermute | solution.py:318
  85.2 4.6 %collective-permute-start.2 = (bf16[128,1024]{1,0:T(8,128)(2,1)S(1)}, bf16[128,1024]{1,0:T(8,128)(2,1)S(1)}, u32[]{:S(2)}, u32[]{:S(2)}) collective-permute-start(bf16[128,1024]{1,0:T(8,128)(2,1)S(1)} %copy-done.1), channel_id=1, source_target_pairs={{0,4},{2,6},{4,0},{6,2},{1,5},{3,7},{5,1},{7,3},{8,12},{10,14},{12... | collective-permute-start | bytes 786440 | tf_op jit(solution)/shard_map/ppermute | solution.py:318
  89.9 2.4 %collective-permute-start.3 = (bf16[128,1024]{1,0:T(8,128)(2,1)S(1)}, bf16[128,1024]{1,0:T(8,128)(2,1)S(1)}, u32[]{:S(2)}, u32[]{:S(2)}) collective-permute-start(bf16[128,1024]{1,0:T(8,128)(2,1)S(1)} %copy-done.1), channel_id=1, source_target_pairs={{0,6},{2,4},{4,2},{6,0},{1,7},{3,5},{5,3},{7,1},{8,14},{10,12},{12... | collective-permute-start | bytes 786440 | tf_op jit(solution)/shard_map/ppermute | solution.py:318
  92.3 0.6 collective-permute-done.1.refs_0_.refs_1_
  92.9 7.1 %collective-permute-done.2.refs_1_.refs_2_ = bf16[128,1024]{1,0:T(8,128)(2,1)S(1)} collective-permute-done((bf16[128,1024]{1,0:T(8,128)(2,1)S(1)}, bf16[128,1024]{1,0:T(8,128)(2,1)S(1)}, u32[]{:S(2)}, u32[]{:S(2)}) %collective-permute-start.2) | collective-permute-done | bytes 262176 | tf_op jit(solution)/shard_map/ppermute | solution.py:318
  100.0 5.5 %collective-permute-done.3.refs_2_.refs_3_ = bf16[128,1024]{1,0:T(8,128)(2,1)S(1)} collective-permute-done((bf16[128,1024]{1,0:T(8,128)(2,1)S(1)}, bf16[128,1024]{1,0:T(8,128)(2,1)S(1)}, u32[]{:S(2)}, u32[]{:S(2)}) %collective-permute-start.3) | collective-permute-done | bytes 262176 | tf_op jit(solution)/shard_map/ppermute | solution.py:318
  105.5 0.0 all-to-all-done.2
  105.5 1.0 splat.1
  106.5 3.4 %all-to-all-start.3 = ((bf16[4,256,128]{2,1,0:T(8,128)(2,1)}), bf16[4,256,128]{2,1,0:T(8,128)(2,1)S(1)}, u32[]{:S(2)}, u32[]{:S(2)}) async-start(bf16[4,256,128]{2,1,0:T(8,128)(2,1)} %splat.1), calls=%async_computation.3 | async-start | bytes 524288 | tf_op jit(solution)/shard_map/all_to_all | solution.py:352
  110.0 7.1 %all-to-all-done.3.refs_4_ = bf16[4,256,128]{2,1,0:T(8,128)(2,1)S(1)} async-done(((bf16[4,256,128]{2,1,0:T(8,128)(2,1)}), bf16[4,256,128]{2,1,0:T(8,128)(2,1)S(1)}, u32[]{:S(2)}, u32[]{:S(2)}) %all-to-all-start.3) | async-done | bytes 262176 | tf_op jit(solution)/shard_map/all_to_all | solution.py:352
  117.0 3.8 %project_mlp.1 = (f32[64,1024]{1,0:T(8,128)S(1)}, bf16[256,1024]{1,0:T(8,128)(2,1)S(1)}) custom-call(s32[1]{0:T(128)} %bitcast.own_ref, bf16[128,1024]{1,0:T(8,128)(2,1)S(1)} %copy-done.1, bf16[128,1024]{1,0:T(8,128)(2,1)S(1)} %collective-permute-done.1.refs_0_.refs_1_, bf16[128,1024]{1,0:T(8,128)(2,1)S(1)} %collective-permute-done.2.refs_1_.refs_2_, ...), custom_call_target="tpu_custom_call" | custom-call | tf_op jit(solution)/shard_map/project_mlp/pallas_call | solution.py:290
  120.8 11.2 %all_to_all.26 = bf16[4,64,1024]{2,1,0:T(8,128)(2,1)S(1)} all-to-all(bf16[4,64,1024]{2,1,0:T(8,128)(2,1)S(1)} %bitcast.13), channel_id=1, replica_groups=mesh['z'=12,'y'=4,'core'=2,'head'=4,'scene'=2] {'head'}, dimensions={0} | all-to-all | bytes 1048576 | tf_op jit(solution)/shard_map/all_to_all | solution.py:357
  132.0 0.1 convert_reduce_fusion
  132.1 0.7 fusion
  (5 shorter events, 0.0 us)
Async XLA Ops:
  1.5 45.6 %all-to-all-start = ((bf16[4,160,128]{2,1,0:T(8,128)(2,1)}), bf16[4,160,128]{2,1,0:T(8,128)(2,1)S(1)}, u32[]{:S(2)}, u32[]{:S(2)}) async-start(bf16[4,160,128]{2,1,0:T(8,128)(2,1)} %get-tuple-element.14), calls=%async_computation | async-start | bytes 327680 | tf_op jit(solution)/shard_map/all_to_all | solution.py:340
  47.2 5.7 %collective-permute-start = (bf16[12,320,128]{2,1,0:T(8,128)(2,1)S(1)}, bf16[12,320,128]{2,1,0:T(8,128)(2,1)S(1)}, u32[]{:S(2)}, u32[]{:S(2)}) collective-permute-start(bf16[12,320,128]{2,1,0:T(8,128)(2,1)S(1)} %bitcast.10), channel_id=1, source_target_pairs={{0,8},{8,0},{1,9},{9,1},{2,10},{10,2},{3,11},{11,3},{4,12},{12,4},... | collective-permute-start | bytes 2949128 | tf_op jit(solution)/shard_map/ppermute | solution.py:318
  52.8 19.1 %copy-start.3 = (s32[1,160,1]{1,2,0:T(1,128)S(1)}, s32[1,160,1]{1,2,0:T(1,128)}, u32[]{:S(2)}) copy-start(s32[1,160,1]{1,2,0:T(1,128)} %param.15) | copy-start | bytes 1924
  52.9 19.1 %copy-start.4 = (s32[1,160]{1,0:T(1,128)S(1)}, s32[1,160]{1,0:T(1,128)}, u32[]{:S(2)}) copy-start(s32[1,160]{1,0:T(1,128)} %cell_ref.1) | copy-start | bytes 1924
  52.9 19.1 %copy-start.5 = (f32[1,160]{1,0:T(1,128)S(1)}, f32[1,160]{1,0:T(1,128)}, u32[]{:S(2)}) copy-start(f32[1,160]{1,0:T(1,128)} %splat_ref.1) | copy-start | bytes 1924
  52.9 28.9 %copy-start.1 = (bf16[128,1024]{1,0:T(8,128)(2,1)S(1)}, bf16[128,1024]{1,0:T(8,128)(2,1)}, u32[]{:S(2)}) copy-start(bf16[128,1024]{1,0:T(8,128)(2,1)} %refs_0_) | copy-start | bytes 786436
  57.3 59.8 %copy-start = (bf16[1024,1024]{1,0:T(8,128)(2,1)S(1)}, bf16[1024,1024]{1,0:T(8,128)(2,1)}, u32[]{:S(2)}) copy-start(bf16[1024,1024]{1,0:T(8,128)(2,1)} %refs_7_.1) | copy-start | bytes 6291460
  57.3 59.8 %copy-start.2 = (f32[1024]{0:T(1024)S(1)}, f32[1024]{0:T(1024)}, u32[]{:S(2)}) copy-start(f32[1024]{0:T(1024)} %param.18) | copy-start | bytes 12292
  73.7 31.9 %all-to-all-start.2 = ((bf16[96,8,128]{2,1,0:T(8,128)(2,1)}), bf16[96,8,128]{2,1,0:T(8,128)(2,1)S(1)}, u32[]{:S(2)}, u32[]{:S(2)}) async-start(bf16[96,8,128]{2,1,0:T(8,128)(2,1)} %bitcast.3), calls=%async_computation.2 | async-start | bytes 393216 | tf_op jit(solution)/shard_map/all_to_all | solution.py:350
  81.8 11.0 %collective-permute-start.1 = (bf16[128,1024]{1,0:T(8,128)(2,1)S(1)}, bf16[128,1024]{1,0:T(8,128)(2,1)S(1)}, u32[]{:S(2)}, u32[]{:S(2)}) collective-permute-start(bf16[128,1024]{1,0:T(8,128)(2,1)S(1)} %copy-done.1), channel_id=1, source_target_pairs={{0,2},{2,0},{4,6},{6,4},{1,3},{3,1},{5,7},{7,5},{8,10},{10,8},{12,... | collective-permute-start | bytes 786440 | tf_op jit(solution)/shard_map/ppermute | solution.py:318
  85.2 14.8 %collective-permute-start.2 = (bf16[128,1024]{1,0:T(8,128)(2,1)S(1)}, bf16[128,1024]{1,0:T(8,128)(2,1)S(1)}, u32[]{:S(2)}, u32[]{:S(2)}) collective-permute-start(bf16[128,1024]{1,0:T(8,128)(2,1)S(1)} %copy-done.1), channel_id=1, source_target_pairs={{0,4},{2,6},{4,0},{6,2},{1,5},{3,7},{5,1},{7,3},{8,12},{10,14},{12... | collective-permute-start | bytes 786440 | tf_op jit(solution)/shard_map/ppermute | solution.py:318
  89.9 15.6 %collective-permute-start.3 = (bf16[128,1024]{1,0:T(8,128)(2,1)S(1)}, bf16[128,1024]{1,0:T(8,128)(2,1)S(1)}, u32[]{:S(2)}, u32[]{:S(2)}) collective-permute-start(bf16[128,1024]{1,0:T(8,128)(2,1)S(1)} %copy-done.1), channel_id=1, source_target_pairs={{0,6},{2,4},{4,2},{6,0},{1,7},{3,5},{5,3},{7,1},{8,14},{10,12},{12... | collective-permute-start | bytes 786440 | tf_op jit(solution)/shard_map/ppermute | solution.py:318
  106.5 10.5 %all-to-all-start.3 = ((bf16[4,256,128]{2,1,0:T(8,128)(2,1)}), bf16[4,256,128]{2,1,0:T(8,128)(2,1)S(1)}, u32[]{:S(2)}, u32[]{:S(2)}) async-start(bf16[4,256,128]{2,1,0:T(8,128)(2,1)} %splat.1), calls=%async_computation.3 | async-start | bytes 524288 | tf_op jit(solution)/shard_map/all_to_all | solution.py:352

commit v6 on v2

--- a/solution.py
+++ b/solution.py
@@ -71,12 +71,17 @@
 def attend_block(q_ref, group, k_s, v_s):
     low = lax.broadcasted_iota(jnp.int32, (1, LANES), 1) < HS
     q = q_ref[group, :, :LANES]
-    for head in range(2):
-        keep = jnp.where(low if head == 0 else ~low, 1.0, 0.0).astype(bf16)
-        s = dot_nt(q * keep, k_s[...])
-        top = jnp.max(s, axis=1, keepdims=True)
-        p = jnp.exp2((s - top) * EXPONENT).astype(bf16)
-        yield head, top * EXPONENT, dot(p, v_s[head])
+    tok, span, step = q.shape[0], k_s.shape[0], 640
+    keeps = [jnp.where(low if head == 0 else ~low, 1.0, 0.0).astype(bf16) for head in range(2)]
+    s = dot_nt(jnp.concatenate([q * keep for keep in keeps], axis=0), k_s[...])
+    top = jnp.max(s, axis=1, keepdims=True)
+    sums = [None, None]
+    for begin in range(0, span, step):
+        p = jnp.exp2((s[:, begin : begin + step] - top) * EXPONENT).astype(bf16)
+        for head in range(2):
+            term = dot(p[head * tok : (head + 1) * tok], v_s[head, begin : begin + step, :])
+            sums[head] = term if sums[head] is None else sums[head] + term
+    return [(head, top[head * tok : (head + 1) * tok] * EXPONENT, sums[head]) for head in range(2)]
 
 
 def stage_keys(kv_ref, k_s, v_s):
@@ -90,36 +95,40 @@
     v_s[1] = values * high_b + low_b
 
 
-def first_kernel(kv_ref, q_ref, top_ref, sum_ref, k_s, v_s):
+def other_half(head):
+    return (LANES - 1, LANES - 2) if head == 0 else (0, 1)
+
+
+def first_kernel(kv_ref, q_ref, sum_ref, k_s, v_s):
     groups, tok = q_ref.shape[0], q_ref.shape[1]
     stage_keys(kv_ref, k_s, v_s)
+    lane = lax.broadcasted_iota(jnp.int32, (1, LANES), 1)
+    for group in range(groups):
+        for head, top, sums in attend_block(q_ref, group, k_s, v_s):
+            sum_ref[head, pl.ds(group * tok, tok), :] = jnp.where(lane == other_half(head)[1], top, sums)
+
+
+def second_kernel(kv_ref, q_ref, sum_ref, out_ref, k_s, v_s, o_s, extra_s, slot_s, slot_t):
+    groups, tok = q_ref.shape[0], q_ref.shape[1]
+    tiles = out_ref.shape[0]
+    slots, width = groups * SLOTS, groups * tok
+    stage_keys(kv_ref, k_s, v_s)
+    lane = lax.broadcasted_iota(jnp.int32, (tok, LANES), 1)
+    lane_f = lane.astype(f32)
     for group in range(groups):
         rows = pl.ds(group * tok, tok)
-        for head, top, sums in attend_block(q_ref, group, k_s, v_s):
-            top_ref[head, rows, :] = jnp.broadcast_to(top, (tok, LANES))
-            sum_ref[head, rows, :] = sums
-
-
-def second_kernel(tiles, kv_ref, q_ref, top_ref, sum_ref, _, out_ref, k_s, v_s, ox_s, slot_s, slot_t):
-    groups, tok = q_ref.shape[0], q_ref.shape[1]
-    stage_keys(kv_ref, k_s, v_s)
-    low = lax.broadcasted_iota(jnp.int32, (1, LANES), 1) < HS
-    lane = lax.broadcasted_iota(jnp.int32, (tok, LANES), 1)
-    lane_f = lane.astype(f32)
-    width = groups * tok
-    for group in range(groups):
         meta = q_ref[group, :, LANES:].astype(f32)
         tile, cell = meta[:, 0:1], meta[:, 2:3]
         place = meta[:, 1:2] + float(group * SLOTS)
         gain = meta[:, 3:4] + meta[:, 4:5]
-        rows = pl.ds(group * tok, tok)
         sums = []
         extra = jnp.where(lane_f == 96.0 + place, cell, 0.0)
         for head, top_b, sum_b in attend_block(q_ref, group, k_s, v_s):
-            top_a = top_ref[head, rows, :][:, 0:1]
+            at, top_at = other_half(head)
+            sum_a = sum_ref[head, rows, :]
+            top_a = sum_a[:, top_at : top_at + 1]
             top = jnp.maximum(top_a, top_b)
-            o = sum_ref[head, rows, :] * jnp.exp2(top_a - top) + sum_b * jnp.exp2(top_b - top)
-            at = LANES - 1 if head == 0 else 0
+            o = sum_a * jnp.exp2(top_a - top) + sum_b * jnp.exp2(top_b - top)
             total = o[:, at : at + 1]
             sums.append(o * (gain / total))
             left = top + jnp.log2(total)
@@ -127,19 +136,21 @@
                 piece = left.astype(bf16).astype(f32)
                 left = left - piece
                 extra = jnp.where(lane_f == step * 32.0 + head * 16.0 + place, piece, extra)
-        ox_s[rows, :] = jnp.where(low, sums[0], sums[1]).astype(bf16)
-        ox_s[pl.ds(width + group * tok, tok), :] = extra.astype(bf16)
-        slot_s[rows, :] = jnp.where(
-            lane == 0, tile * PIECE + place, jnp.where(lane == 1, tile * PIECE + float(SLOTS * groups), -1.0)
-        )
+        o_s[rows, :] = jnp.where(lane < HS, sums[0], sums[1]).astype(bf16)
+        extra_s[rows, :] = extra.astype(bf16)
+        slot_s[rows, :] = jnp.where(lane == 0, tile * slots + place, tile * 8.0)
     slot_t[...] = jnp.transpose(slot_s[...])
-    chunk = 16 * PIECE
-    for begin in range(0, tiles * PIECE, chunk):
-        row = (lax.broadcasted_iota(jnp.int32, (chunk, width), 0) + begin).astype(f32)
-        main = jnp.where(row == slot_t[0:1, :], 1.0, 0.0).astype(bf16)
-        tail = jnp.where(row == slot_t[1:2, :], 1.0, 0.0).astype(bf16)
-        packed = dot(main, ox_s[:width, :]) + dot(tail, ox_s[width:, :])
-        out_ref[pl.ds(begin, chunk), :] = packed.astype(bf16)
+
+    def one_hot(begin, count, at):
+        row = (lax.broadcasted_iota(jnp.int32, (count, width), 0) + begin).astype(f32)
+        return jnp.where(row == slot_t[at : at + 1, :], 1.0, 0.0).astype(bf16)
+
+    step = 24
+    for begin in range(0, tiles, step):
+        main = dot(one_hot(begin * slots, step * slots, 0), o_s[...]).astype(bf16)
+        tail = dot(one_hot(begin * 8, step * 8, 1), extra_s[...]).astype(bf16)
+        out_ref[pl.ds(begin, step), :slots, :] = main.reshape(step, slots, LANES)
+        out_ref[pl.ds(begin, step), slots:, :] = tail.reshape(step, 8, LANES)
 
 
 def attention_cost(queries, keys):
@@ -153,43 +164,45 @@
     groups, tok, _ = q_all.shape
     span, rows = blocks * tok2 // 2, groups * tok
     vmem = pl.BlockSpec(memory_space=pltpu.VMEM)
-    state = jax.ShapeDtypeStruct((2, rows, LANES), f32)
     return pl.pallas_call(
         first_kernel,
-        out_shape=(state, state),
+        out_shape=jax.ShapeDtypeStruct((2, rows, LANES), f32),
         in_specs=[vmem, vmem],
-        out_specs=(vmem, vmem),
+        out_specs=vmem,
         scratch_shapes=[pltpu.VMEM((span, LANES), bf16), pltpu.VMEM((2, span, LANES), bf16)],
-        compiler_params=pltpu.CompilerParams(vmem_limit_bytes=20 * MIB),
+        compiler_params=pltpu.CompilerParams(vmem_limit_bytes=16 * MIB),
         cost_estimate=attention_cost(rows, span),
         name="attend_own_core",
     )(kv, q_all)
 
 
-def attend_second(kv, q_all, top, sums, early, tiles):
+def attend_second(kv, q_all, sums, tiles):
     blocks, tok2, _ = kv.shape
     groups, tok, _ = q_all.shape
     span, rows = blocks * tok2 // 2, groups * tok
     vmem = pl.BlockSpec(memory_space=pltpu.VMEM)
     return pl.pallas_call(
-        functools.partial(second_kernel, tiles),
-        out_shape=jax.ShapeDtypeStruct((tiles * PIECE, LANES), bf16),
-        in_specs=[vmem] * 4 + [pl.BlockSpec(memory_space=pl.ANY)],
+        second_kernel,
+        out_shape=jax.ShapeDtypeStruct((tiles, PIECE, LANES), bf16),
+        in_specs=[vmem] * 3,
         out_specs=vmem,
         scratch_shapes=[
             pltpu.VMEM((span, LANES), bf16),
             pltpu.VMEM((2, span, LANES), bf16),
-            pltpu.VMEM((2 * rows, LANES), bf16),
+            pltpu.VMEM((rows, LANES), bf16),
+            pltpu.VMEM((rows, LANES), bf16),
             pltpu.VMEM((rows, LANES), f32),
             pltpu.VMEM((LANES, rows), f32),
         ],
-        compiler_params=pltpu.CompilerParams(vmem_limit_bytes=24 * MIB),
+        compiler_params=pltpu.CompilerParams(vmem_limit_bytes=16 * MIB),
         cost_estimate=attention_cost(rows, span),
         name="attend_other_core",
-    )(kv, q_all, top, sums, early)
-
-
-def splat_kernel(cells, groups, x_ref, out_ref, x_s, y_s, r_s):
+    )(kv, q_all, sums)
+
+
+def splat_kernel(groups, x_ref, *refs):
+    out_ref, x_s, y_s, r_s = refs[-4:]
+    cells = out_ref.shape[1]
     sources = x_ref.shape[0] // PIECE
     slots = groups * SLOTS
     x_s[...] = x_ref[...].astype(f32)
@@ -226,12 +239,12 @@
         out_ref[copy] = features
 
 
-def splat(received, cells, groups, copies):
+def splat(received, early, cells, groups, copies):
     rows = received.shape[0]
     return pl.pallas_call(
-        functools.partial(splat_kernel, cells, groups),
+        functools.partial(splat_kernel, groups),
         out_shape=jax.ShapeDtypeStruct((copies, cells, LANES), bf16),
-        in_specs=[pl.BlockSpec(memory_space=pltpu.VMEM)],
+        in_specs=[pl.BlockSpec(memory_space=pltpu.VMEM)] + [pl.BlockSpec(memory_space=pl.ANY)] * len(early),
         out_specs=pl.BlockSpec(memory_space=pltpu.VMEM),
         scratch_shapes=[
             pltpu.VMEM((rows, LANES), f32),
@@ -240,51 +253,72 @@
         ],
         compiler_params=pltpu.CompilerParams(vmem_limit_bytes=12 * MIB),
         name="join_splat",
-    )(received)
-
-
-def mlp_kernel(own_ref, f_ref, ow_ref, base_ref, gain_ref, up_ref, down_ref, bev_ref, mix_ref, bev_s):
-    heads = f_ref.shape[0]
+    )(received, *early)
+
+
+def mlp_kernel(own_ref, *refs):
+    weights, (f_ref, base_hbm, gain_ref, up_ref, down_hbm) = refs[:4], refs[4:9]
+    bev_ref, mix_ref, bev_s, base_s, down_s, sems = refs[9:]
+    base_copy = pltpu.make_async_copy(base_hbm, base_s, sems.at[0])
+    down_copy = pltpu.make_async_copy(down_hbm, down_s, sems.at[1])
+    base_copy.start()
+    down_copy.start()
     share = bev_ref.shape[0]
-    features = jnp.concatenate([f_ref[h] for h in range(heads)], axis=1)
-    bev = base_ref[...].astype(f32) + dot(features, ow_ref[...].reshape(features.shape[1], -1))
+    own = own_ref[0]
+    projected = None
+    for k in range(0, len(weights), 2):
+        features = jnp.concatenate([f_ref[own ^ k], f_ref[own ^ (k + 1)]], axis=1)
+        term = dot(features, jnp.concatenate([weights[k][...], weights[k + 1][...]], axis=0))
+        projected = term if projected is None else projected + term
+    base_copy.wait()
+    bev = base_s[...].astype(f32) + projected
     bev_s[...] = bev
     mean_square = jnp.mean(bev * bev, axis=1, keepdims=True)
     normed = (bev * lax.rsqrt(mean_square + 1e-06) * gain_ref[...]).astype(bf16)
-    hidden_units = up_ref.shape[1]
+    bev_ref[...] = bev_s[pl.ds(pl.multiple_of(own * share, share), share), :]
     step = 256
-    mixed = None
-    for begin in range(0, hidden_units, step):
+    hidden = []
+    for begin in range(0, up_ref.shape[1], step):
         u = dot(normed, up_ref[:, begin : begin + step])
-        hidden = (0.5 * u * (1.0 + lax.erf(u * math.sqrt(0.5)))).astype(bf16)
-        term = dot(hidden, down_ref[begin : begin + step, :])
-        mixed = term if mixed is None else mixed + term
+        hidden.append((0.5 * u * (1.0 + lax.erf(u * math.sqrt(0.5)))).astype(bf16))
+    down_copy.wait()
+    mixed = dot(jnp.concatenate(hidden, axis=1), down_s[...])
     mix_ref[...] = mixed.astype(bf16)
-    start = pl.multiple_of(own_ref[0] * share, share)
-    bev_ref[...] = bev_s[pl.ds(start, share), :]
-
-
-def mlp(own, features, out_weight, base, gain, up, down):
+
+
+def mlp(own, weights, features, base, gain, up, down):
     heads = features.shape[0]
     cells, width = base.shape
-    vmem = pl.BlockSpec(memory_space=pltpu.VMEM)
+    vmem, hbm = pl.BlockSpec(memory_space=pltpu.VMEM), pl.BlockSpec(memory_space=pltpu.HBM)
     return pl.pallas_call(
         mlp_kernel,
         out_shape=(
             jax.ShapeDtypeStruct((cells // heads, width), f32),
             jax.ShapeDtypeStruct((cells, width), bf16),
         ),
-        in_specs=[pl.BlockSpec(memory_space=pltpu.SMEM)] + [vmem] * 6,
+        in_specs=[pl.BlockSpec(memory_space=pltpu.SMEM)] + [vmem] * 5 + [hbm, vmem, vmem, hbm],
         out_specs=(vmem, vmem),
-        scratch_shapes=[pltpu.VMEM((cells, width), f32)],
+        scratch_shapes=[
+            pltpu.VMEM((cells, width), f32),
+            pltpu.VMEM((cells, width), bf16),
+            pltpu.VMEM(down.shape, bf16),
+            pltpu.SemaphoreType.DMA((2,)),
+        ],
         compiler_params=pltpu.CompilerParams(vmem_limit_bytes=20 * MIB),
         name="project_mlp",
-    )(own, features, out_weight, base, gain, up, down)
-
-
-def to_all(x, axis):
-    count = lax.axis_size(axis)
-    return lax.all_to_all(jnp.broadcast_to(x[None], (count,) + x.shape), axis, 0, 0)
+    )(
+        own,
+        *weights,
+        features,
+        pltpu.with_memory_space_constraint(base, pltpu.HBM),
+        gain,
+        up,
+        pltpu.with_memory_space_constraint(down, pltpu.HBM),
+    )
+
+
+def swap(x, axis, bit):
+    return lax.ppermute(x, axis, [(i, i ^ bit) for i in range(lax.axis_size(axis))])
 
 
 def body(
@@ -309,16 +343,20 @@
         queries, key_states, value_states, tile_of.reshape(1, tok), cell_of, splat_weight, groups
     )
     q_all = lax.all_to_all(q_copies, "y", 0, 0)
-    ow_all = to_all(out_weight, "head")
     own_kv = lax.all_gather(kv, "z")
-    other_kv = lax.ppermute(own_kv, "core", [(0, 1), (1, 0)])
-    top, sums = attend_first(own_kv, q_all)
-    packed = attend_second(other_kv, q_all, top, sums, ow_all, tiles)
-    received = lax.all_to_all(packed.reshape(tiles, PIECE, LANES), ("z", "y", "core"), 0, 0)
-    features = splat(received.reshape(tiles * PIECE, LANES), cells, groups, heads)
+    own_kv, q_all = lax.optimization_barrier((own_kv, q_all))
+    other_kv = swap(own_kv, "core", 1)
+    sums = attend_first(own_kv, q_all)
+    packed = attend_second(other_kv, q_all, sums, tiles)
+    packed, out_weight = lax.optimization_barrier((packed, out_weight))
+    weights = tuple(swap(out_weight, "head", k) for k in range(heads - 1, 0, -1))[::-1]
+    received = lax.all_to_all(packed, ("z", "y", "core"), 0, 0)
+    features = splat(received.reshape(tiles * PIECE, LANES), weights, cells, groups, heads)
     features = lax.all_to_all(features, "head", 0, 0)
     own = lax.axis_index("head").astype(jnp.int32).reshape(1)
-    bev_rows, mixed = mlp(own, features, ow_all, bev_base[0], norm_gain[None, :], up_weight, down_weight)
+    bev_rows, mixed = mlp(
+        own, (out_weight,) + weights, features, bev_base[0], norm_gain[None, :], up_weight, down_weight
+    )
     mixed = lax.all_to_all(mixed.reshape(heads, cells // heads, mixed.shape[1]), "head", 0, 0)
     return (bev_rows + jnp.sum(mixed.astype(f32), axis=0)).astype(bf16)[None]
 

time: 150 us -> 128 us (0.85)
  blocking collectives: 87.6 us -> 51.6 us
  starting transfers between devices: 16.6 us -> 33.3 us
  local copies, waits for them, and re-layouts: 9.26 us -> 0.7 us
  waiting for transfers between devices: 16.4 us -> 23 us
    all_to_all x1 -> x0, blocking collectives: 35.6 us -> none  [body(): lax.all_to_all(packed.reshape(tiles, PIECE, LANES), ('z', 'y', 'core'), 0...]
    ppermute x1 -> x4, waiting for transfers between devices: 0.01 us -> 13.3 us  [swap(): lax.ppermute(x, axis, [(i, i ^ bit) for i in range(lax.axis_size(axis))])]
    ppermute x1 -> x4, starting transfers between devices: 1.91 us -> 12.5 us  [swap(): lax.ppermute(x, axis, [(i, i ^ bit) for i in range(lax.axis_size(axis))])]
    all_to_all x1, waiting for transfers between devices: 9.51 us -> 2.45 us  [body(): received = lax.all_to_all(packed, ('z', 'y', 'core'), 0, 0)]
    unnamed x18 -> x6, local copies, waits for them, and re-layouts: 7.2 us -> 0.7 us
    all_to_all x1, starting transfers between devices: 4.29 us -> 9.57 us  [body(): received = lax.all_to_all(packed, ('z', 'y', 'core'), 0, 0)]
    pallas_call x3, Pallas kernels: 13.3 us -> 11.1 us  [the longest x1 6.34 us: attend_second(): pl.pallas_call(second_kernel, out_shape=jax.ShapeDtypeStruct((tiles, PIEC...]
    broadcast_in_dim x1 -> x0, local copies, waits for them, and re-layouts: 2.06 us -> none  [to_all(): jnp.broadcast_to(x[None], (count,) + x.shape)]
  transfers between devices with their start and end apart: 4 -> 7, of which waited for: 2 -> 5; matrix products, arithmetic and copies ran while one was open for 1% -> 0% of each run, Pallas kernels for 3% -> 3%
where the time goes in v6:
time: 128 us; the launch traced here: 126 us
  blocking collectives  51.6 us (40%)
  starting transfers between devices  33.3 us (26%)
  waiting for transfers between devices  23 us (18%)
  Pallas kernels  16.9 us (13%)
    all_gather x1, blocking collectives, body(): own_kv = lax.all_gather(kv, 'z')  38.7 us
    ppermute x4, waiting for transfers between devices, swap(): lax.ppermute(x, axis, [(i, i ^ bit) for i in range(lax.axis_size(axis))])  13.3 us
    all_to_all x1, blocking collectives, body(): lax.all_to_all(mixed.reshape(heads, cells // heads, mixed.shape[1]), 'hea...  13 us
    ppermute x4, starting transfers between devices, swap(): lax.ppermute(x, axis, [(i, i ^ bit) for i in range(lax.axis_size(axis))])  12.5 us
    all_to_all x1, starting transfers between devices, body(): received = lax.all_to_all(packed, ('z', 'y', 'core'), 0, 0)  9.57 us
    all_to_all x1, waiting for transfers between devices, body(): features = lax.all_to_all(features, 'head', 0, 0)  7.24 us
    all_to_all x1, starting transfers between devices, body(): q_all = lax.all_to_all(q_copies, 'y', 0, 0)  6.97 us
    pallas_call x1, Pallas kernels, attend_second(): pl.pallas_call(second_kernel, out_shape=jax.ShapeDtypeStruct((tiles, PIEC...  6.34 us
  transfers between devices with their start and end apart: 7, of which 5 were waited for; matrix products, arithmetic and copies ran while one was open for 0% of the time, Pallas kernels for 3%

profile of v6, /device:TPU:56, one launch (start us, length us, event | category | flops | bytes accessed | tf_op | source)
XLA Modules:
  0.0 126.4 jit_solution(10340276292294199038)
XLA Ops:
  0.0 1.8 %prologue.1 = (bf16[4,160,256]{2,1,0:T(8,128)(2,1)}, bf16[320,128]{1,0:T(8,128)(2,1)}) custom-call(bf16[1,160,128]{2,1,0:T(8,128)(2,1)} %q_ref.1, bf16[1,160,128]{2,1,0:T(8,128)(2,1)} %k_ref.1, bf16[1,160,128]{2,1,0:T(8,128)(2,1)} %v_ref.1, s32[1,160]{1,0:T(1,128)} %bitcast.15, s32[1,160]{1,0:T(1,128)} %cell_ref.1, f32[1,160]{1,0:T(1,128)} %splat_ref.1), custom_call_target="tpu_custom_call" | custom-call | tf_op jit(solution)/shard_map/prologue/pallas_call | solution.py:57
  1.8 7.0 %all-to-all-start = ((bf16[4,160,256]{2,1,0:T(8,128)(2,1)}), bf16[4,160,256]{2,1,0:T(8,128)(2,1)S(1)}, u32[]{:S(2)}, u32[]{:S(2)}) async-start(bf16[4,160,256]{2,1,0:T(8,128)(2,1)} %get-tuple-element.14), calls=%async_computation | async-start | bytes 655360 | tf_op jit(solution)/shard_map/all_to_all | solution.py:345
  8.8 38.7 %all-gather = bf16[3840,128]{1,0:T(8,128)(2,1)S(1)} all-gather(bf16[320,128]{1,0:T(8,128)(2,1)} %get-tuple-element.13), channel_id=2, replica_groups=mesh['z'=12,'y'=4,'core'=2,'head'=4,'scene'=2] {'z'}, dimensions={0}, use_global_device_ids=true | all-gather | bytes 1064960 | tf_op jit(solution)/shard_map/all_gather | solution.py:346
  47.5 0.0 all-to-all-done.q_ref
  47.5 1.9 %collective-permute-start = (bf16[12,320,128]{2,1,0:T(8,128)(2,1)S(1)}, bf16[12,320,128]{2,1,0:T(8,128)(2,1)S(1)}, u32[]{:S(2)}, u32[]{:S(2)}) collective-permute-start(bf16[12,320,128]{2,1,0:T(8,128)(2,1)S(1)} %bitcast.10), channel_id=1, source_target_pairs={{0,8},{8,0},{1,9},{9,1},{2,10},{10,2},{3,11},{11,3},{4,12},{12,4},... | collective-permute-start | bytes 2949128 | tf_op jit(solution)/shard_map/ppermute | solution.py:321
  49.4 3.8 %attend_own_core.1.sum_ref = f32[2,640,128]{2,1,0:T(8,128)S(1)} custom-call(bf16[12,320,128]{2,1,0:T(8,128)(2,1)S(1)} %bitcast.11, bf16[4,160,256]{2,1,0:T(8,128)(2,1)S(1)} %all-to-all-done.q_ref), custom_call_target="tpu_custom_call" | custom-call | flops 1258291200 | bytes 327680 | tf_op jit(solution)/shard_map/attend_own_core/pallas_call | solution.py:167
  53.2 0.0 collective-permute-done.kv_ref
  53.2 6.3 %attend_other_core.1 = bf16[96,24,128]{2,1,0:T(8,128)(2,1)} custom-call(bf16[12,320,128]{2,1,0:T(8,128)(2,1)S(1)} %collective-permute-done.kv_ref, bf16[4,160,256]{2,1,0:T(8,128)(2,1)S(1)} %all-to-all-done.q_ref, f32[2,640,128]{2,1,0:T(8,128)S(1)} %attend_own_core.1.sum_ref), custom_call_target="tpu_custom_call" | custom-call | flops 1258291200 | bytes 327680 | tf_op jit(solution)/shard_map/attend_other_core/pallas_call | solution.py:184
  59.5 0.0 copy-start
  59.5 0.0 copy-start.2
  59.5 9.6 %all-to-all-start.1 = ((bf16[96,24,128]{2,1,0:T(8,128)(2,1)}), bf16[96,24,128]{2,1,0:T(8,128)(2,1)S(1)}, u32[]{:S(2)}, u32[]{:S(2)}) async-start(bf16[96,24,128]{2,1,0:T(8,128)(2,1)} %attend_other_core.1), calls=%async_computation.1 | async-start | bytes 1179648 | tf_op jit(solution)/shard_map/all_to_all | solution.py:353
  69.1 3.4 %collective-permute-start.1 = (bf16[128,1024]{1,0:T(8,128)(2,1)}, bf16[128,1024]{1,0:T(8,128)(2,1)S(1)}, u32[]{:S(2)}, u32[]{:S(2)}) collective-permute-start(bf16[128,1024]{1,0:T(8,128)(2,1)} %refs_0_), channel_id=1, source_target_pairs={{0,2},{2,0},{4,6},{6,4},{1,3},{3,1},{5,7},{7,5},{8,10},{10,8},{12,... | collective-permute-start | bytes 786440 | tf_op jit(solution)/shard_map/ppermute | solution.py:321
  72.5 4.6 %collective-permute-start.2 = (bf16[128,1024]{1,0:T(8,128)(2,1)}, bf16[128,1024]{1,0:T(8,128)(2,1)S(1)}, u32[]{:S(2)}, u32[]{:S(2)}) collective-permute-start(bf16[128,1024]{1,0:T(8,128)(2,1)} %refs_0_), channel_id=1, source_target_pairs={{0,4},{2,6},{4,0},{6,2},{1,5},{3,7},{5,1},{7,3},{8,12},{10,14},{12... | collective-permute-start | bytes 786440 | tf_op jit(solution)/shard_map/ppermute | solution.py:321
  77.2 2.6 %collective-permute-start.3 = (bf16[128,1024]{1,0:T(8,128)(2,1)}, bf16[128,1024]{1,0:T(8,128)(2,1)S(1)}, u32[]{:S(2)}, u32[]{:S(2)}) collective-permute-start(bf16[128,1024]{1,0:T(8,128)(2,1)} %refs_0_), channel_id=1, source_target_pairs={{0,6},{2,4},{4,2},{6,0},{1,7},{3,5},{5,3},{7,1},{8,14},{10,12},{12... | collective-permute-start | bytes 786440 | tf_op jit(solution)/shard_map/ppermute | solution.py:321
  79.7 0.6 collective-permute-done.1.refs_0_.refs_1_
  80.3 7.1 %collective-permute-done.2.refs_1_.refs_2_ = bf16[128,1024]{1,0:T(8,128)(2,1)S(1)} collective-permute-done((bf16[128,1024]{1,0:T(8,128)(2,1)}, bf16[128,1024]{1,0:T(8,128)(2,1)S(1)}, u32[]{:S(2)}, u32[]{:S(2)}) %collective-permute-start.2) | collective-permute-done | bytes 262176 | tf_op jit(solution)/shard_map/ppermute | solution.py:321
  87.5 5.5 %collective-permute-done.3.refs_2_.refs_3_ = bf16[128,1024]{1,0:T(8,128)(2,1)S(1)} collective-permute-done((bf16[128,1024]{1,0:T(8,128)(2,1)}, bf16[128,1024]{1,0:T(8,128)(2,1)S(1)}, u32[]{:S(2)}, u32[]{:S(2)}) %collective-permute-start.3) | collective-permute-done | bytes 262176 | tf_op jit(solution)/shard_map/ppermute | solution.py:321
  93.0 2.5 %all-to-all-done.1 = bf16[96,24,128]{2,1,0:T(8,128)(2,1)S(1)} async-done(((bf16[96,24,128]{2,1,0:T(8,128)(2,1)}), bf16[96,24,128]{2,1,0:T(8,128)(2,1)S(1)}, u32[]{:S(2)}, u32[]{:S(2)}) %all-to-all-start.1) | async-done | bytes 589856 | tf_op jit(solution)/shard_map/all_to_all | solution.py:353
  95.4 1.0 join_splat.1
  96.5 0.0 copy-start.1
  96.5 0.7 copy-done.1
  97.2 4.3 %all-to-all-start.2 = ((bf16[4,256,128]{2,1,0:T(8,128)(2,1)}), bf16[4,256,128]{2,1,0:T(8,128)(2,1)S(1)}, u32[]{:S(2)}, u32[]{:S(2)}) async-start(bf16[4,256,128]{2,1,0:T(8,128)(2,1)} %copy-done.1), calls=%async_computation.2 | async-start | bytes 524288 | tf_op jit(solution)/shard_map/all_to_all | solution.py:355
  101.5 7.2 %all-to-all-done.2.refs_4_ = bf16[4,256,128]{2,1,0:T(8,128)(2,1)S(1)} async-done(((bf16[4,256,128]{2,1,0:T(8,128)(2,1)}), bf16[4,256,128]{2,1,0:T(8,128)(2,1)S(1)}, u32[]{:S(2)}, u32[]{:S(2)}) %all-to-all-start.2) | async-done | bytes 262176 | tf_op jit(solution)/shard_map/all_to_all | solution.py:355
  108.7 0.0 copy-done
  108.7 0.0 copy-done.2
  108.7 4.0 %project_mlp.1 = (f32[64,1024]{1,0:T(8,128)S(1)}, bf16[256,1024]{1,0:T(8,128)(2,1)S(1)}) custom-call(s32[1]{0:T(128)} %bitcast.own_ref, bf16[128,1024]{1,0:T(8,128)(2,1)} %refs_0_, bf16[128,1024]{1,0:T(8,128)(2,1)S(1)} %collective-permute-done.1.refs_0_.refs_1_, bf16[128,1024]{1,0:T(8,128)(2,1)S(1)} %collective-permute-done.2.refs_1_.refs_2_, ...), custom_call_target="tpu_custom_call" | custom-call | tf_op jit(solution)/shard_map/project_mlp/pallas_call | solution.py:293
  112.7 13.0 %all_to_all.20 = bf16[4,64,1024]{2,1,0:T(8,128)(2,1)S(1)} all-to-all(bf16[4,64,1024]{2,1,0:T(8,128)(2,1)S(1)} %bitcast.12), channel_id=1, replica_groups=mesh['z'=12,'y'=4,'core'=2,'head'=4,'scene'=2] {'head'}, dimensions={0} | all-to-all | bytes 1048576 | tf_op jit(solution)/shard_map/all_to_all | solution.py:360
  125.7 0.1 convert_reduce_fusion
  125.7 0.7 fusion
Async XLA Ops:
  1.8 45.6 %all-to-all-start = ((bf16[4,160,256]{2,1,0:T(8,128)(2,1)}), bf16[4,160,256]{2,1,0:T(8,128)(2,1)S(1)}, u32[]{:S(2)}, u32[]{:S(2)}) async-start(bf16[4,160,256]{2,1,0:T(8,128)(2,1)} %get-tuple-element.14), calls=%async_computation | async-start | bytes 655360 | tf_op jit(solution)/shard_map/all_to_all | solution.py:345
  47.5 5.7 %collective-permute-start = (bf16[12,320,128]{2,1,0:T(8,128)(2,1)S(1)}, bf16[12,320,128]{2,1,0:T(8,128)(2,1)S(1)}, u32[]{:S(2)}, u32[]{:S(2)}) collective-permute-start(bf16[12,320,128]{2,1,0:T(8,128)(2,1)S(1)} %bitcast.10), channel_id=1, source_target_pairs={{0,8},{8,0},{1,9},{9,1},{2,10},{10,2},{3,11},{11,3},{4,12},{12,4},... | collective-permute-start | bytes 2949128 | tf_op jit(solution)/shard_map/ppermute | solution.py:321
  59.5 49.2 %copy-start = (bf16[1024,1024]{1,0:T(8,128)(2,1)S(1)}, bf16[1024,1024]{1,0:T(8,128)(2,1)}, u32[]{:S(2)}) copy-start(bf16[1024,1024]{1,0:T(8,128)(2,1)} %refs_7_.1) | copy-start | bytes 6291460
  59.5 49.2 %copy-start.2 = (f32[1024]{0:T(1024)S(1)}, f32[1024]{0:T(1024)}, u32[]{:S(2)}) copy-start(f32[1024]{0:T(1024)} %param.18) | copy-start | bytes 12292
  59.5 35.9 %all-to-all-start.1 = ((bf16[96,24,128]{2,1,0:T(8,128)(2,1)}), bf16[96,24,128]{2,1,0:T(8,128)(2,1)S(1)}, u32[]{:S(2)}, u32[]{:S(2)}) async-start(bf16[96,24,128]{2,1,0:T(8,128)(2,1)} %attend_other_core.1), calls=%async_computation.1 | async-start | bytes 1179648 | tf_op jit(solution)/shard_map/all_to_all | solution.py:353
  69.1 11.3 %collective-permute-start.1 = (bf16[128,1024]{1,0:T(8,128)(2,1)}, bf16[128,1024]{1,0:T(8,128)(2,1)S(1)}, u32[]{:S(2)}, u32[]{:S(2)}) collective-permute-start(bf16[128,1024]{1,0:T(8,128)(2,1)} %refs_0_), channel_id=1, source_target_pairs={{0,2},{2,0},{4,6},{6,4},{1,3},{3,1},{5,7},{7,5},{8,10},{10,8},{12,... | collective-permute-start | bytes 786440 | tf_op jit(solution)/shard_map/ppermute | solution.py:321
  72.5 15.0 %collective-permute-start.2 = (bf16[128,1024]{1,0:T(8,128)(2,1)}, bf16[128,1024]{1,0:T(8,128)(2,1)S(1)}, u32[]{:S(2)}, u32[]{:S(2)}) collective-permute-start(bf16[128,1024]{1,0:T(8,128)(2,1)} %refs_0_), channel_id=1, source_target_pairs={{0,4},{2,6},{4,0},{6,2},{1,5},{3,7},{5,1},{7,3},{8,12},{10,14},{12... | collective-permute-start | bytes 786440 | tf_op jit(solution)/shard_map/ppermute | solution.py:321
  77.2 15.8 %collective-permute-start.3 = (bf16[128,1024]{1,0:T(8,128)(2,1)}, bf16[128,1024]{1,0:T(8,128)(2,1)S(1)}, u32[]{:S(2)}, u32[]{:S(2)}) collective-permute-start(bf16[128,1024]{1,0:T(8,128)(2,1)} %refs_0_), channel_id=1, source_target_pairs={{0,6},{2,4},{4,2},{6,0},{1,7},{3,5},{5,3},{7,1},{8,14},{10,12},{12... | collective-permute-start | bytes 786440 | tf_op jit(solution)/shard_map/ppermute | solution.py:321
  96.5 0.7 copy-start.1
  97.2 11.5 %all-to-all-start.2 = ((bf16[4,256,128]{2,1,0:T(8,128)(2,1)}), bf16[4,256,128]{2,1,0:T(8,128)(2,1)S(1)}, u32[]{:S(2)}, u32[]{:S(2)}) async-start(bf16[4,256,128]{2,1,0:T(8,128)(2,1)} %copy-done.1), calls=%async_computation.2 | async-start | bytes 524288 | tf_op jit(solution)/shard_map/all_to_all | solution.py:355

commit v7 on v6

--- a/solution.py
+++ b/solution.py
@@ -12,7 +12,7 @@
 HS = 64
 LANES = 128
 SLOTS = 4
-PIECE = 24
+PIECE = 18
 EXPONENT = math.log2(math.e) / math.sqrt(HS)
 MIB = 1024 * 1024
 
@@ -110,7 +110,6 @@
 
 def second_kernel(kv_ref, q_ref, sum_ref, out_ref, k_s, v_s, o_s, extra_s, slot_s, slot_t):
     groups, tok = q_ref.shape[0], q_ref.shape[1]
-    tiles = out_ref.shape[0]
     slots, width = groups * SLOTS, groups * tok
     stage_keys(kv_ref, k_s, v_s)
     lane = lax.broadcasted_iota(jnp.int32, (tok, LANES), 1)
@@ -138,19 +137,14 @@
                 extra = jnp.where(lane_f == step * 32.0 + head * 16.0 + place, piece, extra)
         o_s[rows, :] = jnp.where(lane < HS, sums[0], sums[1]).astype(bf16)
         extra_s[rows, :] = extra.astype(bf16)
-        slot_s[rows, :] = jnp.where(lane == 0, tile * slots + place, tile * 8.0)
+        slot_s[rows, :] = tile * PIECE + jnp.where(lane == 0, place, float(slots))
     slot_t[...] = jnp.transpose(slot_s[...])
-
-    def one_hot(begin, count, at):
-        row = (lax.broadcasted_iota(jnp.int32, (count, width), 0) + begin).astype(f32)
-        return jnp.where(row == slot_t[at : at + 1, :], 1.0, 0.0).astype(bf16)
-
-    step = 24
-    for begin in range(0, tiles, step):
-        main = dot(one_hot(begin * slots, step * slots, 0), o_s[...]).astype(bf16)
-        tail = dot(one_hot(begin * 8, step * 8, 1), extra_s[...]).astype(bf16)
-        out_ref[pl.ds(begin, step), :slots, :] = main.reshape(step, slots, LANES)
-        out_ref[pl.ds(begin, step), slots:, :] = tail.reshape(step, 8, LANES)
+    step = 16 * PIECE
+    for begin in range(0, out_ref.shape[0], step):
+        row = (lax.broadcasted_iota(jnp.int32, (step, width), 0) + begin).astype(f32)
+        main = jnp.where(row == slot_t[0:1, :], 1.0, 0.0).astype(bf16)
+        tail = jnp.where(row == slot_t[1:2, :], 1.0, 0.0).astype(bf16)
+        out_ref[pl.ds(begin, step), :] = (dot(main, o_s[...]) + dot(tail, extra_s[...])).astype(bf16)
 
 
 def attention_cost(queries, keys):
@@ -183,7 +177,7 @@
     vmem = pl.BlockSpec(memory_space=pltpu.VMEM)
     return pl.pallas_call(
         second_kernel,
-        out_shape=jax.ShapeDtypeStruct((tiles, PIECE, LANES), bf16),
+        out_shape=jax.ShapeDtypeStruct((tiles * PIECE, LANES), bf16),
         in_specs=[vmem] * 3,
         out_specs=vmem,
         scratch_shapes=[
@@ -262,7 +256,6 @@
     base_copy = pltpu.make_async_copy(base_hbm, base_s, sems.at[0])
     down_copy = pltpu.make_async_copy(down_hbm, down_s, sems.at[1])
     base_copy.start()
-    down_copy.start()
     share = bev_ref.shape[0]
     own = own_ref[0]
     projected = None
@@ -271,6 +264,7 @@
         term = dot(features, jnp.concatenate([weights[k][...], weights[k + 1][...]], axis=0))
         projected = term if projected is None else projected + term
     base_copy.wait()
+    down_copy.start()
     bev = base_s[...].astype(f32) + projected
     bev_s[...] = bev
     mean_square = jnp.mean(bev * bev, axis=1, keepdims=True)
@@ -350,7 +344,7 @@
     packed = attend_second(other_kv, q_all, sums, tiles)
     packed, out_weight = lax.optimization_barrier((packed, out_weight))
     weights = tuple(swap(out_weight, "head", k) for k in range(heads - 1, 0, -1))[::-1]
-    received = lax.all_to_all(packed, ("z", "y", "core"), 0, 0)
+    received = lax.all_to_all(packed.reshape(tiles, PIECE // 2, 2, LANES), ("z", "y", "core"), 0, 0)
     features = splat(received.reshape(tiles * PIECE, LANES), weights, cells, groups, heads)
     features = lax.all_to_all(features, "head", 0, 0)
     own = lax.axis_index("head").astype(jnp.int32).reshape(1)

time: 128 us -> 126 us (0.984)
  waiting for transfers between devices: 23 us -> 21 us
  Pallas kernels: 16.9 us -> 18.8 us
    all_to_all x1, waiting for transfers between devices: 2.45 us -> 0.01 us  [body(): lax.all_to_all(packed.reshape(tiles, PIECE // 2, 2, LANES), ('z', 'y', 'c...]
    pallas_call x1, Pallas kernels: 3.97 us -> 5.27 us  [mlp(): pl.pallas_call(mlp_kernel, out_shape=(jax.ShapeDtypeStruct((cells // head...]
  transfers between devices with their start and end apart: 7 -> 7, of which waited for: 5 -> 4; matrix products, arithmetic and copies ran while one was open for 0% -> 0% of each run, Pallas kernels for 3% -> 3%
where the time goes in v7:
time: 126 us; the launch traced here: 125 us
  blocking collectives  50.8 us (40%)
  starting transfers between devices  32.5 us (26%)
  waiting for transfers between devices  21 us (17%)
  Pallas kernels  18.8 us (15%)
    all_gather x1, blocking collectives, body(): own_kv = lax.all_gather(kv, 'z')  38.7 us
    ppermute x4, waiting for transfers between devices, swap(): lax.ppermute(x, axis, [(i, i ^ bit) for i in range(lax.axis_size(axis))])  13.3 us
    ppermute x4, starting transfers between devices, swap(): lax.ppermute(x, axis, [(i, i ^ bit) for i in range(lax.axis_size(axis))])  12.5 us
    all_to_all x1, blocking collectives, body(): lax.all_to_all(mixed.reshape(heads, cells // heads, mixed.shape[1]), 'hea...  12.1 us
    all_to_all x1, starting transfers between devices, body(): lax.all_to_all(packed.reshape(tiles, PIECE // 2, 2, LANES), ('z', 'y', 'c...  9.57 us
    all_to_all x1, waiting for transfers between devices, body(): features = lax.all_to_all(features, 'head', 0, 0)  7.72 us
    all_to_all x1, starting transfers between devices, body(): q_all = lax.all_to_all(q_copies, 'y', 0, 0)  6.97 us
    pallas_call x1, Pallas kernels, attend_second(): pl.pallas_call(second_kernel, out_shape=jax.ShapeDtypeStruct((tiles * PIE...  6.94 us
  transfers between devices with their start and end apart: 7, of which 4 were waited for; matrix products, arithmetic and copies ran while one was open for 0% of the time, Pallas kernels for 3%

profile of v7, /device:TPU:56, one launch (start us, length us, event | category | flops | bytes accessed | tf_op | source)
XLA Modules:
  0.0 124.6 jit_solution(12435753002953405368)
XLA Ops:
  0.0 1.8 %prologue.1 = (bf16[4,160,256]{2,1,0:T(8,128)(2,1)}, bf16[320,128]{1,0:T(8,128)(2,1)}) custom-call(bf16[1,160,128]{2,1,0:T(8,128)(2,1)} %q_ref.1, bf16[1,160,128]{2,1,0:T(8,128)(2,1)} %k_ref.1, bf16[1,160,128]{2,1,0:T(8,128)(2,1)} %v_ref.1, s32[1,160]{1,0:T(1,128)} %bitcast.16, s32[1,160]{1,0:T(1,128)} %cell_ref.1, f32[1,160]{1,0:T(1,128)} %splat_ref.1), custom_call_target="tpu_custom_call" | custom-call | tf_op jit(solution)/shard_map/prologue/pallas_call | solution.py:57
  1.8 7.0 %all-to-all-start = ((bf16[4,160,256]{2,1,0:T(8,128)(2,1)}), bf16[4,160,256]{2,1,0:T(8,128)(2,1)S(1)}, u32[]{:S(2)}, u32[]{:S(2)}) async-start(bf16[4,160,256]{2,1,0:T(8,128)(2,1)} %get-tuple-element.14), calls=%async_computation | async-start | bytes 655360 | tf_op jit(solution)/shard_map/all_to_all | solution.py:339
  8.8 38.7 %all-gather = bf16[3840,128]{1,0:T(8,128)(2,1)S(1)} all-gather(bf16[320,128]{1,0:T(8,128)(2,1)} %get-tuple-element.13), channel_id=2, replica_groups=mesh['z'=12,'y'=4,'core'=2,'head'=4,'scene'=2] {'z'}, dimensions={0}, use_global_device_ids=true | all-gather | bytes 1064960 | tf_op jit(solution)/shard_map/all_gather | solution.py:340
  47.5 0.0 all-to-all-done.q_ref
  47.5 1.9 %collective-permute-start = (bf16[12,320,128]{2,1,0:T(8,128)(2,1)S(1)}, bf16[12,320,128]{2,1,0:T(8,128)(2,1)S(1)}, u32[]{:S(2)}, u32[]{:S(2)}) collective-permute-start(bf16[12,320,128]{2,1,0:T(8,128)(2,1)S(1)} %bitcast.11), channel_id=1, source_target_pairs={{0,8},{8,0},{1,9},{9,1},{2,10},{10,2},{3,11},{11,3},{4,12},{12,4},... | collective-permute-start | bytes 2949128 | tf_op jit(solution)/shard_map/ppermute | solution.py:315
  49.4 3.8 %attend_own_core.1.sum_ref = f32[2,640,128]{2,1,0:T(8,128)S(1)} custom-call(bf16[12,320,128]{2,1,0:T(8,128)(2,1)S(1)} %bitcast.12, bf16[4,160,256]{2,1,0:T(8,128)(2,1)S(1)} %all-to-all-done.q_ref), custom_call_target="tpu_custom_call" | custom-call | flops 1258291200 | bytes 327680 | tf_op jit(solution)/shard_map/attend_own_core/pallas_call | solution.py:161
  53.2 0.0 collective-permute-done.kv_ref
  53.2 6.9 %attend_other_core.1 = bf16[1728,128]{1,0:T(8,128)(2,1)} custom-call(bf16[12,320,128]{2,1,0:T(8,128)(2,1)S(1)} %collective-permute-done.kv_ref, bf16[4,160,256]{2,1,0:T(8,128)(2,1)S(1)} %all-to-all-done.q_ref, f32[2,640,128]{2,1,0:T(8,128)S(1)} %attend_own_core.1.sum_ref), custom_call_target="tpu_custom_call" | custom-call | flops 1258291200 | bytes 327680 | tf_op jit(solution)/shard_map/attend_other_core/pallas_call | solution.py:178
  60.1 0.0 copy-start
  60.1 0.0 copy-start.2
  60.1 9.6 %all-to-all-start.1 = ((bf16[96,9,2,128]{3,2,1,0:T(2,128)(2,1)}), bf16[96,9,2,128]{3,2,1,0:T(2,128)(2,1)S(1)}, u32[]{:S(2)}, u32[]{:S(2)}) async-start(bf16[96,9,2,128]{3,2,1,0:T(2,128)(2,1)} %bitcast.3), calls=%async_computation.1 | async-start | bytes 884736 | tf_op jit(solution)/shard_map/all_to_all | solution.py:347
  69.7 3.4 %collective-permute-start.1 = (bf16[128,1024]{1,0:T(8,128)(2,1)}, bf16[128,1024]{1,0:T(8,128)(2,1)S(1)}, u32[]{:S(2)}, u32[]{:S(2)}) collective-permute-start(bf16[128,1024]{1,0:T(8,128)(2,1)} %refs_0_), channel_id=1, source_target_pairs={{0,2},{2,0},{4,6},{6,4},{1,3},{3,1},{5,7},{7,5},{8,10},{10,8},{12,... | collective-permute-start | bytes 786440 | tf_op jit(solution)/shard_map/ppermute | solution.py:315
  73.1 4.6 %collective-permute-start.2 = (bf16[128,1024]{1,0:T(8,128)(2,1)}, bf16[128,1024]{1,0:T(8,128)(2,1)S(1)}, u32[]{:S(2)}, u32[]{:S(2)}) collective-permute-start(bf16[128,1024]{1,0:T(8,128)(2,1)} %refs_0_), channel_id=1, source_target_pairs={{0,4},{2,6},{4,0},{6,2},{1,5},{3,7},{5,1},{7,3},{8,12},{10,14},{12... | collective-permute-start | bytes 786440 | tf_op jit(solution)/shard_map/ppermute | solution.py:315
  77.8 2.6 %collective-permute-start.3 = (bf16[128,1024]{1,0:T(8,128)(2,1)}, bf16[128,1024]{1,0:T(8,128)(2,1)S(1)}, u32[]{:S(2)}, u32[]{:S(2)}) collective-permute-start(bf16[128,1024]{1,0:T(8,128)(2,1)} %refs_0_), channel_id=1, source_target_pairs={{0,6},{2,4},{4,2},{6,0},{1,7},{3,5},{5,3},{7,1},{8,14},{10,12},{12... | collective-permute-start | bytes 786440 | tf_op jit(solution)/shard_map/ppermute | solution.py:315
  80.3 0.6 collective-permute-done.1.refs_0_.refs_1_
  80.9 7.1 %collective-permute-done.2.refs_1_.refs_2_ = bf16[128,1024]{1,0:T(8,128)(2,1)S(1)} collective-permute-done((bf16[128,1024]{1,0:T(8,128)(2,1)}, bf16[128,1024]{1,0:T(8,128)(2,1)S(1)}, u32[]{:S(2)}, u32[]{:S(2)}) %collective-permute-start.2) | collective-permute-done | bytes 262176 | tf_op jit(solution)/shard_map/ppermute | solution.py:315
  88.1 5.5 %collective-permute-done.3.refs_2_.refs_3_ = bf16[128,1024]{1,0:T(8,128)(2,1)S(1)} collective-permute-done((bf16[128,1024]{1,0:T(8,128)(2,1)}, bf16[128,1024]{1,0:T(8,128)(2,1)S(1)}, u32[]{:S(2)}, u32[]{:S(2)}) %collective-permute-start.3) | collective-permute-done | bytes 262176 | tf_op jit(solution)/shard_map/ppermute | solution.py:315
  93.6 0.0 all-to-all-done.1
  93.6 1.0 join_splat.1
  94.6 0.0 copy-start.1
  94.6 0.7 copy-done.1
  95.3 3.4 %all-to-all-start.2 = ((bf16[4,256,128]{2,1,0:T(8,128)(2,1)}), bf16[4,256,128]{2,1,0:T(8,128)(2,1)S(1)}, u32[]{:S(2)}, u32[]{:S(2)}) async-start(bf16[4,256,128]{2,1,0:T(8,128)(2,1)} %copy-done.1), calls=%async_computation.2 | async-start | bytes 524288 | tf_op jit(solution)/shard_map/all_to_all | solution.py:349
  98.7 7.7 %all-to-all-done.2.refs_4_ = bf16[4,256,128]{2,1,0:T(8,128)(2,1)S(1)} async-done(((bf16[4,256,128]{2,1,0:T(8,128)(2,1)}), bf16[4,256,128]{2,1,0:T(8,128)(2,1)S(1)}, u32[]{:S(2)}, u32[]{:S(2)}) %all-to-all-start.2) | async-done | bytes 262176 | tf_op jit(solution)/shard_map/all_to_all | solution.py:349
  106.5 0.0 copy-done
  106.5 0.0 copy-done.2
  106.5 5.3 %project_mlp.1 = (f32[64,1024]{1,0:T(8,128)S(1)}, bf16[256,1024]{1,0:T(8,128)(2,1)S(1)}) custom-call(s32[1]{0:T(128)} %bitcast.own_ref, bf16[128,1024]{1,0:T(8,128)(2,1)} %refs_0_, bf16[128,1024]{1,0:T(8,128)(2,1)S(1)} %collective-permute-done.1.refs_0_.refs_1_, bf16[128,1024]{1,0:T(8,128)(2,1)S(1)} %collective-permute-done.2.refs_1_.refs_2_, ...), custom_call_target="tpu_custom_call" | custom-call | tf_op jit(solution)/shard_map/project_mlp/pallas_call | solution.py:287
  111.7 12.1 %all_to_all.20 = bf16[4,64,1024]{2,1,0:T(8,128)(2,1)S(1)} all-to-all(bf16[4,64,1024]{2,1,0:T(8,128)(2,1)S(1)} %bitcast.13), channel_id=1, replica_groups=mesh['z'=12,'y'=4,'core'=2,'head'=4,'scene'=2] {'head'}, dimensions={0} | all-to-all | bytes 1048576 | tf_op jit(solution)/shard_map/all_to_all | solution.py:354
  123.9 0.1 convert_reduce_fusion
  124.0 0.7 fusion
Async XLA Ops:
  1.8 45.6 %all-to-all-start = ((bf16[4,160,256]{2,1,0:T(8,128)(2,1)}), bf16[4,160,256]{2,1,0:T(8,128)(2,1)S(1)}, u32[]{:S(2)}, u32[]{:S(2)}) async-start(bf16[4,160,256]{2,1,0:T(8,128)(2,1)} %get-tuple-element.14), calls=%async_computation | async-start | bytes 655360 | tf_op jit(solution)/shard_map/all_to_all | solution.py:339
  47.5 5.7 %collective-permute-start = (bf16[12,320,128]{2,1,0:T(8,128)(2,1)S(1)}, bf16[12,320,128]{2,1,0:T(8,128)(2,1)S(1)}, u32[]{:S(2)}, u32[]{:S(2)}) collective-permute-start(bf16[12,320,128]{2,1,0:T(8,128)(2,1)S(1)} %bitcast.11), channel_id=1, source_target_pairs={{0,8},{8,0},{1,9},{9,1},{2,10},{10,2},{3,11},{11,3},{4,12},{12,4},... | collective-permute-start | bytes 2949128 | tf_op jit(solution)/shard_map/ppermute | solution.py:315
  60.1 46.3 %copy-start = (bf16[1024,1024]{1,0:T(8,128)(2,1)S(1)}, bf16[1024,1024]{1,0:T(8,128)(2,1)}, u32[]{:S(2)}) copy-start(bf16[1024,1024]{1,0:T(8,128)(2,1)} %refs_7_.1) | copy-start | bytes 6291460
  60.1 46.3 %copy-start.2 = (f32[1024]{0:T(1024)S(1)}, f32[1024]{0:T(1024)}, u32[]{:S(2)}) copy-start(f32[1024]{0:T(1024)} %param.18) | copy-start | bytes 12292
  60.1 33.5 %all-to-all-start.1 = ((bf16[96,9,2,128]{3,2,1,0:T(2,128)(2,1)}), bf16[96,9,2,128]{3,2,1,0:T(2,128)(2,1)S(1)}, u32[]{:S(2)}, u32[]{:S(2)}) async-start(bf16[96,9,2,128]{3,2,1,0:T(2,128)(2,1)} %bitcast.3), calls=%async_computation.1 | async-start | bytes 884736 | tf_op jit(solution)/shard_map/all_to_all | solution.py:347
  69.7 11.3 %collective-permute-start.1 = (bf16[128,1024]{1,0:T(8,128)(2,1)}, bf16[128,1024]{1,0:T(8,128)(2,1)S(1)}, u32[]{:S(2)}, u32[]{:S(2)}) collective-permute-start(bf16[128,1024]{1,0:T(8,128)(2,1)} %refs_0_), channel_id=1, source_target_pairs={{0,2},{2,0},{4,6},{6,4},{1,3},{3,1},{5,7},{7,5},{8,10},{10,8},{12,... | collective-permute-start | bytes 786440 | tf_op jit(solution)/shard_map/ppermute | solution.py:315
  73.1 15.0 %collective-permute-start.2 = (bf16[128,1024]{1,0:T(8,128)(2,1)}, bf16[128,1024]{1,0:T(8,128)(2,1)S(1)}, u32[]{:S(2)}, u32[]{:S(2)}) collective-permute-start(bf16[128,1024]{1,0:T(8,128)(2,1)} %refs_0_), channel_id=1, source_target_pairs={{0,4},{2,6},{4,0},{6,2},{1,5},{3,7},{5,1},{7,3},{8,12},{10,14},{12... | collective-permute-start | bytes 786440 | tf_op jit(solution)/shard_map/ppermute | solution.py:315
  77.8 15.8 %collective-permute-start.3 = (bf16[128,1024]{1,0:T(8,128)(2,1)}, bf16[128,1024]{1,0:T(8,128)(2,1)S(1)}, u32[]{:S(2)}, u32[]{:S(2)}) collective-permute-start(bf16[128,1024]{1,0:T(8,128)(2,1)} %refs_0_), channel_id=1, source_target_pairs={{0,6},{2,4},{4,2},{6,0},{1,7},{3,5},{5,3},{7,1},{8,14},{10,12},{12... | collective-permute-start | bytes 786440 | tf_op jit(solution)/shard_map/ppermute | solution.py:315
  94.6 0.7 copy-start.1
  95.3 11.1 %all-to-all-start.2 = ((bf16[4,256,128]{2,1,0:T(8,128)(2,1)}), bf16[4,256,128]{2,1,0:T(8,128)(2,1)S(1)}, u32[]{:S(2)}, u32[]{:S(2)}) async-start(bf16[4,256,128]{2,1,0:T(8,128)(2,1)} %copy-done.1), calls=%async_computation.2 | async-start | bytes 524288 | tf_op jit(solution)/shard_map/all_to_all | solution.py:349

commit v8 on v7

--- a/solution.py
+++ b/solution.py
@@ -15,6 +15,7 @@
 PIECE = 18
 EXPONENT = math.log2(math.e) / math.sqrt(HS)
 MIB = 1024 * 1024
+MLP_STEPS = 2
 
 f32 = jnp.float32
 bf16 = jnp.bfloat16
@@ -68,10 +69,10 @@
     )(queries, key_states, value_states, tile, cell, splat_weight)
 
 
-def attend_block(q_ref, group, k_s, v_s):
+def attend_blocks(q_ref, first, count, k_s, v_s):
     low = lax.broadcasted_iota(jnp.int32, (1, LANES), 1) < HS
-    q = q_ref[group, :, :LANES]
-    tok, span, step = q.shape[0], k_s.shape[0], 640
+    q = jnp.concatenate([q_ref[first + i, :, :LANES] for i in range(count)], axis=0)
+    rows, span, step = q.shape[0], k_s.shape[0], 640
     keeps = [jnp.where(low if head == 0 else ~low, 1.0, 0.0).astype(bf16) for head in range(2)]
     s = dot_nt(jnp.concatenate([q * keep for keep in keeps], axis=0), k_s[...])
     top = jnp.max(s, axis=1, keepdims=True)
@@ -79,9 +80,9 @@
     for begin in range(0, span, step):
         p = jnp.exp2((s[:, begin : begin + step] - top) * EXPONENT).astype(bf16)
         for head in range(2):
-            term = dot(p[head * tok : (head + 1) * tok], v_s[head, begin : begin + step, :])
+            term = dot(p[head * rows : (head + 1) * rows], v_s[head, begin : begin + step, :])
             sums[head] = term if sums[head] is None else sums[head] + term
-    return [(head, top[head * tok : (head + 1) * tok] * EXPONENT, sums[head]) for head in range(2)]
+    return [(head, top[head * rows : (head + 1) * rows] * EXPONENT, sums[head]) for head in range(2)]
 
 
 def stage_keys(kv_ref, k_s, v_s):
@@ -103,12 +104,12 @@
     groups, tok = q_ref.shape[0], q_ref.shape[1]
     stage_keys(kv_ref, k_s, v_s)
     lane = lax.broadcasted_iota(jnp.int32, (1, LANES), 1)
-    for group in range(groups):
-        for head, top, sums in attend_block(q_ref, group, k_s, v_s):
-            sum_ref[head, pl.ds(group * tok, tok), :] = jnp.where(lane == other_half(head)[1], top, sums)
-
-
-def second_kernel(kv_ref, q_ref, sum_ref, out_ref, k_s, v_s, o_s, extra_s, slot_s, slot_t):
+    for group in range(0, groups, 2):
+        for head, top, sums in attend_blocks(q_ref, group, 2, k_s, v_s):
+            sum_ref[head, pl.ds(group * tok, 2 * tok), :] = jnp.where(lane == other_half(head)[1], top, sums)
+
+
+def second_kernel(kv_ref, q_ref, sum_ref, out_ref, k_s, v_s, o_s, extra_s, slot_s, slot_t, packed_s):
     groups, tok = q_ref.shape[0], q_ref.shape[1]
     slots, width = groups * SLOTS, groups * tok
     stage_keys(kv_ref, k_s, v_s)
@@ -122,7 +123,7 @@
         gain = meta[:, 3:4] + meta[:, 4:5]
         sums = []
         extra = jnp.where(lane_f == 96.0 + place, cell, 0.0)
-        for head, top_b, sum_b in attend_block(q_ref, group, k_s, v_s):
+        for head, top_b, sum_b in attend_blocks(q_ref, group, 1, k_s, v_s):
             at, top_at = other_half(head)
             sum_a = sum_ref[head, rows, :]
             top_a = sum_a[:, top_at : top_at + 1]
@@ -137,14 +138,18 @@
                 extra = jnp.where(lane_f == step * 32.0 + head * 16.0 + place, piece, extra)
         o_s[rows, :] = jnp.where(lane < HS, sums[0], sums[1]).astype(bf16)
         extra_s[rows, :] = extra.astype(bf16)
-        slot_s[rows, :] = tile * PIECE + jnp.where(lane == 0, place, float(slots))
+        slot_s[rows, :] = jnp.where(lane == 0, tile * PIECE + place, tile)
     slot_t[...] = jnp.transpose(slot_s[...])
     step = 16 * PIECE
+    tiles = out_ref.shape[0] // PIECE
     for begin in range(0, out_ref.shape[0], step):
         row = (lax.broadcasted_iota(jnp.int32, (step, width), 0) + begin).astype(f32)
         main = jnp.where(row == slot_t[0:1, :], 1.0, 0.0).astype(bf16)
-        tail = jnp.where(row == slot_t[1:2, :], 1.0, 0.0).astype(bf16)
-        out_ref[pl.ds(begin, step), :] = (dot(main, o_s[...]) + dot(tail, extra_s[...])).astype(bf16)
+        packed_s[pl.ds(begin, step), :] = dot(main, o_s[...])
+    row = lax.broadcasted_iota(jnp.int32, (tiles, width), 0).astype(f32)
+    tail = jnp.where(row == slot_t[1:2, :], 1.0, 0.0).astype(bf16)
+    packed_s[pl.ds(slots, tiles, stride=PIECE), :] = dot(tail, extra_s[...])
+    out_ref[...] = packed_s[...].astype(bf16)
 
 
 def attention_cost(queries, keys):
@@ -187,6 +192,7 @@
             pltpu.VMEM((rows, LANES), bf16),
             pltpu.VMEM((rows, LANES), f32),
             pltpu.VMEM((LANES, rows), f32),
+            pltpu.VMEM((tiles * PIECE, LANES), f32),
         ],
         compiler_params=pltpu.CompilerParams(vmem_limit_bytes=16 * MIB),
         cost_estimate=attention_cost(rows, span),
@@ -256,6 +262,7 @@
     base_copy = pltpu.make_async_copy(base_hbm, base_s, sems.at[0])
     down_copy = pltpu.make_async_copy(down_hbm, down_s, sems.at[1])
     base_copy.start()
+    down_copy.start()
     share = bev_ref.shape[0]
     own = own_ref[0]
     projected = None
@@ -264,19 +271,20 @@
         term = dot(features, jnp.concatenate([weights[k][...], weights[k + 1][...]], axis=0))
         projected = term if projected is None else projected + term
     base_copy.wait()
-    down_copy.start()
     bev = base_s[...].astype(f32) + projected
     bev_s[...] = bev
     mean_square = jnp.mean(bev * bev, axis=1, keepdims=True)
     normed = (bev * lax.rsqrt(mean_square + 1e-06) * gain_ref[...]).astype(bf16)
     bev_ref[...] = bev_s[pl.ds(pl.multiple_of(own * share, share), share), :]
-    step = 256
-    hidden = []
+    step = up_ref.shape[1] // MLP_STEPS
+    mixed = None
     for begin in range(0, up_ref.shape[1], step):
         u = dot(normed, up_ref[:, begin : begin + step])
-        hidden.append((0.5 * u * (1.0 + lax.erf(u * math.sqrt(0.5)))).astype(bf16))
-    down_copy.wait()
-    mixed = dot(jnp.concatenate(hidden, axis=1), down_s[...])
+        hidden = (0.5 * u * (1.0 + lax.erf(u * math.sqrt(0.5)))).astype(bf16)
+        if begin == 0:
+            down_copy.wait()
+        term = dot(hidden, down_s[begin : begin + step, :])
+        mixed = term if mixed is None else mixed + term
     mix_ref[...] = mixed.astype(bf16)
 
 

time: 126 us -> 123 us (0.976)
  Pallas kernels: 18.8 us -> 16.3 us
where the time goes in v8:
time: 123 us; the launch traced here: 122 us
  blocking collectives  50.8 us (41%)
  starting transfers between devices  32.3 us (26%)
  waiting for transfers between devices  21.2 us (17%)
  Pallas kernels  16.3 us (13%)
    all_gather x1, blocking collectives, body(): own_kv = lax.all_gather(kv, 'z')  38.7 us
    ppermute x4, waiting for transfers between devices, swap(): lax.ppermute(x, axis, [(i, i ^ bit) for i in range(lax.axis_size(axis))])  13.4 us
    ppermute x4, starting transfers between devices, swap(): lax.ppermute(x, axis, [(i, i ^ bit) for i in range(lax.axis_size(axis))])  12.3 us
    all_to_all x1, blocking collectives, body(): lax.all_to_all(mixed.reshape(heads, cells // heads, mixed.shape[1]), 'hea...  12.2 us
    all_to_all x1, starting transfers between devices, body(): lax.all_to_all(packed.reshape(tiles, PIECE // 2, 2, LANES), ('z', 'y', 'c...  9.57 us
    all_to_all x1, waiting for transfers between devices, body(): features = lax.all_to_all(features, 'head', 0, 0)  7.78 us
    all_to_all x1, starting transfers between devices, body(): q_all = lax.all_to_all(q_copies, 'y', 0, 0)  6.97 us
    pallas_call x1, Pallas kernels, attend_second(): pl.pallas_call(second_kernel, out_shape=jax.ShapeDtypeStruct((tiles * PIE...  6.12 us
  transfers between devices with their start and end apart: 7, of which 4 were waited for; matrix products, arithmetic and copies ran while one was open for 0% of the time, Pallas kernels for 3%

profile of v8, /device:TPU:56, one launch (start us, length us, event | category | flops | bytes accessed | tf_op | source)
XLA Modules:
  0.0 122.2 jit_solution(8682792181420819558)
XLA Ops:
  0.0 1.8 %prologue.1 = (bf16[4,160,256]{2,1,0:T(8,128)(2,1)}, bf16[320,128]{1,0:T(8,128)(2,1)}) custom-call(bf16[1,160,128]{2,1,0:T(8,128)(2,1)} %q_ref.1, bf16[1,160,128]{2,1,0:T(8,128)(2,1)} %k_ref.1, bf16[1,160,128]{2,1,0:T(8,128)(2,1)} %v_ref.1, s32[1,160]{1,0:T(1,128)} %bitcast.16, s32[1,160]{1,0:T(1,128)} %cell_ref.1, f32[1,160]{1,0:T(1,128)} %splat_ref.1), custom_call_target="tpu_custom_call" | custom-call | tf_op jit(solution)/shard_map/prologue/pallas_call | solution.py:58
  1.8 7.0 %all-to-all-start = ((bf16[4,160,256]{2,1,0:T(8,128)(2,1)}), bf16[4,160,256]{2,1,0:T(8,128)(2,1)S(1)}, u32[]{:S(2)}, u32[]{:S(2)}) async-start(bf16[4,160,256]{2,1,0:T(8,128)(2,1)} %get-tuple-element.14), calls=%async_computation | async-start | bytes 655360 | tf_op jit(solution)/shard_map/all_to_all | solution.py:347
  8.8 38.7 %all-gather = bf16[3840,128]{1,0:T(8,128)(2,1)S(1)} all-gather(bf16[320,128]{1,0:T(8,128)(2,1)} %get-tuple-element.13), channel_id=2, replica_groups=mesh['z'=12,'y'=4,'core'=2,'head'=4,'scene'=2] {'z'}, dimensions={0}, use_global_device_ids=true | all-gather | bytes 1064960 | tf_op jit(solution)/shard_map/all_gather | solution.py:348
  47.5 0.0 all-to-all-done.q_ref
  47.5 1.9 %collective-permute-start = (bf16[12,320,128]{2,1,0:T(8,128)(2,1)S(1)}, bf16[12,320,128]{2,1,0:T(8,128)(2,1)S(1)}, u32[]{:S(2)}, u32[]{:S(2)}) collective-permute-start(bf16[12,320,128]{2,1,0:T(8,128)(2,1)S(1)} %bitcast.11), channel_id=1, source_target_pairs={{0,8},{8,0},{1,9},{9,1},{2,10},{10,2},{3,11},{11,3},{4,12},{12,4},... | collective-permute-start | bytes 2949128 | tf_op jit(solution)/shard_map/ppermute | solution.py:323
  49.4 3.3 %attend_own_core.1.sum_ref = f32[2,640,128]{2,1,0:T(8,128)S(1)} custom-call(bf16[12,320,128]{2,1,0:T(8,128)(2,1)S(1)} %bitcast.12, bf16[4,160,256]{2,1,0:T(8,128)(2,1)S(1)} %all-to-all-done.q_ref), custom_call_target="tpu_custom_call" | custom-call | flops 1258291200 | bytes 327680 | tf_op jit(solution)/shard_map/attend_own_core/pallas_call | solution.py:166
  52.7 0.0 collective-permute-done.kv_ref
  52.7 6.1 %attend_other_core.1 = bf16[1728,128]{1,0:T(8,128)(2,1)} custom-call(bf16[12,320,128]{2,1,0:T(8,128)(2,1)S(1)} %collective-permute-done.kv_ref, bf16[4,160,256]{2,1,0:T(8,128)(2,1)S(1)} %all-to-all-done.q_ref, f32[2,640,128]{2,1,0:T(8,128)S(1)} %attend_own_core.1.sum_ref), custom_call_target="tpu_custom_call" | custom-call | flops 1258291200 | bytes 327680 | tf_op jit(solution)/shard_map/attend_other_core/pallas_call | solution.py:183
  58.8 0.0 copy-start
  58.9 0.0 copy-start.2
  58.9 9.6 %all-to-all-start.1 = ((bf16[96,9,2,128]{3,2,1,0:T(2,128)(2,1)}), bf16[96,9,2,128]{3,2,1,0:T(2,128)(2,1)S(1)}, u32[]{:S(2)}, u32[]{:S(2)}) async-start(bf16[96,9,2,128]{3,2,1,0:T(2,128)(2,1)} %bitcast.3), calls=%async_computation.1 | async-start | bytes 884736 | tf_op jit(solution)/shard_map/all_to_all | solution.py:355
  68.4 3.4 %collective-permute-start.1 = (bf16[128,1024]{1,0:T(8,128)(2,1)}, bf16[128,1024]{1,0:T(8,128)(2,1)S(1)}, u32[]{:S(2)}, u32[]{:S(2)}) collective-permute-start(bf16[128,1024]{1,0:T(8,128)(2,1)} %refs_0_), channel_id=1, source_target_pairs={{0,2},{2,0},{4,6},{6,4},{1,3},{3,1},{5,7},{7,5},{8,10},{10,8},{12,... | collective-permute-start | bytes 786440 | tf_op jit(solution)/shard_map/ppermute | solution.py:323
  71.8 4.6 %collective-permute-start.2 = (bf16[128,1024]{1,0:T(8,128)(2,1)}, bf16[128,1024]{1,0:T(8,128)(2,1)S(1)}, u32[]{:S(2)}, u32[]{:S(2)}) collective-permute-start(bf16[128,1024]{1,0:T(8,128)(2,1)} %refs_0_), channel_id=1, source_target_pairs={{0,4},{2,6},{4,0},{6,2},{1,5},{3,7},{5,1},{7,3},{8,12},{10,14},{12... | collective-permute-start | bytes 786440 | tf_op jit(solution)/shard_map/ppermute | solution.py:323
  76.5 2.4 %collective-permute-start.3 = (bf16[128,1024]{1,0:T(8,128)(2,1)}, bf16[128,1024]{1,0:T(8,128)(2,1)S(1)}, u32[]{:S(2)}, u32[]{:S(2)}) collective-permute-start(bf16[128,1024]{1,0:T(8,128)(2,1)} %refs_0_), channel_id=1, source_target_pairs={{0,6},{2,4},{4,2},{6,0},{1,7},{3,5},{5,3},{7,1},{8,14},{10,12},{12... | collective-permute-start | bytes 786440 | tf_op jit(solution)/shard_map/ppermute | solution.py:323
  78.9 0.8 collective-permute-done.1.refs_0_.refs_1_
  79.7 7.1 %collective-permute-done.2.refs_1_.refs_2_ = bf16[128,1024]{1,0:T(8,128)(2,1)S(1)} collective-permute-done((bf16[128,1024]{1,0:T(8,128)(2,1)}, bf16[128,1024]{1,0:T(8,128)(2,1)S(1)}, u32[]{:S(2)}, u32[]{:S(2)}) %collective-permute-start.2) | collective-permute-done | bytes 262176 | tf_op jit(solution)/shard_map/ppermute | solution.py:323
  86.8 5.5 %collective-permute-done.3.refs_2_.refs_3_ = bf16[128,1024]{1,0:T(8,128)(2,1)S(1)} collective-permute-done((bf16[128,1024]{1,0:T(8,128)(2,1)}, bf16[128,1024]{1,0:T(8,128)(2,1)S(1)}, u32[]{:S(2)}, u32[]{:S(2)}) %collective-permute-start.3) | collective-permute-done | bytes 262176 | tf_op jit(solution)/shard_map/ppermute | solution.py:323
  92.3 0.0 all-to-all-done.1
  92.3 1.0 join_splat.1
  93.3 0.0 copy-start.1
  93.3 0.7 copy-done.1
  94.0 3.4 %all-to-all-start.2 = ((bf16[4,256,128]{2,1,0:T(8,128)(2,1)}), bf16[4,256,128]{2,1,0:T(8,128)(2,1)S(1)}, u32[]{:S(2)}, u32[]{:S(2)}) async-start(bf16[4,256,128]{2,1,0:T(8,128)(2,1)} %copy-done.1), calls=%async_computation.2 | async-start | bytes 524288 | tf_op jit(solution)/shard_map/all_to_all | solution.py:357
  97.5 7.8 %all-to-all-done.2.refs_4_ = bf16[4,256,128]{2,1,0:T(8,128)(2,1)S(1)} async-done(((bf16[4,256,128]{2,1,0:T(8,128)(2,1)}), bf16[4,256,128]{2,1,0:T(8,128)(2,1)S(1)}, u32[]{:S(2)}, u32[]{:S(2)}) %all-to-all-start.2) | async-done | bytes 262176 | tf_op jit(solution)/shard_map/all_to_all | solution.py:357
  105.2 0.0 copy-done
  105.2 0.0 copy-done.2
  105.2 4.1 %project_mlp.1 = (f32[64,1024]{1,0:T(8,128)S(1)}, bf16[256,1024]{1,0:T(8,128)(2,1)S(1)}) custom-call(s32[1]{0:T(128)} %bitcast.own_ref, bf16[128,1024]{1,0:T(8,128)(2,1)} %refs_0_, bf16[128,1024]{1,0:T(8,128)(2,1)S(1)} %collective-permute-done.1.refs_0_.refs_1_, bf16[128,1024]{1,0:T(8,128)(2,1)S(1)} %collective-permute-done.2.refs_1_.refs_2_, ...), custom_call_target="tpu_custom_call" | custom-call | tf_op jit(solution)/shard_map/project_mlp/pallas_call | solution.py:295
  109.3 12.2 %all_to_all.20 = bf16[4,64,1024]{2,1,0:T(8,128)(2,1)S(1)} all-to-all(bf16[4,64,1024]{2,1,0:T(8,128)(2,1)S(1)} %bitcast.13), channel_id=1, replica_groups=mesh['z'=12,'y'=4,'core'=2,'head'=4,'scene'=2] {'head'}, dimensions={0} | all-to-all | bytes 1048576 | tf_op jit(solution)/shard_map/all_to_all | solution.py:362
  121.5 0.1 convert_reduce_fusion
  121.5 0.7 fusion
Async XLA Ops:
  1.8 45.6 %all-to-all-start = ((bf16[4,160,256]{2,1,0:T(8,128)(2,1)}), bf16[4,160,256]{2,1,0:T(8,128)(2,1)S(1)}, u32[]{:S(2)}, u32[]{:S(2)}) async-start(bf16[4,160,256]{2,1,0:T(8,128)(2,1)} %get-tuple-element.14), calls=%async_computation | async-start | bytes 655360 | tf_op jit(solution)/shard_map/all_to_all | solution.py:347
  47.5 5.3 %collective-permute-start = (bf16[12,320,128]{2,1,0:T(8,128)(2,1)S(1)}, bf16[12,320,128]{2,1,0:T(8,128)(2,1)S(1)}, u32[]{:S(2)}, u32[]{:S(2)}) collective-permute-start(bf16[12,320,128]{2,1,0:T(8,128)(2,1)S(1)} %bitcast.11), channel_id=1, source_target_pairs={{0,8},{8,0},{1,9},{9,1},{2,10},{10,2},{3,11},{11,3},{4,12},{12,4},... | collective-permute-start | bytes 2949128 | tf_op jit(solution)/shard_map/ppermute | solution.py:323
  58.8 46.4 %copy-start = (bf16[1024,1024]{1,0:T(8,128)(2,1)S(1)}, bf16[1024,1024]{1,0:T(8,128)(2,1)}, u32[]{:S(2)}) copy-start(bf16[1024,1024]{1,0:T(8,128)(2,1)} %refs_7_.1) | copy-start | bytes 6291460
  58.9 46.4 %copy-start.2 = (f32[1024]{0:T(1024)S(1)}, f32[1024]{0:T(1024)}, u32[]{:S(2)}) copy-start(f32[1024]{0:T(1024)} %param.18) | copy-start | bytes 12292
  58.9 33.5 %all-to-all-start.1 = ((bf16[96,9,2,128]{3,2,1,0:T(2,128)(2,1)}), bf16[96,9,2,128]{3,2,1,0:T(2,128)(2,1)S(1)}, u32[]{:S(2)}, u32[]{:S(2)}) async-start(bf16[96,9,2,128]{3,2,1,0:T(2,128)(2,1)} %bitcast.3), calls=%async_computation.1 | async-start | bytes 884736 | tf_op jit(solution)/shard_map/all_to_all | solution.py:355
  68.4 11.3 %collective-permute-start.1 = (bf16[128,1024]{1,0:T(8,128)(2,1)}, bf16[128,1024]{1,0:T(8,128)(2,1)S(1)}, u32[]{:S(2)}, u32[]{:S(2)}) collective-permute-start(bf16[128,1024]{1,0:T(8,128)(2,1)} %refs_0_), channel_id=1, source_target_pairs={{0,2},{2,0},{4,6},{6,4},{1,3},{3,1},{5,7},{7,5},{8,10},{10,8},{12,... | collective-permute-start | bytes 786440 | tf_op jit(solution)/shard_map/ppermute | solution.py:323
  71.8 15.0 %collective-permute-start.2 = (bf16[128,1024]{1,0:T(8,128)(2,1)}, bf16[128,1024]{1,0:T(8,128)(2,1)S(1)}, u32[]{:S(2)}, u32[]{:S(2)}) collective-permute-start(bf16[128,1024]{1,0:T(8,128)(2,1)} %refs_0_), channel_id=1, source_target_pairs={{0,4},{2,6},{4,0},{6,2},{1,5},{3,7},{5,1},{7,3},{8,12},{10,14},{12... | collective-permute-start | bytes 786440 | tf_op jit(solution)/shard_map/ppermute | solution.py:323
  76.5 15.8 %collective-permute-start.3 = (bf16[128,1024]{1,0:T(8,128)(2,1)}, bf16[128,1024]{1,0:T(8,128)(2,1)S(1)}, u32[]{:S(2)}, u32[]{:S(2)}) collective-permute-start(bf16[128,1024]{1,0:T(8,128)(2,1)} %refs_0_), channel_id=1, source_target_pairs={{0,6},{2,4},{4,2},{6,0},{1,7},{3,5},{5,3},{7,1},{8,14},{10,12},{12... | collective-permute-start | bytes 786440 | tf_op jit(solution)/shard_map/ppermute | solution.py:323
  93.3 0.7 copy-start.1
  94.0 11.2 %all-to-all-start.2 = ((bf16[4,256,128]{2,1,0:T(8,128)(2,1)}), bf16[4,256,128]{2,1,0:T(8,128)(2,1)S(1)}, u32[]{:S(2)}, u32[]{:S(2)}) async-start(bf16[4,256,128]{2,1,0:T(8,128)(2,1)} %copy-done.1), calls=%async_computation.2 | async-start | bytes 524288 | tf_op jit(solution)/shard_map/all_to_all | solution.py:357

commit v9 on v8

--- a/solution.py
+++ b/solution.py
@@ -200,7 +200,7 @@
     )(kv, q_all, sums)
 
 
-def splat_kernel(groups, x_ref, *refs):
+def splat_kernel(groups, _, x_ref, *refs):
     out_ref, x_s, y_s, r_s = refs[-4:]
     cells = out_ref.shape[1]
     sources = x_ref.shape[0] // PIECE
@@ -239,12 +239,13 @@
         out_ref[copy] = features
 
 
-def splat(received, early, cells, groups, copies):
+def splat(own, received, early, cells, groups, copies):
     rows = received.shape[0]
     return pl.pallas_call(
         functools.partial(splat_kernel, groups),
         out_shape=jax.ShapeDtypeStruct((copies, cells, LANES), bf16),
-        in_specs=[pl.BlockSpec(memory_space=pltpu.VMEM)] + [pl.BlockSpec(memory_space=pl.ANY)] * len(early),
+        in_specs=[pl.BlockSpec(memory_space=pltpu.SMEM), pl.BlockSpec(memory_space=pltpu.VMEM)]
+        + [pl.BlockSpec(memory_space=pl.ANY)] * len(early),
         out_specs=pl.BlockSpec(memory_space=pltpu.VMEM),
         scratch_shapes=[
             pltpu.VMEM((rows, LANES), f32),
@@ -253,7 +254,7 @@
         ],
         compiler_params=pltpu.CompilerParams(vmem_limit_bytes=12 * MIB),
         name="join_splat",
-    )(received, *early)
+    )(own, received, *early)
 
 
 def mlp_kernel(own_ref, *refs):
@@ -353,9 +354,9 @@
     packed, out_weight = lax.optimization_barrier((packed, out_weight))
     weights = tuple(swap(out_weight, "head", k) for k in range(heads - 1, 0, -1))[::-1]
     received = lax.all_to_all(packed.reshape(tiles, PIECE // 2, 2, LANES), ("z", "y", "core"), 0, 0)
-    features = splat(received.reshape(tiles * PIECE, LANES), weights, cells, groups, heads)
+    own = lax.axis_index("head").astype(jnp.int32).reshape(1)
+    features = splat(own, received.reshape(tiles * PIECE, LANES), weights, cells, groups, heads)
     features = lax.all_to_all(features, "head", 0, 0)
-    own = lax.axis_index("head").astype(jnp.int32).reshape(1)
     bev_rows, mixed = mlp(
         own, (out_weight,) + weights, features, bev_base[0], norm_gain[None, :], up_weight, down_weight
     )

time: 123 us -> 122 us (level)
  blocking collectives: 50.8 us -> 61.3 us
  waiting for transfers between devices: 21.2 us -> 13.4 us
  starting transfers between devices: 32.3 us -> 28.9 us
    all_to_all x0 -> x1, blocking collectives: none -> 10 us  [body(): features = lax.all_to_all(features, 'head', 0, 0)]
    all_to_all x1 -> x0, waiting for transfers between devices: 7.78 us -> none  [body(): features = lax.all_to_all(features, 'head', 0, 0)]
    all_to_all x1 -> x0, starting transfers between devices: 3.4 us -> none  [body(): features = lax.all_to_all(features, 'head', 0, 0)]
  transfers between devices with their start and end apart: 7 -> 6, of which waited for: 4 -> 3; matrix products, arithmetic and copies ran while one was open for 0% -> 0% of each run, Pallas kernels for 3% -> 3%
where the time goes in v9:
time: 122 us; the launch traced here: 121 us
  blocking collectives  61.3 us (50%)
  starting transfers between devices  28.9 us (24%)
  Pallas kernels  16.3 us (13%)
  waiting for transfers between devices  13.4 us (11%)
    all_gather x1, blocking collectives, body(): own_kv = lax.all_gather(kv, 'z')  38.7 us
    ppermute x4, waiting for transfers between devices, swap(): lax.ppermute(x, axis, [(i, i ^ bit) for i in range(lax.axis_size(axis))])  13.4 us
    all_to_all x1, blocking collectives, body(): lax.all_to_all(mixed.reshape(heads, cells // heads, mixed.shape[1]), 'hea...  12.6 us
    ppermute x4, starting transfers between devices, swap(): lax.ppermute(x, axis, [(i, i ^ bit) for i in range(lax.axis_size(axis))])  12.3 us
    all_to_all x1, blocking collectives, body(): features = lax.all_to_all(features, 'head', 0, 0)  10 us
    all_to_all x1, starting transfers between devices, body(): lax.all_to_all(packed.reshape(tiles, PIECE // 2, 2, LANES), ('z', 'y', 'c...  9.57 us
    all_to_all x1, starting transfers between devices, body(): q_all = lax.all_to_all(q_copies, 'y', 0, 0)  6.97 us
    pallas_call x1, Pallas kernels, attend_second(): pl.pallas_call(second_kernel, out_shape=jax.ShapeDtypeStruct((tiles * PIE...  6.11 us
  transfers between devices with their start and end apart: 6, of which 3 were waited for; matrix products, arithmetic and copies ran while one was open for 0% of the time, Pallas kernels for 3%

profile of v9, /device:TPU:56, one launch (start us, length us, event | category | flops | bytes accessed | tf_op | source)
XLA Modules:
  0.0 120.8 jit_solution(1062780681541723253)
XLA Ops:
  0.0 1.8 %prologue.1 = (bf16[4,160,256]{2,1,0:T(8,128)(2,1)}, bf16[320,128]{1,0:T(8,128)(2,1)}) custom-call(bf16[1,160,128]{2,1,0:T(8,128)(2,1)} %q_ref.1, bf16[1,160,128]{2,1,0:T(8,128)(2,1)} %k_ref.1, bf16[1,160,128]{2,1,0:T(8,128)(2,1)} %v_ref.1, s32[1,160]{1,0:T(1,128)} %bitcast.16, s32[1,160]{1,0:T(1,128)} %cell_ref.1, f32[1,160]{1,0:T(1,128)} %splat_ref.1), custom_call_target="tpu_custom_call" | custom-call | tf_op jit(solution)/shard_map/prologue/pallas_call | solution.py:58
  1.8 7.0 %all-to-all-start = ((bf16[4,160,256]{2,1,0:T(8,128)(2,1)}), bf16[4,160,256]{2,1,0:T(8,128)(2,1)S(1)}, u32[]{:S(2)}, u32[]{:S(2)}) async-start(bf16[4,160,256]{2,1,0:T(8,128)(2,1)} %get-tuple-element.14), calls=%async_computation | async-start | bytes 655360 | tf_op jit(solution)/shard_map/all_to_all | solution.py:348
  8.8 38.7 %all-gather = bf16[3840,128]{1,0:T(8,128)(2,1)S(1)} all-gather(bf16[320,128]{1,0:T(8,128)(2,1)} %get-tuple-element.13), channel_id=2, replica_groups=mesh['z'=12,'y'=4,'core'=2,'head'=4,'scene'=2] {'z'}, dimensions={0}, use_global_device_ids=true | all-gather | bytes 1064960 | tf_op jit(solution)/shard_map/all_gather | solution.py:349
  47.5 0.0 all-to-all-done.q_ref
  47.5 1.9 %collective-permute-start = (bf16[12,320,128]{2,1,0:T(8,128)(2,1)S(1)}, bf16[12,320,128]{2,1,0:T(8,128)(2,1)S(1)}, u32[]{:S(2)}, u32[]{:S(2)}) collective-permute-start(bf16[12,320,128]{2,1,0:T(8,128)(2,1)S(1)} %bitcast.11), channel_id=1, source_target_pairs={{0,8},{8,0},{1,9},{9,1},{2,10},{10,2},{3,11},{11,3},{4,12},{12,4},... | collective-permute-start | bytes 2949128 | tf_op jit(solution)/shard_map/ppermute | solution.py:324
  49.4 3.3 %attend_own_core.1.sum_ref = f32[2,640,128]{2,1,0:T(8,128)S(1)} custom-call(bf16[12,320,128]{2,1,0:T(8,128)(2,1)S(1)} %bitcast.12, bf16[4,160,256]{2,1,0:T(8,128)(2,1)S(1)} %all-to-all-done.q_ref), custom_call_target="tpu_custom_call" | custom-call | flops 1258291200 | bytes 327680 | tf_op jit(solution)/shard_map/attend_own_core/pallas_call | solution.py:166
  52.7 0.0 collective-permute-done.kv_ref
  52.7 6.1 %attend_other_core.1 = bf16[1728,128]{1,0:T(8,128)(2,1)} custom-call(bf16[12,320,128]{2,1,0:T(8,128)(2,1)S(1)} %collective-permute-done.kv_ref, bf16[4,160,256]{2,1,0:T(8,128)(2,1)S(1)} %all-to-all-done.q_ref, f32[2,640,128]{2,1,0:T(8,128)S(1)} %attend_own_core.1.sum_ref), custom_call_target="tpu_custom_call" | custom-call | flops 1258291200 | bytes 327680 | tf_op jit(solution)/shard_map/attend_other_core/pallas_call | solution.py:183
  58.8 0.0 copy-start
  58.8 0.0 copy-start.1
  58.8 9.6 %all-to-all-start.1 = ((bf16[96,9,2,128]{3,2,1,0:T(2,128)(2,1)}), bf16[96,9,2,128]{3,2,1,0:T(2,128)(2,1)S(1)}, u32[]{:S(2)}, u32[]{:S(2)}) async-start(bf16[96,9,2,128]{3,2,1,0:T(2,128)(2,1)} %bitcast.3), calls=%async_computation.1 | async-start | bytes 884736 | tf_op jit(solution)/shard_map/all_to_all | solution.py:356
  68.4 3.4 %collective-permute-start.1 = (bf16[128,1024]{1,0:T(8,128)(2,1)}, bf16[128,1024]{1,0:T(8,128)(2,1)S(1)}, u32[]{:S(2)}, u32[]{:S(2)}) collective-permute-start(bf16[128,1024]{1,0:T(8,128)(2,1)} %refs_0_), channel_id=1, source_target_pairs={{0,2},{2,0},{4,6},{6,4},{1,3},{3,1},{5,7},{7,5},{8,10},{10,8},{12,... | collective-permute-start | bytes 786440 | tf_op jit(solution)/shard_map/ppermute | solution.py:324
  71.8 4.6 %collective-permute-start.2 = (bf16[128,1024]{1,0:T(8,128)(2,1)}, bf16[128,1024]{1,0:T(8,128)(2,1)S(1)}, u32[]{:S(2)}, u32[]{:S(2)}) collective-permute-start(bf16[128,1024]{1,0:T(8,128)(2,1)} %refs_0_), channel_id=1, source_target_pairs={{0,4},{2,6},{4,0},{6,2},{1,5},{3,7},{5,1},{7,3},{8,12},{10,14},{12... | collective-permute-start | bytes 786440 | tf_op jit(solution)/shard_map/ppermute | solution.py:324
  76.5 2.4 %collective-permute-start.3 = (bf16[128,1024]{1,0:T(8,128)(2,1)}, bf16[128,1024]{1,0:T(8,128)(2,1)S(1)}, u32[]{:S(2)}, u32[]{:S(2)}) collective-permute-start(bf16[128,1024]{1,0:T(8,128)(2,1)} %refs_0_), channel_id=1, source_target_pairs={{0,6},{2,4},{4,2},{6,0},{1,7},{3,5},{5,3},{7,1},{8,14},{10,12},{12... | collective-permute-start | bytes 786440 | tf_op jit(solution)/shard_map/ppermute | solution.py:324
  78.9 0.8 collective-permute-done.1.refs_0_.refs_1_
  79.7 7.1 %collective-permute-done.2.refs_1_.refs_2_ = bf16[128,1024]{1,0:T(8,128)(2,1)S(1)} collective-permute-done((bf16[128,1024]{1,0:T(8,128)(2,1)}, bf16[128,1024]{1,0:T(8,128)(2,1)S(1)}, u32[]{:S(2)}, u32[]{:S(2)}) %collective-permute-start.2) | collective-permute-done | bytes 262176 | tf_op jit(solution)/shard_map/ppermute | solution.py:324
  86.8 5.5 %collective-permute-done.3.refs_2_.refs_3_ = bf16[128,1024]{1,0:T(8,128)(2,1)S(1)} collective-permute-done((bf16[128,1024]{1,0:T(8,128)(2,1)}, bf16[128,1024]{1,0:T(8,128)(2,1)S(1)}, u32[]{:S(2)}, u32[]{:S(2)}) %collective-permute-start.3) | collective-permute-done | bytes 262176 | tf_op jit(solution)/shard_map/ppermute | solution.py:324
  92.3 0.0 all-to-all-done.1
  92.3 1.0 join_splat.1
  93.3 10.0 %all_to_all.20.refs_4_ = bf16[4,256,128]{2,1,0:T(8,128)(2,1)S(1)} all-to-all(bf16[4,256,128]{2,1,0:T(8,128)(2,1)S(1)} %join_splat.1), channel_id=1, replica_groups=mesh['z'=12,'y'=4,'core'=2,'head'=4,'scene'=2] {'head'}, dimensions={0} | all-to-all | bytes 524288 | tf_op jit(solution)/shard_map/all_to_all | solution.py:359
  103.3 0.0 copy-done
  103.4 0.0 copy-done.1
  103.4 4.0 %project_mlp.1 = (f32[64,1024]{1,0:T(8,128)S(1)}, bf16[256,1024]{1,0:T(8,128)(2,1)S(1)}) custom-call(s32[1]{0:T(128)} %bitcast._.own_ref, bf16[128,1024]{1,0:T(8,128)(2,1)} %refs_0_, bf16[128,1024]{1,0:T(8,128)(2,1)S(1)} %collective-permute-done.1.refs_0_.refs_1_, bf16[128,1024]{1,0:T(8,128)(2,1)S(1)} %collective-permute-done.2.refs_1_.refs_2_, ...), custom_call_target="tpu_custom_call" | custom-call | tf_op jit(solution)/shard_map/project_mlp/pallas_call | solution.py:296
  107.4 12.6 %all_to_all.21 = bf16[4,64,1024]{2,1,0:T(8,128)(2,1)S(1)} all-to-all(bf16[4,64,1024]{2,1,0:T(8,128)(2,1)S(1)} %bitcast.13), channel_id=1, replica_groups=mesh['z'=12,'y'=4,'core'=2,'head'=4,'scene'=2] {'head'}, dimensions={0} | all-to-all | bytes 1048576 | tf_op jit(solution)/shard_map/all_to_all | solution.py:363
  120.0 0.1 convert_reduce_fusion
  120.1 0.7 fusion
Async XLA Ops:
  1.8 45.6 %all-to-all-start = ((bf16[4,160,256]{2,1,0:T(8,128)(2,1)}), bf16[4,160,256]{2,1,0:T(8,128)(2,1)S(1)}, u32[]{:S(2)}, u32[]{:S(2)}) async-start(bf16[4,160,256]{2,1,0:T(8,128)(2,1)} %get-tuple-element.14), calls=%async_computation | async-start | bytes 655360 | tf_op jit(solution)/shard_map/all_to_all | solution.py:348
  47.5 5.3 %collective-permute-start = (bf16[12,320,128]{2,1,0:T(8,128)(2,1)S(1)}, bf16[12,320,128]{2,1,0:T(8,128)(2,1)S(1)}, u32[]{:S(2)}, u32[]{:S(2)}) collective-permute-start(bf16[12,320,128]{2,1,0:T(8,128)(2,1)S(1)} %bitcast.11), channel_id=1, source_target_pairs={{0,8},{8,0},{1,9},{9,1},{2,10},{10,2},{3,11},{11,3},{4,12},{12,4},... | collective-permute-start | bytes 2949128 | tf_op jit(solution)/shard_map/ppermute | solution.py:324
  58.8 44.5 %copy-start = (bf16[1024,1024]{1,0:T(8,128)(2,1)S(1)}, bf16[1024,1024]{1,0:T(8,128)(2,1)}, u32[]{:S(2)}) copy-start(bf16[1024,1024]{1,0:T(8,128)(2,1)} %refs_7_.1) | copy-start | bytes 6291460
  58.8 44.5 %copy-start.1 = (f32[1024]{0:T(1024)S(1)}, f32[1024]{0:T(1024)}, u32[]{:S(2)}) copy-start(f32[1024]{0:T(1024)} %param.18) | copy-start | bytes 12292
  58.8 33.5 %all-to-all-start.1 = ((bf16[96,9,2,128]{3,2,1,0:T(2,128)(2,1)}), bf16[96,9,2,128]{3,2,1,0:T(2,128)(2,1)S(1)}, u32[]{:S(2)}, u32[]{:S(2)}) async-start(bf16[96,9,2,128]{3,2,1,0:T(2,128)(2,1)} %bitcast.3), calls=%async_computation.1 | async-start | bytes 884736 | tf_op jit(solution)/shard_map/all_to_all | solution.py:356
  68.4 11.3 %collective-permute-start.1 = (bf16[128,1024]{1,0:T(8,128)(2,1)}, bf16[128,1024]{1,0:T(8,128)(2,1)S(1)}, u32[]{:S(2)}, u32[]{:S(2)}) collective-permute-start(bf16[128,1024]{1,0:T(8,128)(2,1)} %refs_0_), channel_id=1, source_target_pairs={{0,2},{2,0},{4,6},{6,4},{1,3},{3,1},{5,7},{7,5},{8,10},{10,8},{12,... | collective-permute-start | bytes 786440 | tf_op jit(solution)/shard_map/ppermute | solution.py:324
  71.8 15.0 %collective-permute-start.2 = (bf16[128,1024]{1,0:T(8,128)(2,1)}, bf16[128,1024]{1,0:T(8,128)(2,1)S(1)}, u32[]{:S(2)}, u32[]{:S(2)}) collective-permute-start(bf16[128,1024]{1,0:T(8,128)(2,1)} %refs_0_), channel_id=1, source_target_pairs={{0,4},{2,6},{4,0},{6,2},{1,5},{3,7},{5,1},{7,3},{8,12},{10,14},{12... | collective-permute-start | bytes 786440 | tf_op jit(solution)/shard_map/ppermute | solution.py:324
  76.5 15.8 %collective-permute-start.3 = (bf16[128,1024]{1,0:T(8,128)(2,1)}, bf16[128,1024]{1,0:T(8,128)(2,1)S(1)}, u32[]{:S(2)}, u32[]{:S(2)}) collective-permute-start(bf16[128,1024]{1,0:T(8,128)(2,1)} %refs_0_), channel_id=1, source_target_pairs={{0,6},{2,4},{4,2},{6,0},{1,7},{3,5},{5,3},{7,1},{8,14},{10,12},{12... | collective-permute-start | bytes 786440 | tf_op jit(solution)/shard_map/ppermute | solution.py:324

commit v10 on v9

--- a/solution.py
+++ b/solution.py
@@ -258,21 +258,23 @@
 
 
 def mlp_kernel(own_ref, *refs):
-    weights, (f_ref, base_hbm, gain_ref, up_ref, down_hbm) = refs[:4], refs[4:9]
-    bev_ref, mix_ref, bev_s, base_s, down_s, sems = refs[9:]
-    base_copy = pltpu.make_async_copy(base_hbm, base_s, sems.at[0])
+    weights, (f_ref, base_ref, gain_ref, up_ref, down_hbm) = refs[:4], refs[4:9]
+    bev_ref, mix_ref, bev_s, own_s, down_s, sems = refs[9:]
+    own_copy = pltpu.make_async_copy(weights[0], own_s, sems.at[0])
     down_copy = pltpu.make_async_copy(down_hbm, down_s, sems.at[1])
-    base_copy.start()
+    own_copy.start()
     down_copy.start()
     share = bev_ref.shape[0]
     own = own_ref[0]
+    rows = [own_s] + list(weights[1:])
     projected = None
-    for k in range(0, len(weights), 2):
+    for k in range(len(rows) - 2, -1, -2):
+        if k == 0:
+            own_copy.wait()
         features = jnp.concatenate([f_ref[own ^ k], f_ref[own ^ (k + 1)]], axis=1)
-        term = dot(features, jnp.concatenate([weights[k][...], weights[k + 1][...]], axis=0))
+        term = dot(features, jnp.concatenate([rows[k][...], rows[k + 1][...]], axis=0))
         projected = term if projected is None else projected + term
-    base_copy.wait()
-    bev = base_s[...].astype(f32) + projected
+    bev = base_ref[...].astype(f32) + projected
     bev_s[...] = bev
     mean_square = jnp.mean(bev * bev, axis=1, keepdims=True)
     normed = (bev * lax.rsqrt(mean_square + 1e-06) * gain_ref[...]).astype(bf16)
@@ -299,11 +301,11 @@
             jax.ShapeDtypeStruct((cells // heads, width), f32),
             jax.ShapeDtypeStruct((cells, width), bf16),
         ),
-        in_specs=[pl.BlockSpec(memory_space=pltpu.SMEM)] + [vmem] * 5 + [hbm, vmem, vmem, hbm],
+        in_specs=[pl.BlockSpec(memory_space=pltpu.SMEM)] + [hbm] + [vmem] * 7 + [hbm],
         out_specs=(vmem, vmem),
         scratch_shapes=[
             pltpu.VMEM((cells, width), f32),
-            pltpu.VMEM((cells, width), bf16),
+            pltpu.VMEM(weights[0].shape, bf16),
             pltpu.VMEM(down.shape, bf16),
             pltpu.SemaphoreType.DMA((2,)),
         ],
@@ -311,9 +313,10 @@
         name="project_mlp",
     )(
         own,
-        *weights,
+        pltpu.with_memory_space_constraint(weights[0], pltpu.HBM),
+        *weights[1:],
         features,
-        pltpu.with_memory_space_constraint(base, pltpu.HBM),
+        base,
         gain,
         up,
         pltpu.with_memory_space_constraint(down, pltpu.HBM),

time: 122 us -> 121 us (level)
  no operation moved by 1% of the time
where the time goes in v10:
time: 121 us; the launch traced here: 120 us
  blocking collectives  61.3 us (51%)
  starting transfers between devices  28.9 us (24%)
  Pallas kernels  15.3 us (13%)
  waiting for transfers between devices  13.4 us (11%)
    all_gather x1, blocking collectives, body(): own_kv = lax.all_gather(kv, 'z')  38.7 us
    ppermute x4, waiting for transfers between devices, swap(): lax.ppermute(x, axis, [(i, i ^ bit) for i in range(lax.axis_size(axis))])  13.4 us
    all_to_all x1, blocking collectives, body(): lax.all_to_all(mixed.reshape(heads, cells // heads, mixed.shape[1]), 'hea...  12.6 us
    ppermute x4, starting transfers between devices, swap(): lax.ppermute(x, axis, [(i, i ^ bit) for i in range(lax.axis_size(axis))])  12.3 us
    all_to_all x1, blocking collectives, body(): features = lax.all_to_all(features, 'head', 0, 0)  10 us
    all_to_all x1, starting transfers between devices, body(): lax.all_to_all(packed.reshape(tiles, PIECE // 2, 2, LANES), ('z', 'y', 'c...  9.58 us
    all_to_all x1, starting transfers between devices, body(): q_all = lax.all_to_all(q_copies, 'y', 0, 0)  6.97 us
    pallas_call x1, Pallas kernels, attend_second(): pl.pallas_call(second_kernel, out_shape=jax.ShapeDtypeStruct((tiles * PIE...  6.11 us
  transfers between devices with their start and end apart: 6, of which 3 were waited for; matrix products, arithmetic and copies ran while one was open for 0% of the time, Pallas kernels for 3%

profile of v10, /device:TPU:56, one launch (start us, length us, event | category | flops | bytes accessed | tf_op | source)
XLA Modules:
  0.0 119.8 jit_solution(2078762911353684637)
XLA Ops:
  0.0 1.8 %prologue.1 = (bf16[4,160,256]{2,1,0:T(8,128)(2,1)}, bf16[320,128]{1,0:T(8,128)(2,1)}) custom-call(bf16[1,160,128]{2,1,0:T(8,128)(2,1)} %q_ref.1, bf16[1,160,128]{2,1,0:T(8,128)(2,1)} %k_ref.1, bf16[1,160,128]{2,1,0:T(8,128)(2,1)} %v_ref.1, s32[1,160]{1,0:T(1,128)} %bitcast.16, s32[1,160]{1,0:T(1,128)} %cell_ref.1, f32[1,160]{1,0:T(1,128)} %splat_ref.1), custom_call_target="tpu_custom_call" | custom-call | tf_op jit(solution)/shard_map/prologue/pallas_call | solution.py:58
  1.8 7.0 %all-to-all-start = ((bf16[4,160,256]{2,1,0:T(8,128)(2,1)}), bf16[4,160,256]{2,1,0:T(8,128)(2,1)S(1)}, u32[]{:S(2)}, u32[]{:S(2)}) async-start(bf16[4,160,256]{2,1,0:T(8,128)(2,1)} %get-tuple-element.14), calls=%async_computation | async-start | bytes 655360 | tf_op jit(solution)/shard_map/all_to_all | solution.py:351
  8.8 38.7 %all-gather = bf16[3840,128]{1,0:T(8,128)(2,1)S(1)} all-gather(bf16[320,128]{1,0:T(8,128)(2,1)} %get-tuple-element.13), channel_id=2, replica_groups=mesh['z'=12,'y'=4,'core'=2,'head'=4,'scene'=2] {'z'}, dimensions={0}, use_global_device_ids=true | all-gather | bytes 1064960 | tf_op jit(solution)/shard_map/all_gather | solution.py:352
  47.5 0.0 all-to-all-done.q_ref
  47.5 1.9 %collective-permute-start = (bf16[12,320,128]{2,1,0:T(8,128)(2,1)S(1)}, bf16[12,320,128]{2,1,0:T(8,128)(2,1)S(1)}, u32[]{:S(2)}, u32[]{:S(2)}) collective-permute-start(bf16[12,320,128]{2,1,0:T(8,128)(2,1)S(1)} %bitcast.11), channel_id=1, source_target_pairs={{0,8},{8,0},{1,9},{9,1},{2,10},{10,2},{3,11},{11,3},{4,12},{12,4},... | collective-permute-start | bytes 2949128 | tf_op jit(solution)/shard_map/ppermute | solution.py:327
  49.4 3.3 %attend_own_core.1.sum_ref = f32[2,640,128]{2,1,0:T(8,128)S(1)} custom-call(bf16[12,320,128]{2,1,0:T(8,128)(2,1)S(1)} %bitcast.12, bf16[4,160,256]{2,1,0:T(8,128)(2,1)S(1)} %all-to-all-done.q_ref), custom_call_target="tpu_custom_call" | custom-call | flops 1258291200 | bytes 327680 | tf_op jit(solution)/shard_map/attend_own_core/pallas_call | solution.py:166
  52.7 0.0 collective-permute-done.kv_ref
  52.7 6.1 %attend_other_core.1 = bf16[1728,128]{1,0:T(8,128)(2,1)} custom-call(bf16[12,320,128]{2,1,0:T(8,128)(2,1)S(1)} %collective-permute-done.kv_ref, bf16[4,160,256]{2,1,0:T(8,128)(2,1)S(1)} %all-to-all-done.q_ref, f32[2,640,128]{2,1,0:T(8,128)S(1)} %attend_own_core.1.sum_ref), custom_call_target="tpu_custom_call" | custom-call | flops 1258291200 | bytes 327680 | tf_op jit(solution)/shard_map/attend_other_core/pallas_call | solution.py:183
  58.8 0.0 copy-start
  58.8 0.0 copy-start.2
  58.8 9.6 %all-to-all-start.1 = ((bf16[96,9,2,128]{3,2,1,0:T(2,128)(2,1)}), bf16[96,9,2,128]{3,2,1,0:T(2,128)(2,1)S(1)}, u32[]{:S(2)}, u32[]{:S(2)}) async-start(bf16[96,9,2,128]{3,2,1,0:T(2,128)(2,1)} %bitcast.3), calls=%async_computation.1 | async-start | bytes 884736 | tf_op jit(solution)/shard_map/all_to_all | solution.py:359
  68.4 3.4 %collective-permute-start.1 = (bf16[128,1024]{1,0:T(8,128)(2,1)}, bf16[128,1024]{1,0:T(8,128)(2,1)S(1)}, u32[]{:S(2)}, u32[]{:S(2)}) collective-permute-start(bf16[128,1024]{1,0:T(8,128)(2,1)} %refs_0_), channel_id=1, source_target_pairs={{0,2},{2,0},{4,6},{6,4},{1,3},{3,1},{5,7},{7,5},{8,10},{10,8},{12,... | collective-permute-start | bytes 786440 | tf_op jit(solution)/shard_map/ppermute | solution.py:327
  71.8 4.6 %collective-permute-start.2 = (bf16[128,1024]{1,0:T(8,128)(2,1)}, bf16[128,1024]{1,0:T(8,128)(2,1)S(1)}, u32[]{:S(2)}, u32[]{:S(2)}) collective-permute-start(bf16[128,1024]{1,0:T(8,128)(2,1)} %refs_0_), channel_id=1, source_target_pairs={{0,4},{2,6},{4,0},{6,2},{1,5},{3,7},{5,1},{7,3},{8,12},{10,14},{12... | collective-permute-start | bytes 786440 | tf_op jit(solution)/shard_map/ppermute | solution.py:327
  76.5 2.4 %collective-permute-start.3 = (bf16[128,1024]{1,0:T(8,128)(2,1)}, bf16[128,1024]{1,0:T(8,128)(2,1)S(1)}, u32[]{:S(2)}, u32[]{:S(2)}) collective-permute-start(bf16[128,1024]{1,0:T(8,128)(2,1)} %refs_0_), channel_id=1, source_target_pairs={{0,6},{2,4},{4,2},{6,0},{1,7},{3,5},{5,3},{7,1},{8,14},{10,12},{12... | collective-permute-start | bytes 786440 | tf_op jit(solution)/shard_map/ppermute | solution.py:327
  78.9 0.8 collective-permute-done.1.refs_0_.refs_1_
  79.7 7.1 %collective-permute-done.2.refs_1_.refs_2_ = bf16[128,1024]{1,0:T(8,128)(2,1)S(1)} collective-permute-done((bf16[128,1024]{1,0:T(8,128)(2,1)}, bf16[128,1024]{1,0:T(8,128)(2,1)S(1)}, u32[]{:S(2)}, u32[]{:S(2)}) %collective-permute-start.2) | collective-permute-done | bytes 262176 | tf_op jit(solution)/shard_map/ppermute | solution.py:327
  86.8 5.5 %collective-permute-done.3.refs_2_.refs_3_ = bf16[128,1024]{1,0:T(8,128)(2,1)S(1)} collective-permute-done((bf16[128,1024]{1,0:T(8,128)(2,1)}, bf16[128,1024]{1,0:T(8,128)(2,1)S(1)}, u32[]{:S(2)}, u32[]{:S(2)}) %collective-permute-start.3) | collective-permute-done | bytes 262176 | tf_op jit(solution)/shard_map/ppermute | solution.py:327
  92.3 0.0 all-to-all-done.1
  92.3 0.0 copy-start.1
  92.3 1.0 join_splat.1
  93.3 10.0 %all_to_all.20.refs_4_ = bf16[4,256,128]{2,1,0:T(8,128)(2,1)S(1)} all-to-all(bf16[4,256,128]{2,1,0:T(8,128)(2,1)S(1)} %join_splat.1), channel_id=1, replica_groups=mesh['z'=12,'y'=4,'core'=2,'head'=4,'scene'=2] {'head'}, dimensions={0} | all-to-all | bytes 524288 | tf_op jit(solution)/shard_map/all_to_all | solution.py:362
  103.4 0.0 copy-done
  103.4 0.0 copy-done.2
  103.4 0.0 copy-done.1
  103.4 3.0 %project_mlp.1 = (f32[64,1024]{1,0:T(8,128)S(1)}, bf16[256,1024]{1,0:T(8,128)(2,1)S(1)}) custom-call(s32[1]{0:T(128)} %bitcast._.own_ref, bf16[128,1024]{1,0:T(8,128)(2,1)} %refs_0_, bf16[128,1024]{1,0:T(8,128)(2,1)S(1)} %collective-permute-done.1.refs_0_.refs_1_, bf16[128,1024]{1,0:T(8,128)(2,1)S(1)} %collective-permute-done.2.refs_1_.refs_2_, ...), custom_call_target="tpu_custom_call" | custom-call | tf_op jit(solution)/shard_map/project_mlp/pallas_call | solution.py:298
  106.4 12.6 %all_to_all.21 = bf16[4,64,1024]{2,1,0:T(8,128)(2,1)S(1)} all-to-all(bf16[4,64,1024]{2,1,0:T(8,128)(2,1)S(1)} %bitcast.13), channel_id=1, replica_groups=mesh['z'=12,'y'=4,'core'=2,'head'=4,'scene'=2] {'head'}, dimensions={0} | all-to-all | bytes 1048576 | tf_op jit(solution)/shard_map/all_to_all | solution.py:366
  119.0 0.1 convert_reduce_fusion
  119.1 0.7 fusion
Async XLA Ops:
  1.8 45.6 %all-to-all-start = ((bf16[4,160,256]{2,1,0:T(8,128)(2,1)}), bf16[4,160,256]{2,1,0:T(8,128)(2,1)S(1)}, u32[]{:S(2)}, u32[]{:S(2)}) async-start(bf16[4,160,256]{2,1,0:T(8,128)(2,1)} %get-tuple-element.14), calls=%async_computation | async-start | bytes 655360 | tf_op jit(solution)/shard_map/all_to_all | solution.py:351
  47.5 5.3 %collective-permute-start = (bf16[12,320,128]{2,1,0:T(8,128)(2,1)S(1)}, bf16[12,320,128]{2,1,0:T(8,128)(2,1)S(1)}, u32[]{:S(2)}, u32[]{:S(2)}) collective-permute-start(bf16[12,320,128]{2,1,0:T(8,128)(2,1)S(1)} %bitcast.11), channel_id=1, source_target_pairs={{0,8},{8,0},{1,9},{9,1},{2,10},{10,2},{3,11},{11,3},{4,12},{12,4},... | collective-permute-start | bytes 2949128 | tf_op jit(solution)/shard_map/ppermute | solution.py:327
  58.8 44.5 %copy-start = (bf16[1024,1024]{1,0:T(8,128)(2,1)S(1)}, bf16[1024,1024]{1,0:T(8,128)(2,1)}, u32[]{:S(2)}) copy-start(bf16[1024,1024]{1,0:T(8,128)(2,1)} %refs_7_.1) | copy-start | bytes 6291460
  58.8 44.5 %copy-start.2 = (f32[1024]{0:T(1024)S(1)}, f32[1024]{0:T(1024)}, u32[]{:S(2)}) copy-start(f32[1024]{0:T(1024)} %param.18) | copy-start | bytes 12292
  58.8 33.5 %all-to-all-start.1 = ((bf16[96,9,2,128]{3,2,1,0:T(2,128)(2,1)}), bf16[96,9,2,128]{3,2,1,0:T(2,128)(2,1)S(1)}, u32[]{:S(2)}, u32[]{:S(2)}) async-start(bf16[96,9,2,128]{3,2,1,0:T(2,128)(2,1)} %bitcast.3), calls=%async_computation.1 | async-start | bytes 884736 | tf_op jit(solution)/shard_map/all_to_all | solution.py:359
  68.4 11.3 %collective-permute-start.1 = (bf16[128,1024]{1,0:T(8,128)(2,1)}, bf16[128,1024]{1,0:T(8,128)(2,1)S(1)}, u32[]{:S(2)}, u32[]{:S(2)}) collective-permute-start(bf16[128,1024]{1,0:T(8,128)(2,1)} %refs_0_), channel_id=1, source_target_pairs={{0,2},{2,0},{4,6},{6,4},{1,3},{3,1},{5,7},{7,5},{8,10},{10,8},{12,... | collective-permute-start | bytes 786440 | tf_op jit(solution)/shard_map/ppermute | solution.py:327
  71.8 15.0 %collective-permute-start.2 = (bf16[128,1024]{1,0:T(8,128)(2,1)}, bf16[128,1024]{1,0:T(8,128)(2,1)S(1)}, u32[]{:S(2)}, u32[]{:S(2)}) collective-permute-start(bf16[128,1024]{1,0:T(8,128)(2,1)} %refs_0_), channel_id=1, source_target_pairs={{0,4},{2,6},{4,0},{6,2},{1,5},{3,7},{5,1},{7,3},{8,12},{10,14},{12... | collective-permute-start | bytes 786440 | tf_op jit(solution)/shard_map/ppermute | solution.py:327
  76.5 15.8 %collective-permute-start.3 = (bf16[128,1024]{1,0:T(8,128)(2,1)}, bf16[128,1024]{1,0:T(8,128)(2,1)S(1)}, u32[]{:S(2)}, u32[]{:S(2)}) collective-permute-start(bf16[128,1024]{1,0:T(8,128)(2,1)} %refs_0_), channel_id=1, source_target_pairs={{0,6},{2,4},{4,2},{6,0},{1,7},{3,5},{5,3},{7,1},{8,14},{10,12},{12... | collective-permute-start | bytes 786440 | tf_op jit(solution)/shard_map/ppermute | solution.py:327
  92.3 11.1 %copy-start.1 = (bf16[1,256,1024]{2,1,0:T(8,128)(2,1)S(1)}, bf16[1,256,1024]{2,1,0:T(8,128)(2,1)}, u32[]{:S(2)}) copy-start(bf16[1,256,1024]{2,1,0:T(8,128)(2,1)} %param.17) | copy-start | bytes 1572868
